TPU v7x, 32 devices: a whole 2x2x4 slice. The times are simulated.
32 devices in a mesh: dp: 8 (over z, x), rep: 4 (over y, core).
Axes of the slice: x: 2, y: 2, z: 4, core: 2. Of those that a mesh axis runs over, the one named last changes fastest.
Arguments:
- inputs: bfloat16 [8192, 2048], P(('dp', 'rep')), may hold values from -6 to 6
- layout: int32 [32, 3], replicated, may hold values from 1 to 16, as said below
- labels: int32 [8192], P(('dp', 'rep')), may hold values from 0 to 39
- cot_depth: bfloat16 [8192, 512], P(('dp', 'rep')), may hold values from -6 to 6
- w_reduce: bfloat16 [2048, 512], replicated, may hold values from -0.125 to 0.125
- w_spatial: bfloat16 [4608, 512], replicated, may hold values from -0.09375 to 0.09375
- w_expand: bfloat16 [512, 2048], replicated, may hold values from -0.25 to 0.25
- w_heads: bfloat16 [2048, 18432], P('rep'), may hold values from -0.046875 to 0.046875
- w_gates: bfloat16 [1024, 512], replicated, may hold values from -0.25 to 0.25
- w_messages: bfloat16 [27648, 512], P('rep'), may hold values from -0.0546875 to 0.0546875
- w_classes: bfloat16 [512, 40], replicated, may hold values from -0.5 to 0.5
- gain_mid: float32 [2, 512], replicated, may hold values from 0.5 to 2
- shift_mid: float32 [2, 512], replicated, may hold values from -3 to 3
- gain_wide: float32 [2048], replicated, may hold values from 0.5 to 2
- shift_wide: float32 [2048], replicated, may hold values from -3 to 3
- gain_head: float32 [2048], replicated, may hold values from 0.5 to 2
- shift_head: float32 [2048], replicated, may hold values from -3 to 3
Outputs:
- depth: float32 [8192, 512], P(('dp', 'rep'))
- logits: float32 [8192, 40], P(('dp', 'rep'))
- input_grad: float32 [8192, 2048], P(('dp', 'rep'))
- grad_reduce: float32 [2048, 512], P('rep')
- grad_spatial: float32 [4608, 512], P('rep')
- grad_expand: float32 [512, 2048], P('rep')
- grad_heads: float32 [2048, 18432], P('rep', 'dp')
- grad_gates: float32 [1024, 512], P('rep')
- grad_messages: float32 [27648, 512], P('rep', 'dp')
- grad_classes: float32 [512, 40], P('rep')
- grad_gain_mid: float32 [2, 512], replicated
- grad_shift_mid: float32 [2, 512], replicated
- grad_gain_wide: float32 [2048], replicated
- grad_shift_wide: float32 [2048], replicated
- grad_gain_head: float32 [2048], replicated
- grad_shift_head: float32 [2048], replicated
Inputs may be any that keep to these rules, and one draw needn't show every extreme that they name: `layout`: row d describes device d (dp, then rep): its map is 16 x 16 or (8) x (8), images times map area is at most 256 and one device fills all 256 rows in every draw; rows past images times area hold no pixel.
All inputs are finite; a program needn't handle non-finite values.
Results may differ from a plain program's by a relative error of at most 0.02.
Values may be sent and summed in bfloat16 or wider, within the bound.
A program may use at most 384 MiB of HBM per device.

v0:
```python
import jax
import jax.numpy as jnp
from jax import lax
from jax.sharding import PartitionSpec as P

EPS = 1e-05


def geometry(layout, span):
    position = jnp.arange(span, dtype=jnp.int32)
    height = layout[:, 0:1]
    map_width = layout[:, 1:2]
    images = layout[:, 2:3]
    map_area = height * map_width
    inside = position[None, :] % map_area
    row_of = inside // map_width
    col_of = inside % map_width
    living = position[None, :] < images * map_area
    return (row_of, col_of, living, height, map_width)


def taps(shape_info, dilation):
    row_of, col_of, living, height, map_width = shape_info
    offsets = []
    tap_marks = []
    for step_row in (-1, 0, 1):
        for step_col in (-1, 0, 1):
            target_row = row_of + dilation * step_row
            target_col = col_of + dilation * step_col
            inside = (
                living
                & (target_row >= 0)
                & (target_row < height)
                & (target_col >= 0)
                & (target_col < map_width)
            )
            tap_marks.append(inside.astype(jnp.float32))
            offsets.append(dilation * (step_row * map_width + step_col))
    return (jnp.concatenate(offsets, 1), jnp.stack(tap_marks, 1))


def spread(values, offsets, tap_marks):
    pieces = [
        jnp.roll(values, -offsets[tap_number], axis=0)
        * tap_marks[tap_number][:, None].astype(values.dtype)
        for tap_number in range(9)
    ]
    return jnp.concatenate(pieces, 1)


def spread_back(grad_cols, offsets, tap_marks, width_out):
    summed = jnp.zeros((grad_cols.shape[0], width_out), jnp.float32)
    for tap_number in range(9):
        tap_piece = (
            grad_cols[:, tap_number * width_out : (tap_number + 1) * width_out]
            * tap_marks[tap_number][:, None]
        )
        summed = summed + jnp.roll(tap_piece, offsets[tap_number], axis=0)
    return summed


def product(left_side, right_side):
    return jnp.dot(left_side, right_side, preferred_element_type=jnp.float32)


def inner_rows(left_side, right_side):
    return lax.dot_general(
        left_side, right_side, (((0,), (0,)), ((), ())), preferred_element_type=jnp.float32
    )


def against(left_side, right_side):
    return lax.dot_general(
        left_side, right_side, (((1,), (1,)), ((), ())), preferred_element_type=jnp.float32
    )


def tapwise(cols, kernel):
    return lax.dot_general(
        cols, kernel, (((1, 2), (0, 1)), ((), ())), preferred_element_type=jnp.float32
    )


def silu_slope(value_in):
    sigma_of = jax.nn.sigmoid(value_in)
    return sigma_of * (1.0 + value_in * (1.0 - sigma_of))


def normalize(raw_value, column_sums, squares, pixel_count, norm_gain, norm_shift):
    center = column_sums / pixel_count
    spread_of = squares / pixel_count - center * center
    scaling = lax.rsqrt(spread_of + EPS)
    unit_value = (raw_value - center) * scaling
    return (unit_value * norm_gain + norm_shift, unit_value, scaling)


def moments(raw_value, living):
    return lax.psum(
        (jnp.sum(living * raw_value, 0), jnp.sum(living * raw_value * raw_value, 0)), ("dp", "rep")
    )


def norm_back(grad_out, unit_value, scaling, norm_gain, living, pixel_count):
    grad_gain, grad_shift = lax.psum(
        (jnp.sum(living * grad_out * unit_value, 0), jnp.sum(living * grad_out, 0)), ("dp", "rep")
    )
    grad_raw = (
        living
        * (norm_gain * scaling)
        * (grad_out - grad_shift / pixel_count - unit_value * grad_gain / pixel_count)
    )
    return (grad_raw, grad_gain, grad_shift)


def shards(
    inputs,
    layout,
    labels,
    cot_depth,
    w_reduce,
    w_spatial,
    w_expand,
    w_heads,
    w_gates,
    w_messages,
    w_classes,
    gain_mid,
    shift_mid,
    gain_wide,
    shift_wide,
    gain_head,
    shift_head,
):
    pixels = inputs.shape[0]
    wide = inputs.shape[1]
    middle = w_reduce.shape[1]
    classes = w_classes.shape[1]
    group = lax.axis_size("rep")
    first_row = lax.axis_index("dp") * group
    own_row = first_row + lax.axis_index("rep")
    own_info = geometry(lax.dynamic_slice_in_dim(layout, own_row, 1, 0), pixels)
    offsets_one, marks_one = taps(own_info, 1)
    offsets_two, marks_two = taps(own_info, 2)
    offsets_one = offsets_one[0]
    marks_one = marks_one[0]
    offsets_two = offsets_two[0]
    marks_two = marks_two[0]
    living = own_info[2][0].astype(jnp.float32)[:, None]
    peer_offsets, peer_marks = taps(
        geometry(lax.dynamic_slice_in_dim(layout, first_row, group, 0), pixels), 1
    )
    reduced = product(inputs, w_reduce)
    sums_one, squares_one, pixel_count = lax.psum(
        (jnp.sum(living * reduced, 0), jnp.sum(living * reduced * reduced, 0), jnp.sum(living)),
        ("dp", "rep"),
    )
    normed_one, unit_one, scale_one = normalize(
        reduced, sums_one, squares_one, pixel_count, gain_mid[0], shift_mid[0]
    )
    hidden_one = jax.nn.silu(normed_one).astype(jnp.bfloat16)
    cols_two = spread(hidden_one, offsets_two, marks_two)
    spatial = product(cols_two, w_spatial)
    sums_two, squares_two = moments(spatial, living)
    normed_two, unit_two, scale_two = normalize(
        spatial, sums_two, squares_two, pixel_count, gain_mid[1], shift_mid[1]
    )
    hidden_two = jax.nn.silu(normed_two).astype(jnp.bfloat16)
    expanded = product(hidden_two, w_expand)
    sums_three, squares_three = moments(expanded, living)
    normed_three, unit_three, scale_three = normalize(
        expanded, sums_three, squares_three, pixel_count, gain_wide, shift_wide
    )
    pre_act = normed_three + inputs.astype(jnp.float32)
    trunk = jax.nn.silu(pre_act).astype(jnp.bfloat16)
    peer_trunk = lax.all_gather(trunk, "rep", axis=0, tiled=True)
    peer_cols = jnp.concatenate(
        [
            spread(
                peer_trunk[peer * pixels : (peer + 1) * pixels],
                peer_offsets[peer],
                peer_marks[peer],
            )
            for peer in range(group)
        ],
        0,
    )
    head_own = against(peer_cols, w_heads)
    headed = lax.all_to_all(
        head_own.astype(jnp.bfloat16), "rep", split_axis=0, concat_axis=1, tiled=True
    ).astype(head_own.dtype)
    sums_head, squares_head = moments(headed, living)
    normed_head, unit_head, scale_head = normalize(
        headed, sums_head, squares_head, pixel_count, gain_head, shift_head
    )
    features = jax.nn.silu(normed_head)
    rounded = features.astype(jnp.bfloat16)
    depth_part = rounded[:, :middle]
    seg_part = rounded[:, 3 * middle :]
    gate_depth = jax.nn.sigmoid(product(depth_part, w_gates[:middle]))
    gate_seg = jax.nn.sigmoid(product(seg_part, w_gates[middle:]))
    message_kernels = lax.all_gather(w_messages, "rep", axis=0, tiled=True)
    kernel_depth = message_kernels[: 27 * middle]
    kernel_seg = message_kernels[27 * middle :]
    cols_all = spread(rounded, offsets_one, marks_one).reshape(pixels, 9, 4 * middle)
    message_depth = tapwise(cols_all[:, :, middle:], kernel_depth.reshape(9, 3 * middle, middle))
    message_seg = tapwise(cols_all[:, :, : 3 * middle], kernel_seg.reshape(9, 3 * middle, middle))
    depth_full = features[:, :middle] + gate_depth * message_depth
    seg_full = features[:, 3 * middle :] + gate_seg * message_seg
    seg_low = seg_full.astype(jnp.bfloat16)
    logits_full = product(seg_low, w_classes)
    probs = jax.nn.softmax(logits_full, axis=1)
    onehot_table = (labels[:, None] == jnp.arange(classes, dtype=jnp.int32)[None, :]).astype(
        jnp.float32
    )
    grad_logits = (living * (probs - onehot_table)).astype(jnp.bfloat16)
    grad_classes = inner_rows(seg_low, grad_logits)
    grad_seg = against(grad_logits, w_classes)
    grad_depth = living * cot_depth.astype(jnp.float32)
    gate_pre_depth = (grad_depth * message_depth * gate_depth * (1.0 - gate_depth)).astype(
        jnp.bfloat16
    )
    msg_grad_depth = (grad_depth * gate_depth).astype(jnp.bfloat16)
    gate_pre_seg = (grad_seg * message_seg * gate_seg * (1.0 - gate_seg)).astype(jnp.bfloat16)
    msg_grad_seg = (grad_seg * gate_seg).astype(jnp.bfloat16)
    grad_gates = jnp.concatenate(
        [inner_rows(depth_part, gate_pre_depth), inner_rows(seg_part, gate_pre_seg)], 0
    )
    message_local = jnp.concatenate(
        [
            lax.dot_general(
                cols_all[:, :, middle:],
                msg_grad_depth,
                (((0,), (0,)), ((), ())),
                preferred_element_type=jnp.float32,
            ).reshape(27 * middle, middle),
            lax.dot_general(
                cols_all[:, :, : 3 * middle],
                msg_grad_seg,
                (((0,), (0,)), ((), ())),
                preferred_element_type=jnp.float32,
            ).reshape(27 * middle, middle),
        ],
        0,
    )
    message_share = lax.psum_scatter(
        message_local.astype(jnp.bfloat16), "rep", scatter_dimension=0, tiled=True
    ).astype(jnp.float32)
    back_depth = against(msg_grad_depth, kernel_depth).reshape(pixels, 9, 3 * middle)
    back_seg = against(msg_grad_seg, kernel_seg).reshape(pixels, 9, 3 * middle)
    back_cols = jnp.pad(back_depth, ((0, 0), (0, 0), (middle, 0))) + jnp.pad(
        back_seg, ((0, 0), (0, 0), (0, middle))
    )
    stream_grad = spread_back(
        back_cols.reshape(pixels, 36 * middle), offsets_one, marks_one, 4 * middle
    )
    direct_depth = grad_depth + against(gate_pre_depth, w_gates[:middle])
    direct_seg = grad_seg + against(gate_pre_seg, w_gates[middle:])
    feat_grad = stream_grad + jnp.concatenate(
        [direct_depth, jnp.zeros((pixels, 2 * middle), jnp.float32), direct_seg], 1
    )
    head_raw, grad_gain_head, grad_shift_head = norm_back(
        feat_grad * silu_slope(normed_head), unit_head, scale_head, gain_head, living, pixel_count
    )
    head_low = head_raw.astype(jnp.bfloat16)
    peer_grad = lax.all_to_all(head_low, "rep", split_axis=1, concat_axis=0, tiled=True)
    heads_local = inner_rows(peer_grad, peer_cols)
    grad_heads, grad_messages = (
        lax.psum_scatter(heads_local, "dp", scatter_dimension=1, tiled=True),
        lax.psum_scatter(message_share, "dp", scatter_dimension=1, tiled=True),
    )
    trunk_terms = [
        spread_back(
            product(peer_grad[peer * pixels : (peer + 1) * pixels], w_heads),
            peer_offsets[peer],
            peer_marks[peer],
            wide,
        )
        for peer in range(group)
    ]
    trunk_grad = lax.psum_scatter(
        jnp.concatenate(trunk_terms, 0).astype(jnp.bfloat16), "rep", scatter_dimension=0, tiled=True
    ).astype(jnp.float32)
    pre_grad = trunk_grad * silu_slope(pre_act)
    expand_raw, grad_gain_wide, grad_shift_wide = norm_back(
        pre_grad, unit_three, scale_three, gain_wide, living, pixel_count
    )
    expand_low = expand_raw.astype(jnp.bfloat16)
    grad_expand = inner_rows(hidden_two, expand_low)
    hidden_two_grad = against(expand_low, w_expand)
    spatial_raw, gain_grad_two, shift_grad_two = norm_back(
        hidden_two_grad * silu_slope(normed_two),
        unit_two,
        scale_two,
        gain_mid[1],
        living,
        pixel_count,
    )
    spatial_low = spatial_raw.astype(jnp.bfloat16)
    grad_spatial = inner_rows(cols_two, spatial_low)
    hidden_one_grad = spread_back(against(spatial_low, w_spatial), offsets_two, marks_two, middle)
    reduced_raw, gain_grad_one, shift_grad_one = norm_back(
        hidden_one_grad * silu_slope(normed_one),
        unit_one,
        scale_one,
        gain_mid[0],
        living,
        pixel_count,
    )
    reduced_low = reduced_raw.astype(jnp.bfloat16)
    grad_reduce = inner_rows(inputs, reduced_low)
    input_grad = pre_grad + against(reduced_low, w_reduce)
    every_share = (
        lax.psum_scatter(
            grad_reduce.astype(jnp.bfloat16), "rep", scatter_dimension=0, tiled=True
        ).astype(jnp.float32),
        lax.psum_scatter(
            grad_spatial.astype(jnp.bfloat16), "rep", scatter_dimension=0, tiled=True
        ).astype(jnp.float32),
        lax.psum_scatter(
            grad_expand.astype(jnp.bfloat16), "rep", scatter_dimension=0, tiled=True
        ).astype(jnp.float32),
        lax.psum_scatter(
            grad_gates.astype(jnp.bfloat16), "rep", scatter_dimension=0, tiled=True
        ).astype(jnp.float32),
        lax.psum_scatter(
            grad_classes.astype(jnp.bfloat16), "rep", scatter_dimension=0, tiled=True
        ).astype(jnp.float32),
    )
    grad_reduce, grad_spatial, grad_expand, grad_gates, grad_classes = lax.psum(
        (every_share[0], every_share[1], every_share[2], every_share[3], every_share[4]), "dp"
    )
    grad_gain_mid = jnp.stack([gain_grad_one, gain_grad_two], 0)
    grad_shift_mid = jnp.stack([shift_grad_one, shift_grad_two], 0)
    return (
        living * depth_full,
        living * logits_full,
        input_grad,
        grad_reduce,
        grad_spatial,
        grad_expand,
        grad_heads,
        grad_gates,
        grad_messages,
        grad_classes,
        grad_gain_mid,
        grad_shift_mid,
        grad_gain_wide,
        grad_shift_wide,
        grad_gain_head,
        grad_shift_head,
    )


def solution(mesh):
    in_specs = (
        P(("dp", "rep"), None),
        P(),
        P(("dp", "rep")),
        P(("dp", "rep"), None),
        P(),
        P(),
        P(),
        P("rep", None),
        P(),
        P("rep", None),
        P(),
        P(),
        P(),
        P(),
        P(),
        P(),
        P(),
    )
    out_specs = (
        P(("dp", "rep"), None),
        P(("dp", "rep"), None),
        P(("dp", "rep"), None),
        P("rep", None),
        P("rep", None),
        P("rep", None),
        P("rep", "dp"),
        P("rep", None),
        P("rep", "dp"),
        P("rep", None),
        P(),
        P(),
        P(),
        P(),
        P(),
        P(),
    )
    return jax.shard_map(shards, mesh=mesh, in_specs=in_specs, out_specs=out_specs, check_vma=False)
```

profile of v0, /device:TPU:28, one launch (start us, length us, event | category | flops | bytes accessed | tf_op | source)
XLA Modules:
  0.0 2185.4 jit_solution(17100062445124065968)
XLA Ops:
  24.7 40.4 %all-reduce.9 = (f32[512]{0:T(512)S(1)}, f32[]{:T(128)}, f32[512]{0:T(512)S(1)}) all-reduce(f32[512]{0:T(512)S(1)} %get-tuple-element.112, f32[]{:T(128)} %fusion.281, f32[512]{0:T(512)S(1)} %get-tuple-element.111), channel_id=1, replica_groups=mesh['dp'=8,'rep'=4] {'dp','rep'}, use_global_device_ids=true, to_apply=%region_5.6 | all-reduce | flops 1025 | bytes 8200 | tf_op jit(solution)/shard_map/psum | solution.py:153
  74.9 5.2 multiply_reduce_fusion.6
  80.1 40.1 %all-reduce.8 = (f32[512]{0:T(512)S(1)}, f32[512]{0:T(512)S(1)}) all-reduce(f32[512]{0:T(512)S(1)} %get-tuple-element.110, f32[512]{0:T(512)S(1)} %get-tuple-element.109), channel_id=1, replica_groups=mesh['dp'=8,'rep'=4] {'dp','rep'}, use_global_device_ids=true, to_apply=%region_9.15 | all-reduce | flops 1024 | bytes 8192 | tf_op jit(solution)/shard_map/psum | solution.py:98
  121.5 3.3 fusion.9
  124.7 40.0 %all-reduce.7 = (f32[2048]{0:T(1024)S(1)}, f32[2048]{0:T(1024)S(1)}) all-reduce(f32[2048]{0:T(1024)S(1)} %get-tuple-element.102, f32[2048]{0:T(1024)S(1)} %get-tuple-element.101), channel_id=1, replica_groups=mesh['dp'=8,'rep'=4] {'dp','rep'}, use_global_device_ids=true, to_apply=%region_11.17 | all-reduce | flops 4096 | bytes 32768 | tf_op jit(solution)/shard_map/psum | solution.py:98
  167.2 3.4 multiply_convert_fusion.2
  210.5 3.4 fusion.130
  222.6 3.7 fusion.178
  263.5 25.8 %fusion.88 = bf16[1024,512]{1,0:T(8,128)(2,1)} fusion(bf16[512,18432]{1,0:T(8,128)(2,1)} %param.58, bf16[256,18432]{1,0:T(8,128)(2,1)} %fusion.127, bf16[256,18432]{1,0:T(8,128)(2,1)S(1)} %fusion.151, bf16[256,18432]{1,0:T(8,128)(2,1)} %fusion.175, bf16[256,18432]{1,0:T(8,128)(2,1)} %copy-done.37), kind=kOutput, calls=%fused_computation.304 | convolution fusion | flops 19478872064 | bytes 57671680 | tf_op jit(solution)/shard_map/dot_general | solution.py:73
  289.3 3.5 all-to-all-start
  295.9 21.1 all-to-all-done
  319.3 42.4 %all-reduce.6 = (f32[2048]{0:T(1024)S(1)}, f32[2048]{0:T(1024)S(1)}) all-reduce(f32[2048]{0:T(1024)S(1)} %bitcast.245, f32[2048]{0:T(1024)S(1)} %bitcast.246), channel_id=1, replica_groups=mesh['dp'=8,'rep'=4] {'dp','rep'}, use_global_device_ids=true, to_apply=%region_15.25 | all-reduce | flops 4096 | bytes 32768 | tf_op jit(solution)/shard_map/psum | solution.py:98
  363.0 3.6 fusion.296
  383.7 12.5 copy.84
  398.4 21.1 fusion.298
  419.5 7.4 fusion.89
  427.0 7.4 fusion.92
  438.6 14.1 fusion.288
  452.7 13.9 fusion.290
  466.6 15.9 pad_add_fusion
  482.5 13.5 fusion.299
  498.9 3.2 broadcast_multiply_fusion.1
  505.1 3.2 broadcast_multiply_fusion.2
  529.4 3.2 broadcast_multiply_fusion.3
  550.6 11.7 multiply_reduce_fusion.5
  562.2 40.6 %all-reduce.5 = (f32[2048]{0:T(1024)S(1)}, f32[2048]{0:T(1024)S(1)}) all-reduce(f32[2048]{0:T(1024)S(1)} %get-tuple-element.100, f32[2048]{0:T(1024)S(1)} %get-tuple-element.99), channel_id=1, replica_groups=mesh['dp'=8,'rep'=4] {'dp','rep'}, use_global_device_ids=true, to_apply=%region_23.37 | all-reduce | flops 4096 | bytes 32768 | tf_op jit(solution)/shard_map/psum | solution.py:104
  603.5 3.5 multiply_convert_fusion.1
  608.0 3.5 all-to-all-start.1
  642.1 15.8 fusion.271
  657.9 15.4 fusion.270
  673.3 15.4 fusion.269
  688.7 15.4 fusion.268
  704.3 11.6 slice_multiply_fusion.32
  716.1 12.9 slice_multiply_fusion.23
  729.2 13.5 slice_multiply_fusion.14
  744.2 6.5 slice_multiply_fusion.5
  750.7 10.1 fusion.58
  760.8 10.1 fusion.43
  770.9 10.1 fusion.28
  781.0 10.0 fusion.13
  791.0 3.7 pad_maximum_fusion.4
  795.6 11.5 convolution_convert_fusion.1
  807.1 18.8 copy.101
  826.0 10.3 convolution_convert_fusion
  836.2 18.7 copy.102
  854.9 19.6 pad_maximum_fusion.1
  883.3 5.5 multiply_reduce_fusion.4
  888.8 40.4 %all-reduce.4 = (f32[2048]{0:T(1024)S(1)}, f32[2048]{0:T(1024)S(1)}) all-reduce(f32[2048]{0:T(1024)S(1)} %get-tuple-element.98, f32[2048]{0:T(1024)S(1)} %get-tuple-element.97), channel_id=1, replica_groups=mesh['dp'=8,'rep'=4] {'dp','rep'}, use_global_device_ids=true, to_apply=%region_28.42 | all-reduce | flops 4096 | bytes 32768 | tf_op jit(solution)/shard_map/psum | solution.py:104
  929.9 3.5 multiply_convert_fusion
  939.9 40.9 %all-reduce.3 = (f32[512]{0:T(512)S(1)}, f32[512]{0:T(512)S(1)}) all-reduce(f32[512]{0:T(512)S(1)} %get-tuple-element.108, f32[512]{0:T(512)S(1)} %get-tuple-element.107), channel_id=1, replica_groups=mesh['dp'=8,'rep'=4] {'dp','rep'}, use_global_device_ids=true, to_apply=%region_32.46 | all-reduce | flops 1024 | bytes 8192 | tf_op jit(solution)/shard_map/psum | solution.py:104
  984.2 3.8 fusion.320
  991.9 40.2 %all-reduce.2 = (f32[512]{0:T(512)S(1)}, f32[512]{0:T(512)S(1)}) all-reduce(f32[512]{0:T(512)S(1)} %get-tuple-element.106, f32[512]{0:T(512)S(1)} %get-tuple-element.105), channel_id=1, replica_groups=mesh['dp'=8,'rep'=4] {'dp','rep'}, use_global_device_ids=true, to_apply=%region_36.54 | all-reduce | flops 1024 | bytes 8192 | tf_op jit(solution)/shard_map/psum | solution.py:104
  1037.8 5.2 convolution_convert_fusion.2
  1044.2 34.4 %fusion = f32[512,18432]{1,0:T(8,128)} fusion(bf16[1024,512]{1,0:T(8,128)(2,1)S(1)} %bitcast.232, bf16[256,18432]{1,0:T(8,128)(2,1)} %fusion.127, bf16[256,18432]{1,0:T(8,128)(2,1)} %copy-done.36, bf16[256,18432]{1,0:T(8,128)(2,1)} %fusion.175, bf16[256,18432]{1,0:T(8,128)(2,1)} %copy-done.37), kind=kOutput, calls=%fused_computation.6 | convolution fusion | flops 19478347776 | bytes 76546048 | tf_op jit(solution)/shard_map/dot_general | solution.py:67
  1078.7 9.0 convert_element_type.754
  1087.8 12.4 reduce-scatter.28.cloned.1.call-done
  1101.0 27.2 %reduce-scatter.22.cloned.1.call-done = bf16[256,512]{1,0:T(8,128)(2,1)} async-done(((bf16[1024,512]{1,0:T(8,128)(2,1)}), bf16[256,512]{1,0:T(8,128)(2,1)}) %reduce-scatter.22.cloned.1.call-update) | async-done | bytes 262160 | tf_op jit(solution)/shard_map/reduce_scatter | solution.py:322
  1129.4 4.3 convolution_add_fusion
  1133.7 28.5 %reduce-scatter.18.cloned.1.call-done = bf16[128,2048]{1,0:T(8,128)(2,1)} async-done(((bf16[512,2048]{1,0:T(8,128)(2,1)}), bf16[128,2048]{1,0:T(8,128)(2,1)}) %reduce-scatter.18.cloned.1.call-update) | async-done | bytes 524304 | tf_op jit(solution)/shard_map/reduce_scatter | solution.py:319
  1162.2 34.2 %reduce-scatter.14.cloned.1.call-done = bf16[512,512]{0,1:T(8,128)(2,1)} async-done(((bf16[2048,512]{0,1:T(8,128)(2,1)}), bf16[512,512]{0,1:T(8,128)(2,1)}) %reduce-scatter.14.cloned.1.call-update) | async-done | bytes 524304 | tf_op jit(solution)/shard_map/reduce_scatter | solution.py:313
  1196.3 50.4 %reduce-scatter.16.cloned.1.call-done = bf16[1152,512]{1,0:T(8,128)(2,1)} async-done(((bf16[4608,512]{1,0:T(8,128)(2,1)}), bf16[1152,512]{1,0:T(8,128)(2,1)}) %reduce-scatter.16.cloned.1.call-update) | async-done | bytes 1179664 | tf_op jit(solution)/shard_map/reduce_scatter | solution.py:316
  1246.8 275.9 %all-reduce.12 = (f32[512,512]{0,1:T(8,128)S(1)}, f32[1152,512]{1,0:T(8,128)}, f32[128,2048]{1,0:T(8,128)}, f32[256,512]{1,0:T(8,128)}, f32[128,40]{0,1:T(8,128)}) all-reduce(bf16[512,512]{0,1:T(8,128)(2,1)} %reduce-scatter.14.cloned.1.call-done, ...), channel_id=1, replica_groups=mesh['dp'=8,'rep'=4] {'dp'}, use_global_device_ids=true, to_apply=%region_38.56 | all-reduce | flops 1250304 | bytes 7501824 | tf_op jit(solution)/shard_map/psum | solution.py:329
  1524.0 422.1 %reduce-scatter.20.cloned.1.call-done = f32[512,2304]{1,0:T(8,128)} async-done(((f32[512,18432]{1,0:T(8,128)}), f32[512,2304]{1,0:T(8,128)}) %reduce-scatter.20.cloned.1.call-update) | async-done | bytes 4718608 | tf_op jit(solution)/shard_map/reduce_scatter | solution.py:268
  1946.1 232.6 %reduce-scatter.26.cloned.1.call-done = f32[6912,64]{0,1:T(8,128)} async-done(((f32[6912,512]{0,1:T(8,128)}), f32[6912,64]{0,1:T(8,128)}) %reduce-scatter.26.cloned.1.call-update) | async-done | bytes 1769488 | tf_op jit(solution)/shard_map/reduce_scatter | solution.py:269
  (553 shorter events, 186.7 us)
Async XLA Ops:
  7.2 114.3 %copy-start = (bf16[512,2048]{1,0:T(8,128)(2,1)S(1)}, bf16[512,2048]{1,0:T(8,128)(2,1)}, u32[]{:S(2)}) copy-start(bf16[512,2048]{1,0:T(8,128)(2,1)} %param.57) | copy-start | bytes 6291460
  7.2 200.5 %all-gather.3.cloned.1.call-start = ((), (), s32[]{:S(2)}) async-start(), calls=%async_computation.11 | async-start | bytes 5242880 | tf_op jit(solution)/shard_map/all_gather | solution.py:175
  11.9 591.6 %copy-start.34 = (f32[256]{0:T(256)}, f32[256]{0:T(256)S(1)}, u32[]{:S(2)}) copy-start(f32[256]{0:T(256)S(1)} %compare_convert_fusion.1) | copy-start | bytes 3076
  21.0 49.2 %copy-start.45 = (f32[1,512]{1,0:T(1,128)}, f32[1,512]{1,0:T(1,128)S(1)}, u32[]{:S(2)}) copy-start(f32[1,512]{1,0:T(1,128)S(1)} %get-tuple-element.284) | copy-start | bytes 6148
  21.0 100.4 %copy-start.69 = (f32[1,512]{1,0:T(1,128)}, f32[1,512]{1,0:T(1,128)S(1)}, u32[]{:S(2)}) copy-start(f32[1,512]{1,0:T(1,128)S(1)} %get-tuple-element.283) | copy-start | bytes 6148
  21.8 48.4 %copy-start.50 = (f32[1,512]{1,0:T(1,128)}, f32[1,512]{1,0:T(1,128)S(1)}, u32[]{:S(2)}) copy-start(f32[1,512]{1,0:T(1,128)S(1)} %get-tuple-element.286) | copy-start | bytes 6148
  21.8 99.6 %copy-start.161 = (f32[1,512]{1,0:T(1,128)}, f32[1,512]{1,0:T(1,128)S(1)}, u32[]{:S(2)}) copy-start(f32[1,512]{1,0:T(1,128)S(1)} %get-tuple-element.285) | copy-start | bytes 6148
  24.7 47.3 %copy-start.10 = (f32[256,512]{1,0:T(8,128)}, f32[256,512]{1,0:T(8,128)S(1)}, u32[]{:S(2)}) copy-start(f32[256,512]{1,0:T(8,128)S(1)} %get-tuple-element.357) | copy-start | bytes 1572868
  121.4 43.3 %copy-start.39 = (f32[2048]{0:T(1024)S(1)}, f32[2048]{0:T(1024)}, u32[]{:S(2)}) copy-start(f32[2048]{0:T(1024)} %param.64) | copy-start | bytes 24580
  121.5 45.8 %copy-start.8 = (bf16[256,2048]{1,0:T(8,128)(2,1)S(1)}, bf16[256,2048]{1,0:T(8,128)(2,1)}, u32[]{:S(2)}) copy-start(bf16[256,2048]{1,0:T(8,128)(2,1)} %param.51) | copy-start | bytes 3145732
  121.5 45.7 %copy-start.48 = (f32[2048]{0:T(1024)S(1)}, f32[2048]{0:T(1024)}, u32[]{:S(2)}) copy-start(f32[2048]{0:T(1024)} %param.65) | copy-start | bytes 24580
  170.6 227.8 %all-gather.5.cloned.1.call-start = ((), (), s32[]{:S(2)}) async-start(), calls=%async_computation.12 | async-start | bytes 35389440 | tf_op jit(solution)/shard_map/all_gather | solution.py:201
  256.0 33.4 %copy-start.36 = (bf16[256,18432]{1,0:T(8,128)(2,1)}, bf16[256,18432]{1,0:T(8,128)(2,1)S(1)}, u32[]{:S(2)}) copy-start(bf16[256,18432]{1,0:T(8,128)(2,1)S(1)} %fusion.151) | copy-start | bytes 28311556
  289.3 27.6 %all-to-all-start = ((bf16[4,256,512]{2,1,0:T(8,128)(2,1)}), bf16[4,256,512]{2,1,0:T(8,128)(2,1)S(1)}, u32[]{:S(2)}, u32[]{:S(2)}) async-start(bf16[4,256,512]{2,1,0:T(8,128)(2,1)} %bitcast.235), calls=%async_computation | async-start | bytes 2097152 | tf_op jit(solution)/shard_map/all_to_all | solution.py:188
  317.3 44.4 %copy-start.38 = (f32[2048]{0:T(1024)S(1)}, f32[2048]{0:T(1024)}, u32[]{:S(2)}) copy-start(f32[2048]{0:T(1024)} %param.66) | copy-start | bytes 24580
  317.3 45.7 %copy-start.47 = (f32[2048]{0:T(1024)S(1)}, f32[2048]{0:T(1024)}, u32[]{:S(2)}) copy-start(f32[2048]{0:T(1024)} %param.67) | copy-start | bytes 24580
  366.6 67.8 %copy-start.2 = (bf16[256,2048]{1,0:T(8,128)(2,1)}, bf16[256,2048]{1,0:T(8,128)(2,1)S(1)}, u32[]{:S(2)}) copy-start(bf16[256,2048]{1,0:T(8,128)(2,1)S(1)} %get-tuple-element.154) | copy-start | bytes 3145732
  398.4 21.1 copy-start.1
  437.1 15.6 copy-start.14
  438.6 14.1 copy-start.12
  438.6 110.6 %copy-start.16 = (bf16[256,512]{1,0:T(8,128)(2,1)}, bf16[256,512]{1,0:T(8,128)(2,1)S(1)}, u32[]{:S(2)}) copy-start(bf16[256,512]{1,0:T(8,128)(2,1)S(1)} %get-tuple-element.231) | copy-start | bytes 786436
  608.0 34.1 %all-to-all-start.1 = ((bf16[256,4,512]{2,0,1:T(8,128)(2,1)}), bf16[256,4,512]{2,0,1:T(8,128)(2,1)S(1)}, u32[]{:S(2)}, u32[]{:S(2)}) async-start(bf16[256,4,512]{2,0,1:T(8,128)(2,1)} %bitcast.233), calls=%async_computation.1 | async-start | bytes 2097152 | tf_op jit(solution)/shard_map/all_to_all | solution.py:265
  611.6 271.7 %reduce-scatter.12.cloned.1.call-start = ((), (), s32[]{:S(2)}) async-start(), calls=%async_computation.13 | async-start | bytes 5242880 | tf_op jit(solution)/shard_map/reduce_scatter | solution.py:280
  642.1 46.6 %copy-start.6 = (bf16[256,4,512]{2,0,1:T(8,128)(2,1)}, bf16[256,4,512]{2,0,1:T(8,128)(2,1)S(1)}, u32[]{:S(2)}) copy-start(bf16[256,4,512]{2,0,1:T(8,128)(2,1)S(1)} %all-to-all-done.1) | copy-start | bytes 3145732
  688.7 15.5 copy-start.90
  688.7 15.5 copy-start.92
  688.7 15.5 copy-start.98
  688.7 15.5 copy-start.108
  688.7 15.5 copy-start.110
  688.7 15.5 copy-start.124
  688.7 15.5 copy-start.126
  688.7 15.5 copy-start.134
  716.0 13.0 copy-start.78
  716.0 13.0 copy-start.80
  716.0 13.0 copy-start.82
  716.1 13.0 copy-start.100
  716.1 13.0 copy-start.102
  716.1 13.0 copy-start.116
  716.1 13.0 copy-start.118
  716.1 26.6 %slice-start = ((s8[18874368]{0:T(1024)(128)(4,1)}), s8[4194304]{0:T(1024)(128)(4,1)S(1)}, s32[]{:S(2)}) async-start(s8[18874368]{0:T(1024)(128)(4,1)} %bitcast.220), calls=%async_computation.22 | async-start | bytes 8388608
  716.1 26.6 %slice-start.1 = ((s8[18874368]{0:T(1024)(128)(4,1)}), s8[4194304]{0:T(1024)(128)(4,1)S(1)}, s32[]{:S(2)}) async-start(s8[18874368]{0:T(1024)(128)(4,1)} %bitcast.220), calls=%async_computation.23 | async-start | bytes 8388608
  716.1 26.6 %slice-start.2 = ((s8[18874368]{0:T(1024)(128)(4,1)}), s8[4194304]{0:T(1024)(128)(4,1)S(1)}, s32[]{:S(2)}) async-start(s8[18874368]{0:T(1024)(128)(4,1)} %bitcast.220), calls=%async_computation.24 | async-start | bytes 8388608
  729.1 13.6 slice-start.3
  729.1 15.0 slice-start.4
  729.1 15.0 copy-start.72
  729.1 15.0 copy-start.74
  729.2 15.0 copy-start.76
  729.2 15.0 copy-start.94
  729.2 15.0 copy-start.96
  729.2 15.0 copy-start.112
  729.2 15.0 copy-start.114
  729.2 15.0 copy-start.128
  794.7 284.0 %reduce-scatter.24.cloned.1.call-start = ((), (), s32[]{:S(2)}) async-start(), calls=%async_computation.19 | async-start | bytes 35389440 | tf_op jit(solution)/shard_map/reduce_scatter | solution.py:245
  807.1 18.8 copy-start.13
  874.5 225.6 %reduce-scatter.28.cloned.1.call-start = ((), (), s32[]{:S(2)}) async-start(), calls=%async_computation.21 | async-start | bytes 163840
  880.4 247.8 %reduce-scatter.22.cloned.1.call-start = ((), (), s32[]{:S(2)}) async-start(), calls=%async_computation.18 | async-start | bytes 1310720 | tf_op jit(solution)/shard_map/reduce_scatter | solution.py:322
  883.1 46.7 %copy-start.52 = (f32[2048]{0:T(1024)S(1)}, f32[2048]{0:T(1024)}, u32[]{:S(2)}) copy-start(f32[2048]{0:T(1024)} %get-tuple-element.140) | copy-start | bytes 24580
  883.2 279.0 %reduce-scatter.18.cloned.1.call-start = ((), (), s32[]{:S(2)}) async-start(), calls=%async_computation.16 | async-start | bytes 2621440 | tf_op jit(solution)/shard_map/reduce_scatter | solution.py:319
  936.6 259.7 %reduce-scatter.14.cloned.1.call-start = ((), (), s32[]{:S(2)}) async-start(), calls=%async_computation.14 | async-start | bytes 2621440 | tf_op jit(solution)/shard_map/reduce_scatter | solution.py:313
  936.8 44.6 %copy-start.61 = (f32[512]{0:T(512)S(1)}, f32[512]{0:T(512)}, u32[]{:S(2)}) copy-start(f32[512]{0:T(512)} %get-tuple-element.138) | copy-start | bytes 6148
  989.2 43.6 %copy-start.60 = (f32[512]{0:T(512)S(1)}, f32[512]{0:T(512)}, u32[]{:S(2)}) copy-start(f32[512]{0:T(512)} %get-tuple-element.135) | copy-start | bytes 6148
  1036.9 209.9 %reduce-scatter.16.cloned.1.call-start = ((), (), s32[]{:S(2)}) async-start(), calls=%async_computation.15 | async-start | bytes 5898240 | tf_op jit(solution)/shard_map/reduce_scatter | solution.py:316
  1043.0 903.0 %reduce-scatter.20.cloned.1.call-start = ((), (), s32[]{:S(2)}) async-start(), calls=%async_computation.17 | async-start | bytes 42467328 | tf_op jit(solution)/shard_map/reduce_scatter | solution.py:268
  1078.7 1100.0 %reduce-scatter.26.cloned.1.call-start = ((), (), s32[]{:S(2)}) async-start(), calls=%async_computation.20 | async-start | bytes 15925248 | tf_op jit(solution)/shard_map/reduce_scatter | solution.py:269
  (120 other events, 472.2 us)
Sparse Core Ops, SparseCore 0:
  170.7 33.8 all-gather.2
  206.1 184.8 all-gather.4
  794.8 44.9 reduce-scatter.11
  874.7 203.5 reduce-scatter.23
  1080.5 19.5 reduce-scatter.27
  1103.3 24.8 reduce-scatter.21
  1130.7 31.4 reduce-scatter.17
  1164.9 31.4 reduce-scatter.13
  1198.9 47.8 reduce-scatter.15
  1251.5 694.5 reduce-scatter.19
  1950.3 228.3 reduce-scatter.25
where the time goes:
time: 2200 us; the launch traced here: 2190 us
  waiting for transfers between devices  829 us (38%)
  blocking collectives  601 us (27%)
  other arithmetic  293 us (13%)
  matrix products  231 us (10%)
  local copies, waits for them, and re-layouts  135 us (6%)
  between operations  88.5 us (4%)
    reduce_scatter x1, waiting for transfers between devices, shards(): lax.psum_scatter(heads_local, 'dp', scatter_dimension=1, tiled=True)  422 us
    psum x1, blocking collectives, shards(): lax.psum((every_share[0], every_share[1], every_share[2], every_share[3],...  276 us
    reduce_scatter x1, waiting for transfers between devices, shards(): lax.psum_scatter(message_share, 'dp', scatter_dimension=1, tiled=True)  233 us
    psum x4, blocking collectives, norm_back(): lax.psum((jnp.sum(living * grad_out * unit_value, 0), jnp.sum(living * gr...  162 us
    psum x3, blocking collectives, moments(): lax.psum((jnp.sum(living * raw_value, 0), jnp.sum(living * raw_value * ra...  122 us
    dot_general x10, matrix products, product(): return jnp.dot(left_side, right_side, preferred_element_type=jnp.float32)  78.2 us
    mul x13, other arithmetic, spread_back(): grad_cols[:, tap_number * width_out:(tap_number + 1) * width_out]  69.9 us
    dot_general x9, matrix products, against(): lax.dot_general(left_side, right_side, (((1,), (1,)), ((), ())), preferre...  68.2 us
  transfers between devices with their start and end apart: 13, of which 8 were waited for; matrix products, arithmetic and copies ran while one was open for 14% of the time, Pallas kernels for 0%

commit v1 on v0

v1 whole, which is shorter than its diff:
```python
import functools

import jax
import jax.numpy as jnp
from jax import lax
from jax.experimental import pallas as pl
from jax.experimental.pallas import tpu as pltpu
from jax.sharding import PartitionSpec as P

EPS = 1e-05
F32 = jnp.float32
BF16 = jnp.bfloat16
VMEM_LIMIT = 60 * 2**20


def geometry(layout, span):
    position = jnp.arange(span, dtype=jnp.int32)
    height = layout[:, 0:1]
    map_width = layout[:, 1:2]
    images = layout[:, 2:3]
    map_area = height * map_width
    inside = position[None, :] % map_area
    row_of = inside // map_width
    col_of = inside % map_width
    living = position[None, :] < images * map_area
    return (row_of, col_of, living, height, map_width)


def shift_matrices(shape_info, dilation):
    row_of, col_of, living, height, map_width = shape_info
    span = row_of.shape[1]
    position = jnp.arange(span, dtype=jnp.int32)
    every = []
    for step_row in (-1, 0, 1):
        for step_col in (-1, 0, 1):
            target_row = row_of + dilation * step_row
            target_col = col_of + dilation * step_col
            inside = (
                living
                & (target_row >= 0)
                & (target_row < height)
                & (target_col >= 0)
                & (target_col < map_width)
            )
            neighbour = position[None, :] + dilation * (step_row * map_width + step_col)
            picked = jnp.where(inside, neighbour, -1)
            every.append(picked[:, :, None] == position[None, None, :])
    return jnp.stack(every, 0).astype(BF16)


def product(left_side, right_side):
    return jnp.dot(left_side, right_side, preferred_element_type=F32)


def inner_rows(left_side, right_side):
    return lax.dot_general(
        left_side, right_side, (((0,), (0,)), ((), ())), preferred_element_type=F32
    )


def against(left_side, right_side):
    return lax.dot_general(
        left_side, right_side, (((1,), (1,)), ((), ())), preferred_element_type=F32
    )


def params():
    return pltpu.CompilerParams(vmem_limit_bytes=VMEM_LIMIT)


def cost(flops, moved):
    return pl.CostEstimate(flops=flops, bytes_accessed=moved, transcendentals=0)


def heads_forward_kernel(u_ref, w_ref, s_ref, out_ref):
    tap = pl.program_id(0)
    blocks, span = s_ref.shape[1], s_ref.shape[2]
    half = blocks // 2

    @pl.when(tap == 0)
    def _():
        out_ref[...] = jnp.zeros_like(out_ref)

    @pl.loop(0, 2)
    def _(part):
        rows = pl.ds(pl.multiple_of(part * half * span, half * span), half * span)
        y = against(u_ref[rows, :], w_ref[...]).astype(BF16)
        for k in range(half):
            at = pl.ds(pl.multiple_of((part * half + k) * span, span), span)
            out_ref[at, :] += product(s_ref[0, part * half + k], y[k * span : (k + 1) * span])


def heads_forward(u, w_heads, shifts):
    rows, wide = u.shape
    outs = w_heads.shape[0]
    taps, blocks, span, _ = shifts.shape
    return pl.pallas_call(
        heads_forward_kernel,
        grid=(taps,),
        in_specs=[
            pl.BlockSpec((rows, wide), lambda t: (0, 0)),
            pl.BlockSpec((outs, wide), lambda t: (0, t)),
            pl.BlockSpec((1, blocks, span, span), lambda t: (t, 0, 0, 0)),
        ],
        out_specs=pl.BlockSpec((rows, outs), lambda t: (0, 0)),
        out_shape=jax.ShapeDtypeStruct((rows, outs), F32),
        compiler_params=params(),
        cost_estimate=cost(2 * rows * wide * outs * taps, w_heads.size * 2 + u.size * 2),
        name="heads_forward",
    )(u, w_heads, shifts)


def shifted(g_ref, s_ref):
    blocks, span = s_ref.shape[1], s_ref.shape[2]
    return jnp.concatenate(
        [
            inner_rows(s_ref[0, k], g_ref[pl.ds(k * span, span), :]).astype(BF16)
            for k in range(blocks)
        ],
        0,
    )


def heads_data_kernel(g_ref, w_ref, s_ref, out_ref, total):
    tap = pl.program_id(0)
    taken = shifted(g_ref, s_ref)
    wide = w_ref.shape[1]
    step = 512

    @pl.when(tap == 0)
    def _():
        total[...] = jnp.zeros_like(total)

    for c in range(0, wide, step):
        total[:, c : c + step] += product(taken, w_ref[:, c : c + step])

    @pl.when(tap == pl.num_programs(0) - 1)
    def _():
        out_ref[...] = total[...].astype(out_ref.dtype)


def heads_data(g, w_heads, shifts):
    rows, outs = g.shape
    taps, blocks, span, _ = shifts.shape
    wide = w_heads.shape[1] // taps
    return pl.pallas_call(
        heads_data_kernel,
        grid=(taps,),
        in_specs=[
            pl.BlockSpec((rows, outs), lambda t: (0, 0)),
            pl.BlockSpec((outs, wide), lambda t: (0, t)),
            pl.BlockSpec((1, blocks, span, span), lambda t: (t, 0, 0, 0)),
        ],
        out_specs=pl.BlockSpec((rows, wide), lambda t: (0, 0)),
        out_shape=jax.ShapeDtypeStruct((rows, wide), BF16),
        scratch_shapes=[pltpu.VMEM((rows, wide), F32)],
        compiler_params=params(),
        cost_estimate=cost(2 * rows * wide * outs * taps, w_heads.size * 2),
        name="heads_data",
    )(g, w_heads, shifts)


def heads_weight_kernel(g_ref, u_ref, s_ref, out_ref):
    taken = shifted(g_ref, s_ref)
    step = 512
    for c in range(0, u_ref.shape[1], step):
        out_ref[:, c : c + step] = inner_rows(taken, u_ref[:, c : c + step]).astype(out_ref.dtype)


def heads_weight(g, u, shifts):
    rows, outs = g.shape
    wide = u.shape[1]
    taps, blocks, span, _ = shifts.shape
    return pl.pallas_call(
        heads_weight_kernel,
        grid=(taps,),
        in_specs=[
            pl.BlockSpec((rows, outs), lambda t: (0, 0)),
            pl.BlockSpec((rows, wide), lambda t: (0, 0)),
            pl.BlockSpec((1, blocks, span, span), lambda t: (t, 0, 0, 0)),
        ],
        out_specs=pl.BlockSpec((outs, wide), lambda t: (0, t)),
        out_shape=jax.ShapeDtypeStruct((outs, taps * wide), BF16),
        compiler_params=params(),
        cost_estimate=cost(2 * rows * wide * outs * taps, outs * taps * wide * 2),
        name="heads_weight",
    )(g, u, shifts)


def rows_forward_kernel(first_ref, u_ref, w_ref, s_ref, out_ref):
    blocks, span = s_ref.shape[1], s_ref.shape[2]

    @pl.when(pl.program_id(0) == 0)
    def _():
        out_ref[...] = jnp.zeros_like(out_ref)

    y = product(u_ref[...], w_ref[...]).astype(BF16)
    for k in range(blocks):
        at = pl.ds(k * span, span)
        out_ref[at, :] += product(s_ref[0, k], y[k * span : (k + 1) * span])


def rows_forward(first, u, w, shifts, halves):
    rows = u.shape[0]
    depth = u.shape[1] // halves
    outs = w.shape[1]
    steps = w.shape[0] // depth
    taps, blocks, span, _ = shifts.shape
    return pl.pallas_call(
        rows_forward_kernel,
        grid_spec=pltpu.PrefetchScalarGridSpec(
            num_scalar_prefetch=1,
            grid=(steps,),
            in_specs=[
                pl.BlockSpec((rows, depth), lambda b, f: (0, (b + f[0]) % halves)),
                pl.BlockSpec((depth, outs), lambda b, f: (b, 0)),
                pl.BlockSpec((1, blocks, span, span), lambda b, f: ((b + f[0]) // halves, 0, 0, 0)),
            ],
            out_specs=pl.BlockSpec((rows, outs), lambda b, f: (0, 0)),
        ),
        out_shape=jax.ShapeDtypeStruct((rows, outs), F32),
        compiler_params=params(),
        cost_estimate=cost(2 * rows * w.size, w.size * 2),
        name="rows_forward",
    )(first, u, w, shifts)


def rows_back_kernel(halves, first_ref, g_ref, u_ref, w_ref, s_ref, du_ref, dw_ref, total):
    step = pl.program_id(0)
    taken = shifted(g_ref, s_ref)
    depth = w_ref.shape[0]
    which = (step + first_ref[0]) % halves

    @pl.when(step == 0)
    def _():
        total[...] = jnp.zeros_like(total)

    total[which] += against(taken, w_ref[...])
    dw_ref[...] = inner_rows(u_ref[...], taken).astype(dw_ref.dtype)

    @pl.when(step == pl.num_programs(0) - 1)
    def _():
        for k in range(halves):
            du_ref[:, k * depth : (k + 1) * depth] = total[k].astype(du_ref.dtype)


def rows_back(first, g, u, w, shifts, halves, kind):
    rows, outs = g.shape
    depth = u.shape[1] // halves
    steps = w.shape[0] // depth
    taps, blocks, span, _ = shifts.shape
    return pl.pallas_call(
        functools.partial(rows_back_kernel, halves),
        grid_spec=pltpu.PrefetchScalarGridSpec(
            num_scalar_prefetch=1,
            grid=(steps,),
            in_specs=[
                pl.BlockSpec((rows, outs), lambda b, f: (0, 0)),
                pl.BlockSpec((rows, depth), lambda b, f: (0, (b + f[0]) % halves)),
                pl.BlockSpec((depth, outs), lambda b, f: (b, 0)),
                pl.BlockSpec((1, blocks, span, span), lambda b, f: ((b + f[0]) // halves, 0, 0, 0)),
            ],
            out_specs=[
                pl.BlockSpec((rows, halves * depth), lambda b, f: (0, 0)),
                pl.BlockSpec((depth, outs), lambda b, f: (b, 0)),
            ],
            scratch_shapes=[pltpu.VMEM((halves, rows, depth), F32)],
        ),
        out_shape=[
            jax.ShapeDtypeStruct((rows, halves * depth), kind),
            jax.ShapeDtypeStruct(w.shape, BF16),
        ],
        compiler_params=params(),
        cost_estimate=cost(4 * rows * w.size, w.size * 4),
        name="rows_back",
    )(first, g, u, w, shifts)


def silu_slope(value_in):
    sigma_of = jax.nn.sigmoid(value_in)
    return sigma_of * (1.0 + value_in * (1.0 - sigma_of))


MESH = pl.DeviceIdType.MESH


def greet(axes):
    barrier = pltpu.get_barrier_semaphore()
    count = 0
    for axis, size in axes:
        me = lax.axis_index(axis)
        for k in range(1, size):
            pl.semaphore_signal(
                barrier, inc=1, device_id={axis: lax.rem(me + k, size)}, device_id_type=MESH
            )
        count += size - 1
    pl.semaphore_wait(barrier, count)


def total_kernel(axes, x_ref, out_ref, *scratch):
    greet(axes)
    block = x_ref
    for number, (axis, size) in enumerate(axes):
        slots, stage, send_sems, recv_sems = scratch[4 * number : 4 * number + 4]
        me = lax.axis_index(axis)
        others = [lax.rem(me + k, size) for k in range(1, size)]
        for other in others:
            pltpu.make_async_remote_copy(
                src_ref=block,
                dst_ref=slots.at[me],
                send_sem=send_sems.at[other],
                recv_sem=recv_sems.at[me],
                device_id={axis: other},
                device_id_type=MESH,
            ).start()
        slots[me] = block[...]
        for other in others:
            copy = pltpu.make_async_remote_copy(
                src_ref=block,
                dst_ref=slots.at[other],
                send_sem=send_sems.at[other],
                recv_sem=recv_sems.at[other],
                device_id={axis: other},
                device_id_type=MESH,
            )
            copy.wait_recv()
            copy.wait_send()
        total = slots[0]
        for k in range(1, size):
            total = total + slots[k]
        if number == len(axes) - 1:
            out_ref[...] = total
        else:
            stage[...] = total
            block = stage


def total_of(left, right, axes):
    width = left.shape[0]
    packed = jnp.concatenate([left, right], 0).reshape(-1, 128)
    sized = tuple((axis, lax.axis_size(axis)) for axis in axes)
    scratch = []
    for _, size in sized:
        scratch += [
            pltpu.VMEM((size,) + packed.shape, F32),
            pltpu.VMEM(packed.shape, F32),
            pltpu.SemaphoreType.DMA((size,)),
            pltpu.SemaphoreType.DMA((size,)),
        ]
    number = 1 + (width != 512) + 2 * (len(axes) == 1)
    summed = pl.pallas_call(
        functools.partial(total_kernel, sized),
        out_shape=jax.ShapeDtypeStruct(packed.shape, F32),
        in_specs=[pl.BlockSpec(memory_space=pltpu.VMEM)],
        out_specs=pl.BlockSpec(memory_space=pltpu.VMEM),
        scratch_shapes=scratch,
        compiler_params=pltpu.CompilerParams(collective_id=number, has_side_effects=True),
        name="total",
    )(packed).reshape(2, width)
    return summed[0], summed[1]


def normalize(raw_value, column_sums, squares, pixel_count, norm_gain, norm_shift):
    center = column_sums / pixel_count
    spread_of = squares / pixel_count - center * center
    scaling = lax.rsqrt(spread_of + EPS)
    unit_value = (raw_value - center) * scaling
    return (unit_value * norm_gain + norm_shift, unit_value, scaling)


def moments(raw_value, living, axes):
    return total_of(
        jnp.sum(living * raw_value, 0), jnp.sum(living * raw_value * raw_value, 0), axes
    )


def norm_back(grad_out, unit_value, scaling, norm_gain, living, pixel_count, axes):
    grad_gain, grad_shift = total_of(
        jnp.sum(living * grad_out * unit_value, 0), jnp.sum(living * grad_out, 0), axes
    )
    grad_raw = (
        living
        * (norm_gain * scaling)
        * (grad_out - grad_shift / pixel_count - unit_value * grad_gain / pixel_count)
    )
    return (grad_raw, grad_gain, grad_shift)


def swap(value, bit):
    return lax.ppermute(value, "rep", [(k, k ^ bit) for k in range(4)])


def scatter_rep(value):
    return lax.psum_scatter(value.astype(BF16), "rep", scatter_dimension=0, tiled=True)


def total_dp(value):
    parts = lax.axis_size("dp")
    rows = value.shape[0]
    padded = -(-rows // (8 * parts)) * 8 * parts
    value = jnp.pad(value, ((0, padded - rows), (0, 0)))
    share = lax.psum_scatter(value, "dp", scatter_dimension=0, tiled=True)
    return lax.all_gather(share, "dp", axis=0, tiled=True)[:rows].astype(F32)


def shards(
    inputs,
    layout,
    labels,
    cot_depth,
    w_reduce,
    w_spatial,
    w_expand,
    w_heads,
    w_gates,
    w_messages,
    w_classes,
    gain_mid,
    shift_mid,
    gain_wide,
    shift_wide,
    gain_head,
    shift_head,
):
    pixels = inputs.shape[0]
    middle = w_reduce.shape[1]
    classes = w_classes.shape[1]
    group = lax.axis_size("rep")
    everyone = ("rep", "dp")
    rep = lax.axis_index("rep")
    parity = rep % 2
    upper = rep // 2
    first_row = lax.axis_index("dp") * group
    own_info = geometry(lax.dynamic_slice_in_dim(layout, first_row + rep, 1, 0), pixels)
    group_info = geometry(lax.dynamic_slice_in_dim(layout, first_row, group, 0), pixels)
    living = own_info[2][0].astype(F32)[:, None]
    group_living = group_info[2].astype(F32)
    living_all = group_living.reshape(group * pixels, 1)
    pixel_count = jnp.sum(
        jnp.minimum(layout[:, 0] * layout[:, 1] * layout[:, 2], pixels)
    ).astype(F32)
    shifts_own = shift_matrices(own_info, 2)
    shifts_all = shift_matrices(group_info, 1)
    zero = jnp.zeros((1,), jnp.int32)
    first = jnp.reshape(9 * parity, (1,)).astype(jnp.int32)

    reduced = product(inputs, w_reduce)
    sums_one, squares_one = moments(reduced, living, everyone)
    normed_one, unit_one, scale_one = normalize(
        reduced, sums_one, squares_one, pixel_count, gain_mid[0], shift_mid[0]
    )
    hidden_one = jax.nn.silu(normed_one).astype(BF16)
    spatial = rows_forward(zero, hidden_one, w_spatial, shifts_own, 1)
    sums_two, squares_two = moments(spatial, living, everyone)
    normed_two, unit_two, scale_two = normalize(
        spatial, sums_two, squares_two, pixel_count, gain_mid[1], shift_mid[1]
    )
    hidden_two = jax.nn.silu(normed_two).astype(BF16)
    expanded = product(hidden_two, w_expand)
    sums_three, squares_three = moments(expanded, living, everyone)
    normed_three, unit_three, scale_three = normalize(
        expanded, sums_three, squares_three, pixel_count, gain_wide, shift_wide
    )
    pre_act = normed_three + inputs.astype(F32)
    trunk = jax.nn.silu(pre_act).astype(BF16)
    trunk_all = lax.all_gather(trunk, "rep", axis=0, tiled=True)

    headed = heads_forward(trunk_all, w_heads, shifts_all)
    own_gain = lax.dynamic_slice_in_dim(gain_head, rep * middle, middle, 0)
    own_shift = lax.dynamic_slice_in_dim(shift_head, rep * middle, middle, 0)
    sums_head, squares_head = moments(headed, living_all, ("dp",))
    normed_head, unit_head, scale_head = normalize(
        headed, sums_head, squares_head, pixel_count, own_gain, own_shift
    )
    rounded = jax.nn.silu(normed_head).astype(BF16)
    heads_all = lax.all_gather(rounded, "rep", axis=0, tiled=False)

    is_depth = upper == 0
    source = jnp.where(
        is_depth,
        jnp.concatenate([heads_all[1], heads_all[2], heads_all[3]], 1),
        jnp.concatenate([heads_all[0], heads_all[1], heads_all[2]], 1),
    )
    partial = rows_forward(first, source, w_messages, shifts_all, 2).reshape(
        2, 2, pixels, middle
    )

    def of_parity(value, which):
        return lax.dynamic_index_in_dim(value, which, 1, keepdims=False)

    def rows_of(value):
        return value.reshape(2 * pixels, value.shape[-1])

    message = rows_of(of_parity(partial, parity) + swap(of_parity(partial, 1 - parity), 1))
    stream = rows_of(
        of_parity(
            jnp.where(is_depth, heads_all[0], heads_all[3]).reshape(2, 2, pixels, middle), parity
        )
    )
    own_gates = lax.dynamic_slice_in_dim(w_gates, upper * middle, middle, 0)
    stream_living = rows_of(of_parity(group_living.reshape(2, 2, pixels, 1), parity))
    cot_other = swap(cot_depth, 2)
    labels_other = swap(labels, 2)
    stream_cot = jnp.concatenate([cot_depth, cot_other], 0).astype(F32)
    stream_labels = jnp.concatenate([labels_other, labels], 0)
    gate = jax.nn.sigmoid(product(stream, own_gates))
    full = stream.astype(F32) + gate * message
    full_low = full.astype(BF16)
    logits_full = product(full_low, w_classes)
    probs = jax.nn.softmax(logits_full, axis=1)
    onehot_table = (
        stream_labels[:, None] == jnp.arange(classes, dtype=jnp.int32)[None, :]
    ).astype(F32)
    grad_logits = (stream_living * (probs - onehot_table)).astype(BF16)
    classes_local = inner_rows(full_low, jnp.where(is_depth, 0.0, 1.0).astype(BF16) * grad_logits)
    grad_stream = jnp.where(
        is_depth, stream_living * stream_cot, against(grad_logits, w_classes)
    )
    depth_other = swap(full[pixels:], 2)
    logits_other = swap(logits_full[:pixels], 2)
    depth = living * jnp.where(is_depth, full[:pixels], depth_other)
    logits = living * jnp.where(is_depth, logits_other, logits_full[pixels:])
    grad_gate = (grad_stream * message * gate * (1.0 - gate)).astype(BF16)
    grad_message = (grad_stream * gate).astype(BF16)
    gates_local = inner_rows(stream, grad_gate).astype(BF16)
    gates_local = gates_local.reshape(2, pixels, middle)
    gates_share = lax.dynamic_index_in_dim(gates_local, parity, 0, keepdims=False).astype(
        F32
    ) + swap(lax.dynamic_index_in_dim(gates_local, 1 - parity, 0, keepdims=False), 1).astype(F32)
    direct = (grad_stream + against(grad_gate, own_gates)).astype(BF16)

    def both_parities(value, other):
        value = value.reshape(2, pixels, middle)
        other = other.reshape(2, pixels, middle)
        even = jnp.where(parity == 0, value, other)
        odd = jnp.where(parity == 0, other, value)
        return jnp.stack([even, odd], 1).reshape(4 * pixels, middle)

    message_all = both_parities(grad_message, swap(grad_message, 1))
    direct_all = both_parities(direct, jnp.zeros_like(direct))
    source_grad, messages_local = rows_back(
        first, message_all, source, w_messages, shifts_all, 2, BF16
    )
    thirds = [source_grad[:, k * middle : (k + 1) * middle] for k in range(3)]
    by_head = jnp.stack(
        [
            jnp.where(is_depth, direct_all, thirds[0]),
            jnp.where(is_depth, thirds[0], thirds[1]),
            jnp.where(is_depth, thirds[1], thirds[2]),
            jnp.where(is_depth, thirds[2], direct_all),
        ],
        0,
    )
    feat_grad = lax.psum_scatter(by_head, "rep", scatter_dimension=0, tiled=False).astype(F32)
    grad_messages = lax.psum_scatter(messages_local, "dp", scatter_dimension=1, tiled=True)
    head_raw, gain_grad_head, shift_grad_head = norm_back(
        feat_grad * silu_slope(normed_head),
        unit_head,
        scale_head,
        own_gain,
        living_all,
        pixel_count,
        ("dp",),
    )
    head_low = head_raw.astype(BF16)
    heads_local = heads_weight(head_low, trunk_all, shifts_all)
    head_low, heads_local = lax.optimization_barrier((head_low, heads_local))
    grad_heads = lax.psum_scatter(heads_local, "dp", scatter_dimension=1, tiled=True)
    trunk_grad = lax.psum_scatter(
        heads_data(head_low, w_heads, shifts_all), "rep", scatter_dimension=0, tiled=True
    ).astype(F32)
    pre_grad = trunk_grad * silu_slope(pre_act)
    expand_raw, grad_gain_wide, grad_shift_wide = norm_back(
        pre_grad, unit_three, scale_three, gain_wide, living, pixel_count, everyone
    )
    expand_low = expand_raw.astype(BF16)
    grad_expand = scatter_rep(inner_rows(hidden_two, expand_low))
    hidden_two_grad = against(expand_low, w_expand)
    spatial_raw, gain_grad_two, shift_grad_two = norm_back(
        hidden_two_grad * silu_slope(normed_two),
        unit_two,
        scale_two,
        gain_mid[1],
        living,
        pixel_count,
        everyone,
    )
    spatial_low = spatial_raw.astype(BF16)
    hidden_one_grad, spatial_local = rows_back(
        zero, spatial_low, hidden_one, w_spatial, shifts_own, 1, F32
    )
    grad_spatial = scatter_rep(spatial_local)
    reduced_raw, gain_grad_one, shift_grad_one = norm_back(
        hidden_one_grad * silu_slope(normed_one),
        unit_one,
        scale_one,
        gain_mid[0],
        living,
        pixel_count,
        everyone,
    )
    reduced_low = reduced_raw.astype(BF16)
    grad_reduce = scatter_rep(inner_rows(inputs, reduced_low))
    input_grad = pre_grad + against(reduced_low, w_reduce)
    grad_classes = scatter_rep(classes_local)
    pieces = [
        gates_share.astype(BF16),
        grad_expand.reshape(-1, middle),
        grad_spatial,
        grad_classes.reshape(-1, middle),
    ]
    early = total_dp(jnp.concatenate(pieces, 0))
    rows = [piece.shape[0] for piece in pieces]
    starts = [sum(rows[:k]) for k in range(4)]
    grad_gates, expand_sum, grad_spatial, classes_sum = [
        early[at : at + size] for at, size in zip(starts, rows)
    ]
    grad_expand = expand_sum.reshape(grad_expand.shape)
    grad_classes = classes_sum.reshape(grad_classes.shape)
    grad_reduce = total_dp(grad_reduce)
    grad_gain_mid = jnp.stack([gain_grad_one, gain_grad_two], 0)
    grad_shift_mid = jnp.stack([shift_grad_one, shift_grad_two], 0)
    head_norms = lax.all_gather(
        jnp.stack([gain_grad_head, shift_grad_head], 0), "rep", axis=1, tiled=True
    )
    return (
        depth,
        logits,
        input_grad,
        grad_reduce,
        grad_spatial,
        grad_expand,
        grad_heads.astype(F32),
        grad_gates,
        grad_messages.astype(F32),
        grad_classes,
        grad_gain_mid,
        grad_shift_mid,
        grad_gain_wide,
        grad_shift_wide,
        head_norms[0],
        head_norms[1],
    )


def solution(mesh):
    in_specs = (
        P(("dp", "rep"), None),
        P(),
        P(("dp", "rep")),
        P(("dp", "rep"), None),
        P(),
        P(),
        P(),
        P("rep", None),
        P(),
        P("rep", None),
        P(),
        P(),
        P(),
        P(),
        P(),
        P(),
        P(),
    )
    out_specs = (
        P(("dp", "rep"), None),
        P(("dp", "rep"), None),
        P(("dp", "rep"), None),
        P("rep", None),
        P("rep", None),
        P("rep", None),
        P("rep", "dp"),
        P("rep", None),
        P("rep", "dp"),
        P("rep", None),
        P(),
        P(),
        P(),
        P(),
        P(),
        P(),
    )
    return jax.shard_map(shards, mesh=mesh, in_specs=in_specs, out_specs=out_specs, check_vma=False)
```

time: 2200 us -> 1240 us (0.56)
  blocking collectives: 601 us -> 35.4 us
  Pallas kernels: 0 us -> 238 us
  matrix products: 231 us -> 24.9 us
  other arithmetic: 293 us -> 88.8 us
  local copies, waits for them, and re-layouts: 135 us -> 37.7 us
  between operations: 88.5 us -> 23 us
  waiting for transfers between devices: 829 us -> 776 us
    psum x9 -> x0, blocking collectives: 601 us -> none  [the longest x1 276 us: shards(): lax.psum((every_share[0], every_share[1], every_share[2], every_share[3],...]
    pallas_call x0 -> x15, Pallas kernels: none -> 238 us  [the longest x8 84.4 us: total_of(): pl.pallas_call(functools.partial(total_kernel, sized), out_shape=jax.Shap...]
    reduce_scatter x7 -> x8, waiting for transfers between devices: 373 us -> 258 us  [the longest x2 124 us: total_dp(): share = lax.psum_scatter(value, 'dp', scatter_dimension=0, tiled=True)]
    reduce_scatter x1, waiting for transfers between devices: 422 us -> 308 us  [shards(): lax.psum_scatter(heads_local, 'dp', scatter_dimension=1, tiled=True)]
    dot_general x14 -> x4, matrix products: 115 us -> 6.79 us  [product(): return jnp.dot(left_side, right_side, preferred_element_type=F32)]
    unnamed x12 -> x14, waiting for transfers between devices: 13 us -> 121 us
    all_gather x2 -> x3, waiting for transfers between devices: 0.02 us -> 81.3 us  [the longest x1 34.4 us: shards(): heads_all = lax.all_gather(rounded, 'rep', axis=0, tiled=False)]
    mul x13 -> x2, other arithmetic: 69.9 us -> 0.63 us  [the longest x1 0.63 us: shards(): logits = living * jnp.where(is_depth, logits_other, logits_full[pixels:])]
  transfers between devices with their start and end apart: 13 -> 20, of which waited for: 8 -> 15; matrix products, arithmetic and copies ran while one was open for 14% -> 7% of each run, Pallas kernels for 0% -> 4%
where the time goes in v1:
time: 1240 us; the launch traced here: 1230 us
  waiting for transfers between devices  776 us (63%)
  Pallas kernels  238 us (19%)
  other arithmetic  88.8 us (7%)
  local copies, waits for them, and re-layouts  37.7 us (3%)
  blocking collectives  35.4 us (3%)
  matrix products  24.9 us (2%)
  between operations  23 us (2%)
    reduce_scatter x1, waiting for transfers between devices, shards(): lax.psum_scatter(heads_local, 'dp', scatter_dimension=1, tiled=True)  308 us
    reduce_scatter x2, waiting for transfers between devices, total_dp(): share = lax.psum_scatter(value, 'dp', scatter_dimension=0, tiled=True)  124 us
    unnamed x14, waiting for transfers between devices  121 us
    pallas_call x8, Pallas kernels, total_of(): pl.pallas_call(functools.partial(total_kernel, sized), out_shape=jax.Shap...  84.4 us
    reduce_scatter x4, waiting for transfers between devices, scatter_rep(): lax.psum_scatter(value.astype(BF16), 'rep', scatter_dimension=0, tiled=True)  45.9 us
    reduce_scatter x1, waiting for transfers between devices, shards(): lax.psum_scatter(by_head, 'rep', scatter_dimension=0, tiled=False)  44.5 us
    reduce_scatter x1, waiting for transfers between devices, shards(): lax.psum_scatter(heads_data(head_low, w_heads, shifts_all), 'rep', scatte...  43 us
    pallas_call x2, Pallas kernels, rows_back(): pl.pallas_call(functools.partial(rows_back_kernel, halves), grid_spec=plt...  37.1 us
  transfers between devices with their start and end apart: 20, of which 15 were waited for; matrix products, arithmetic and copies ran while one was open for 7% of the time, Pallas kernels for 4%

profile of v1, /device:TPU:28, one launch (start us, length us, event | category | flops | bytes accessed | tf_op | source)
XLA Modules:
  0.0 1228.6 jit_solution(8892028379851750432)
XLA Ops:
  15.9 2.6 multiply_reduce_fusion.7
  19.2 10.1 total.8
  32.9 1.6 and_select_fusion.4
  39.9 8.8 rows_forward.2
  50.6 11.1 total.9
  63.9 3.3 multiply_reduce_fusion.1
  67.8 11.5 total.10
  81.3 3.4 multiply_convert_fusion.3
  87.8 3.3 convert_element_type.146.s_ref
  91.9 27.7 %all-gather.5.cloned.1.call-done.u_ref = bf16[1024,2048]{1,0:T(8,128)(2,1)} async-done(((bf16[256,2048]{1,0:T(8,128)(2,1)}), bf16[1024,2048]{1,0:T(8,128)(2,1)}) %all-gather.5.cloned.1.call-update) | async-done | bytes 4194320 | tf_op jit(solution)/shard_map/all_gather | solution.py:466
  119.6 32.1 %heads_forward.1 = f32[1024,512]{1,0:T(8,128)} custom-call(bf16[1024,2048]{1,0:T(8,128)(2,1)} %all-gather.5.cloned.1.call-done.u_ref, bf16[512,18432]{1,0:T(8,128)(2,1)} %w_ref.10, bf16[9,4,256,256]{3,2,1,0:T(8,128)(2,1)} %convert_element_type.146.s_ref), custom_call_target="tpu_custom_call" | custom-call | flops 19327352832 | bytes 23068672 | tf_op jit(solution)/shard_map/heads_forward/pallas_call | solution.py:97
  151.7 1.9 multiply_reduce_fusion
  154.2 7.9 total.11
  164.2 3.2 multiply_convert_fusion.2
  167.7 34.4 %all-gather.9.cloned.1.call-done = bf16[4096,512]{1,0:T(8,128)(2,1)} async-done(((bf16[1024,512]{1,0:T(8,128)(2,1)}), bf16[4096,512]{1,0:T(8,128)(2,1)}) %all-gather.9.cloned.1.call-update) | async-done | bytes 4194320 | tf_op jit(solution)/shard_map/all_gather | solution.py:476
  202.2 2.5 fusion.92
  204.7 2.1 maximum_select_fusion.u_ref
  206.7 16.6 %rows_forward.3 = f32[1024,512]{1,0:T(8,128)} custom-call(s32[1]{0:T(128)} %bitcast.67.first_ref, bf16[1024,1536]{1,0:T(8,128)(2,1)} %maximum_select_fusion.u_ref, bf16[6912,512]{1,0:T(8,128)(2,1)} %w_ref.9, bf16[9,4,256,256]{3,2,1,0:T(8,128)(2,1)} %convert_element_type.146.s_ref), custom_call_target="tpu_custom_call" | custom-call | flops 7247757312 | bytes 7077888 | tf_op jit(solution)/shard_map/rows_forward/pallas_call | solution.py:209
  223.3 2.3 dynamic-slice_bitcast_fusion
  229.3 2.0 bitcast_add_fusion
  232.5 3.2 collective-permute-done.3
  235.6 2.8 multiply_convert_fusion.4
  238.5 2.0 broadcast_select_fusion.4
  244.1 26.1 %rows_back.2 = (bf16[1024,1536]{1,0:T(8,128)(2,1)}, bf16[6912,512]{1,0:T(8,128)(2,1)}) custom-call(s32[1]{0:T(128)} %bitcast.67.first_ref, bf16[1024,512]{1,0:T(8,128)(2,1)} %bitcast.267, bf16[1024,1536]{1,0:T(8,128)(2,1)} %maximum_select_fusion.u_ref, bf16[6912,512]{1,0:T(8,128)(2,1)} %w_ref.9, bf16[9,4,256,256]{3,2,1,0:T(8,128)(2,1)} %convert_element_type.146.s_ref), custom_call_target="tpu_custom_call" | custom-call | flops 14495514624 | bytes 14155776 | tf_op jit(solution)/shard_map/rows_back/pallas_call | solution.py:252
  270.2 2.5 bitcast_select_fusion.1
  272.7 2.3 pad_maximum_fusion
  275.3 44.5 %reduce-scatter.17.cloned.1.call-done = bf16[1,1024,512]{2,1,0:T(8,128)(2,1)} async-done(((bf16[4,1024,512]{2,1,0:T(8,128)(2,1)}), bf16[1,1024,512]{2,1,0:T(8,128)(2,1)}) %reduce-scatter.17.cloned.1.call-update) | async-done | bytes 1048592 | tf_op jit(solution)/shard_map/reduce_scatter | solution.py:554
  319.8 3.2 multiply_reduce_fusion.3
  323.6 7.9 total.12
  332.9 4.2 multiply_convert_fusion.1.g_ref
  337.1 28.0 %heads_weight.1 = bf16[512,18432]{1,0:T(8,128)(2,1)} custom-call(bf16[1024,512]{1,0:T(8,128)(2,1)} %multiply_convert_fusion.1.g_ref, bf16[1024,2048]{1,0:T(8,128)(2,1)} %all-gather.5.cloned.1.call-done.u_ref, bf16[9,4,256,256]{3,2,1,0:T(8,128)(2,1)} %convert_element_type.146.s_ref), custom_call_target="tpu_custom_call" | custom-call | flops 19327352832 | bytes 18874368 | tf_op jit(solution)/shard_map/heads_weight/pallas_call | solution.py:174
  365.1 30.5 %heads_data.1 = bf16[1024,2048]{1,0:T(8,128)(2,1)} custom-call(bf16[1024,512]{1,0:T(8,128)(2,1)} %multiply_convert_fusion.1.g_ref, bf16[512,18432]{1,0:T(8,128)(2,1)} %w_ref.10, bf16[9,4,256,256]{3,2,1,0:T(8,128)(2,1)} %convert_element_type.146.s_ref), custom_call_target="tpu_custom_call" | custom-call | flops 19327352832 | bytes 18874368 | tf_op jit(solution)/shard_map/heads_data/pallas_call | solution.py:146
  397.3 43.0 %reduce-scatter.19.cloned.1.call-done = bf16[256,2048]{1,0:T(8,128)(2,1)} async-done(((bf16[1024,2048]{1,0:T(8,128)(2,1)}), bf16[256,2048]{1,0:T(8,128)(2,1)}) %reduce-scatter.19.cloned.1.call-update) | async-done | bytes 1048592 | tf_op jit(solution)/shard_map/reduce_scatter | solution.py:569
  440.3 4.9 multiply_reduce_fusion.2
  445.8 12.4 %total.13 = f32[32,128]{1,0:T(8,128)} custom-call(f32[32,128]{1,0:T(8,128)} %pad_maximum_fusion.4.x_ref), custom_call_target="tpu_custom_call" | custom-call | tf_op jit(solution)/shard_map/total/pallas_call | solution.py:351
  460.3 2.9 multiply_convert_fusion
  464.2 2.2 convolution_convert_fusion
  466.7 3.1 multiply_reduce_fusion.9
  470.3 10.3 total.14
  481.4 2.1 multiply_convert_fusion.6.g_ref
  483.5 11.0 rows_back.3
  495.4 1.7 collective-permute-start.1
  497.1 2.3 multiply_reduce_fusion.8
  500.1 13.1 %total.15 = f32[8,128]{1,0:T(8,128)} custom-call(f32[8,128]{1,0:T(8,128)} %pad_maximum_fusion.10.x_ref), custom_call_target="tpu_custom_call" | custom-call | tf_op jit(solution)/shard_map/total/pallas_call | solution.py:351
  514.0 2.4 multiply_convert_fusion.5
  516.4 2.1 fusion.4
  525.1 24.0 %reduce-scatter.25.cloned.1.call-done = bf16[1152,512]{1,0:T(8,128)(2,1)} async-done(((bf16[4608,512]{1,0:T(8,128)(2,1)}), bf16[1152,512]{1,0:T(8,128)(2,1)}) %reduce-scatter.25.cloned.1.call-update) | async-done | bytes 1179664 | tf_op jit(solution)/shard_map/reduce_scatter | solution.py:394
  549.1 2.4 fusion.9
  551.6 10.3 copy.60
  561.9 21.8 %reduce-scatter.21.cloned.1.call-done = bf16[512,512]{0,1:T(8,128)(2,1)} async-done(((bf16[2048,512]{0,1:T(8,128)(2,1)}), bf16[512,512]{0,1:T(8,128)(2,1)}) %reduce-scatter.21.cloned.1.call-update) | async-done | bytes 524304 | tf_op jit(solution)/shard_map/reduce_scatter | solution.py:394
  583.8 2.0 copy.56
  585.9 68.8 %reduce-scatter.27.cloned.1.call-done = bf16[248,512]{1,0:T(8,128)(2,1)} async-done(((bf16[1984,512]{1,0:T(8,128)(2,1)}), bf16[248,512]{1,0:T(8,128)(2,1)}) %reduce-scatter.27.cloned.1.call-update) | async-done | bytes 253968 | tf_op jit(solution)/shard_map/reduce_scatter | solution.py:402
  656.1 3.4 collective-permute-done.2
  660.2 5.2 all_gather.23
  666.0 119.8 %reduce-scatter.35.cloned.1.call-done = bf16[64,6912]{1,0:T(8,128)(2,1)} async-done(((bf16[512,6912]{1,0:T(8,128)(2,1)}), bf16[64,6912]{1,0:T(8,128)(2,1)}) %reduce-scatter.35.cloned.1.call-update) | async-done | bytes 884752
  785.7 2.6 copy.61
  788.3 2.7 copy.54
  792.2 4.3 convolution_add_fusion
  796.4 55.4 %reduce-scatter.31.cloned.1.call-done = bf16[64,512]{1,0:T(8,128)(2,1)} async-done(((bf16[512,512]{1,0:T(8,128)(2,1)}), bf16[64,512]{1,0:T(8,128)(2,1)}) %reduce-scatter.31.cloned.1.call-update) | async-done | bytes 65552 | tf_op jit(solution)/shard_map/reduce_scatter | solution.py:402
  851.8 30.2 %all_gather.21 = bf16[512,512]{1,0:T(8,128)(2,1)S(1)} all-gather(bf16[64,512]{1,0:T(8,128)(2,1)} %reduce-scatter.31.cloned.1.call-done), channel_id=1, replica_groups=mesh['dp'=8,'rep'=4] {'dp'}, dimensions={0}, use_global_device_ids=true | all-gather | bytes 589824 | tf_op jit(solution)/shard_map/all_gather | solution.py:403
  883.1 19.2 %all-gather.7.cloned.1.call-done = bf16[1984,512]{1,0:T(8,128)(2,1)} async-done(((bf16[248,512]{1,0:T(8,128)(2,1)}), bf16[1984,512]{1,0:T(8,128)(2,1)}) %all-gather.7.cloned.1.call-update) | async-done | bytes 2031632 | tf_op jit(solution)/shard_map/all_gather | solution.py:403
  902.3 2.1 slice_convert_fusion
  909.2 308.2 %reduce-scatter.29.cloned.1.call-done = bf16[512,2304]{1,0:T(8,128)(2,1)} async-done(((bf16[512,18432]{1,0:T(8,128)(2,1)}), bf16[512,2304]{1,0:T(8,128)(2,1)}) %reduce-scatter.29.cloned.1.call-update) | async-done | bytes 2359312 | tf_op jit(solution)/shard_map/reduce_scatter | solution.py:568
  1217.4 4.2 convert_element_type.178
  (226 shorter events, 59.9 us)
Async XLA Ops:
  7.2 56.7 %copy-start = (bf16[512,2048]{1,0:T(8,128)(2,1)S(1)}, bf16[512,2048]{1,0:T(8,128)(2,1)}, u32[]{:S(2)}) copy-start(bf16[512,2048]{1,0:T(8,128)(2,1)} %param.25) | copy-start | bytes 6291460
  7.2 112.4 %all-gather.5.cloned.1.call-start = ((), (), s32[]{:S(2)}) async-start(), calls=%async_computation.10 | async-start | bytes 5242880 | tf_op jit(solution)/shard_map/all_gather | solution.py:466
  15.2 17.6 %copy-start.29 = (f32[2,512]{1,0:T(2,128)S(1)}, f32[2,512]{1,0:T(2,128)}, u32[]{:S(2)}) copy-start(f32[2,512]{1,0:T(2,128)} %param.30) | copy-start | bytes 12292
  15.9 17.0 %copy-start.39 = (f32[2,512]{1,0:T(2,128)S(1)}, f32[2,512]{1,0:T(2,128)}, u32[]{:S(2)}) copy-start(f32[2,512]{1,0:T(2,128)} %param.31) | copy-start | bytes 12292
  18.5 30.2 %copy-start.3 = (f32[256,512]{1,0:T(8,128)}, f32[256,512]{1,0:T(8,128)S(1)}, u32[]{:S(2)}) copy-start(f32[256,512]{1,0:T(8,128)S(1)} %get-tuple-element.188) | copy-start | bytes 1572868
  30.1 18.7 %copy-start.16 = (f32[512]{0:T(512)}, f32[512]{0:T(512)S(1)}, u32[]{:S(2)}) copy-start(f32[512]{0:T(512)S(1)} %fusion.82) | copy-start | bytes 6148
  32.8 16.0 %copy-start.24 = (f32[1,512]{1,0:T(1,128)}, f32[1,512]{1,0:T(1,128)S(1)}, u32[]{:S(2)}) copy-start(f32[1,512]{1,0:T(1,128)S(1)} %slice.181) | copy-start | bytes 6148
  32.9 15.9 %copy-start.26 = (f32[1,512]{1,0:T(1,128)}, f32[1,512]{1,0:T(1,128)S(1)}, u32[]{:S(2)}) copy-start(f32[1,512]{1,0:T(1,128)S(1)} %get-tuple-element.157) | copy-start | bytes 6148
  32.9 31.0 %copy-start.42 = (f32[1,512]{1,0:T(1,128)}, f32[1,512]{1,0:T(1,128)S(1)}, u32[]{:S(2)}) copy-start(f32[1,512]{1,0:T(1,128)S(1)} %get-tuple-element.156) | copy-start | bytes 6148
  62.5 4.7 copy-start.33
  63.3 3.9 copy-start.30
  63.9 3.3 copy-start.40
  63.9 15.4 %copy-start.12 = (f32[2048]{0:T(1024)S(1)}, f32[2048]{0:T(1024)}, u32[]{:S(2)}) copy-start(f32[2048]{0:T(1024)} %param.32) | copy-start | bytes 24580
  63.9 17.4 %copy-start.1 = (bf16[256,2048]{1,0:T(8,128)(2,1)S(1)}, bf16[256,2048]{1,0:T(8,128)(2,1)}, u32[]{:S(2)}) copy-start(bf16[256,2048]{1,0:T(8,128)(2,1)} %param.19) | copy-start | bytes 3145732
  63.9 17.4 %copy-start.13 = (f32[2048]{0:T(1024)S(1)}, f32[2048]{0:T(1024)}, u32[]{:S(2)}) copy-start(f32[2048]{0:T(1024)} %param.33) | copy-start | bytes 24580
  81.3 3.4 copy-start.28
  84.7 117.4 %all-gather.9.cloned.1.call-start = ((), (), s32[]{:S(2)}) async-start(), calls=%async_computation.19 | async-start | bytes 5242880 | tf_op jit(solution)/shard_map/all_gather | solution.py:476
  167.5 152.3 %reduce-scatter.17.cloned.1.call-start = ((), (), s32[]{:S(2)}) async-start(), calls=%async_computation.11 | async-start | bytes 5242880 | tf_op jit(solution)/shard_map/reduce_scatter | solution.py:554
  223.3 2.4 copy-start.44
  223.3 3.8 copy-start.9
  225.6 3.7 collective-permute-start
  225.7 3.6 collective-permute-start.4
  227.1 8.5 collective-permute-start.3
  229.2 6.4 copy-start.22
  229.2 2.1 copy-start.10
  229.3 2.7 copy-start.8
  231.3 0.8 copy-start.11
  231.3 4.3 copy-start.20
  232.4 6.0 copy-start.18
  238.5 3.2 collective-permute-start.5
  275.0 57.8 %copy-start.35 = (f32[512]{0:T(512)S(1)}, f32[512]{0:T(512)}, u32[]{:S(2)}) copy-start(f32[512]{0:T(512)} %get-tuple-element.99) | copy-start | bytes 6148
  275.0 165.3 %reduce-scatter.19.cloned.1.call-start = ((), (), s32[]{:S(2)}) async-start(), calls=%async_computation.12 | async-start | bytes 5242880 | tf_op jit(solution)/shard_map/reduce_scatter | solution.py:569
  395.6 0.7 copy-start.21
  395.6 0.7 copy-start.23
  395.6 125.6 %reduce-scatter.33.cloned.1.call-start = ((), (), s32[]{:S(2)}) async-start(), calls=%async_computation.21 | async-start | bytes 163840 | tf_op jit(solution)/shard_map/reduce_scatter | solution.py:394
  397.3 63.0 %copy-start.15 = (f32[2048]{0:T(1024)S(1)}, f32[2048]{0:T(1024)}, u32[]{:S(2)}) copy-start(f32[2048]{0:T(1024)} %get-tuple-element.94) | copy-start | bytes 24580
  397.3 126.4 %reduce-scatter.23.cloned.1.call-start = ((), (), s32[]{:S(2)}) async-start(), calls=%async_computation.14 | async-start | bytes 2621440 | tf_op jit(solution)/shard_map/reduce_scatter | solution.py:394
  458.9 4.2 copy-start.14
  460.2 3.9 copy-start.4
  460.2 3.9 copy-start.31
  460.2 3.9 copy-start.34
  460.2 3.9 copy-start.41
  460.3 3.9 copy-start.43
  463.2 1.0 copy-start.6
  466.4 15.0 %copy-start.32 = (f32[1,512]{1,0:T(1,128)S(1)}, f32[1,512]{1,0:T(1,128)}, u32[]{:S(2)}) copy-start(f32[1,512]{1,0:T(1,128)} %get-tuple-element.140) | copy-start | bytes 6148
  466.4 82.7 %reduce-scatter.25.cloned.1.call-start = ((), (), s32[]{:S(2)}) async-start(), calls=%async_computation.15 | async-start | bytes 5898240 | tf_op jit(solution)/shard_map/reduce_scatter | solution.py:394
  494.5 2.7 copy-start.17
  494.5 2.7 copy-start.25
  494.5 2.7 copy-start.27
  494.5 19.5 %copy-start.38 = (f32[1,512]{1,0:T(1,128)S(1)}, f32[1,512]{1,0:T(1,128)}, u32[]{:S(2)}) copy-start(f32[1,512]{1,0:T(1,128)} %get-tuple-element.139) | copy-start | bytes 6148
  494.5 89.3 %reduce-scatter.21.cloned.1.call-start = ((), (), s32[]{:S(2)}) async-start(), calls=%async_computation.13 | async-start | bytes 2621440 | tf_op jit(solution)/shard_map/reduce_scatter | solution.py:394
  495.4 18.6 %collective-permute-start.1 = (f32[256,512]{1,0:T(8,128)}, f32[256,512]{1,0:T(8,128)}, u32[]{:S(2)}, u32[]{:S(2)}) collective-permute-start(f32[256,512]{1,0:T(8,128)} %slice.234), channel_id=1, source_target_pairs={{0,2},{1,3},{2,0},{3,1},{4,6},{5,7},{6,4},{7,5},{8,10},{9,11},{10,... | collective-permute-start | bytes 1572872 | tf_op jit(solution)/shard_map/ppermute | solution.py:390
  513.2 3.2 copy-start.2
  518.5 1.0 copy-start.5
  518.5 136.1 %reduce-scatter.27.cloned.1.call-start = ((), (), s32[]{:S(2)}) async-start(), calls=%async_computation.16 | async-start | bytes 2285568 | tf_op jit(solution)/shard_map/reduce_scatter | solution.py:402
  521.0 1.1 copy-start.7
  521.1 1.6 collective-permute-start.6
  551.5 234.2 %reduce-scatter.35.cloned.1.call-start = ((), (), s32[]{:S(2)}) async-start(), calls=%async_computation.22 | async-start | bytes 7962624
  561.9 289.9 %reduce-scatter.31.cloned.1.call-start = ((), (), s32[]{:S(2)}) async-start(), calls=%async_computation.20 | async-start | bytes 589824 | tf_op jit(solution)/shard_map/reduce_scatter | solution.py:402
  585.9 316.5 %all-gather.7.cloned.1.call-start = ((), (), s32[]{:S(2)}) async-start(), calls=%async_computation.17 | async-start | bytes 2285568 | tf_op jit(solution)/shard_map/all_gather | solution.py:403
  654.7 5.5 copy-start.36
  654.7 5.5 copy-start.37
  654.7 562.7 %reduce-scatter.29.cloned.1.call-start = ((), (), s32[]{:S(2)}) async-start(), calls=%async_computation.18 | async-start | bytes 21233664 | tf_op jit(solution)/shard_map/reduce_scatter | solution.py:568
  655.5 4.1 collective-permute-start.2
  (1 other events, 0.7 us)
Sparse Core Ops, SparseCore 0:
  84.8 34.6 all-gather.4
  167.6 34.5 all-gather.8
  275.1 44.6 reduce-scatter.16
  395.7 44.5 reduce-scatter.18
  442.6 19.5 reduce-scatter.32
  466.5 31.5 reduce-scatter.22
  501.2 47.8 reduce-scatter.24
  552.3 31.3 reduce-scatter.20
  587.8 66.7 reduce-scatter.26
  658.2 127.5 reduce-scatter.34
  790.0 61.7 reduce-scatter.30
  853.9 48.4 all-gather.6
  906.2 311.1 reduce-scatter.28

commit v2 on v1

--- a/solution.py
+++ b/solution.py
@@ -274,6 +274,284 @@
         cost_estimate=cost(4 * rows * w.size, w.size * 4),
         name="rows_back",
     )(first, g, u, w, shifts)
+
+
+def heads_split_kernel(per_tap, units, lanes, x_ref, g_ref, h_ref, u_ref, v_ref, s_ref, r_ref, out_ref, taken):
+    blocks, span = s_ref.shape[1], s_ref.shape[2]
+    rows = blocks * span
+    start = units * (2 * pl.program_id(0) + x_ref[0])
+
+    @pl.loop(0, units)
+    def _(unit):
+        tap, chunk = (start + unit) // per_tap, (start + unit) % per_tap
+
+        @pl.when((unit == 0) | (chunk == 0))
+        def _():
+            for side, (a_ref, m_ref) in enumerate(((g_ref, s_ref), (h_ref, r_ref))):
+                for k in range(blocks):
+                    at = (side * blocks + k) * span
+                    taken[:, at : at + span] = inner_rows(
+                        a_ref[k * span : (k + 1) * span, :], m_ref[tap, k]
+                    ).astype(BF16)
+
+        at = pl.ds(pl.multiple_of(chunk * lanes, lanes), lanes)
+        to = pl.ds(pl.multiple_of(unit * lanes, lanes), lanes)
+        out_ref[0, :, to] = (
+            product(taken[:, :rows], u_ref[:, at]) + product(taken[:, rows:], v_ref[:, at])
+        ).astype(BF16)
+
+
+def heads_split(x, g, h, u, v, s, r, shards, lanes):
+    rows, outs = g.shape
+    wide = u.shape[1]
+    taps, blocks, span, _ = s.shape
+    units = taps * wide // (2 * shards * lanes)
+    per_tap = wide // lanes
+    whole = pl.BlockSpec(memory_space=pltpu.VMEM)
+    return pl.pallas_call(
+        functools.partial(heads_split_kernel, per_tap, units, lanes),
+        grid_spec=pltpu.PrefetchScalarGridSpec(
+            num_scalar_prefetch=1,
+            grid=(shards,),
+            in_specs=[whole] * 6,
+            out_specs=pl.BlockSpec((1, outs, units * lanes), lambda i, f: (i, 0, 0)),
+            scratch_shapes=[pltpu.VMEM((outs, 2 * rows), BF16)],
+        ),
+        out_shape=jax.ShapeDtypeStruct((shards, outs, units * lanes), BF16),
+        compiler_params=params(),
+        cost_estimate=cost(2 * rows * wide * outs * taps, outs * taps * wide * 2),
+        name="heads_split",
+    )(x, g, h, u, v, s, r)
+
+
+def rows_split_kernel(first_ref, g_ref, h_ref, u_ref, v_ref, s_ref, r_ref, out_ref):
+    blocks, span = s_ref.shape[1], s_ref.shape[2]
+    total = 0.0
+    for a_ref, b_ref, m_ref in ((g_ref, u_ref, s_ref), (h_ref, v_ref, r_ref)):
+        taken = jnp.concatenate(
+            [
+                inner_rows(a_ref[k * span : (k + 1) * span, :], m_ref[0, k]).astype(BF16)
+                for k in range(blocks)
+            ],
+            1,
+        )
+        total = total + product(taken, b_ref[...])
+    out_ref[...] = total.astype(BF16)
+
+
+def rows_split(first, g, h, u, v, s, r, halves, steps):
+    rows, outs = g.shape
+    depth = u.shape[1] // halves
+    taps, blocks, span, _ = s.shape
+    side = pl.BlockSpec((rows, outs), lambda b, f: (0, 0))
+    values = pl.BlockSpec((rows, depth), lambda b, f: (0, (b + f[0]) % halves))
+    picks = pl.BlockSpec((1, blocks, span, span), lambda b, f: ((b + f[0]) // halves, 0, 0, 0))
+    return pl.pallas_call(
+        rows_split_kernel,
+        grid_spec=pltpu.PrefetchScalarGridSpec(
+            num_scalar_prefetch=1,
+            grid=(steps,),
+            in_specs=[side, side, values, values, picks, picks],
+            out_specs=pl.BlockSpec((outs, depth), lambda b, f: (0, b)),
+        ),
+        out_shape=jax.ShapeDtypeStruct((outs, steps * depth), BF16),
+        compiler_params=params(),
+        cost_estimate=cost(4 * rows * outs * steps * depth, outs * steps * depth * 2),
+        name="rows_split",
+    )(first, g, h, u, v, s, r)
+
+
+def rows_data_kernel(halves, first_ref, g_ref, w_ref, s_ref, du_ref, total):
+    step = pl.program_id(0)
+    depth = w_ref.shape[0]
+    which = (step + first_ref[0]) % halves
+
+    @pl.when(step == 0)
+    def _():
+        total[...] = jnp.zeros_like(total)
+
+    total[which] += against(shifted(g_ref, s_ref), w_ref[...])
+
+    @pl.when(step == pl.num_programs(0) - 1)
+    def _():
+        for k in range(halves):
+            du_ref[:, k * depth : (k + 1) * depth] = total[k].astype(du_ref.dtype)
+
+
+def rows_data(first, g, w, shifts, halves, depth):
+    rows, outs = g.shape
+    steps = w.shape[0] // depth
+    taps, blocks, span, _ = shifts.shape
+    return pl.pallas_call(
+        functools.partial(rows_data_kernel, halves),
+        grid_spec=pltpu.PrefetchScalarGridSpec(
+            num_scalar_prefetch=1,
+            grid=(steps,),
+            in_specs=[
+                pl.BlockSpec((rows, outs), lambda b, f: (0, 0)),
+                pl.BlockSpec((depth, outs), lambda b, f: (b, 0)),
+                pl.BlockSpec((1, blocks, span, span), lambda b, f: ((b + f[0]) // halves, 0, 0, 0)),
+            ],
+            out_specs=pl.BlockSpec((rows, halves * depth), lambda b, f: (0, 0)),
+            scratch_shapes=[pltpu.VMEM((halves, rows, depth), F32)],
+        ),
+        out_shape=jax.ShapeDtypeStruct((rows, halves * depth), BF16),
+        compiler_params=params(),
+        cost_estimate=cost(2 * rows * w.size, w.size * 2),
+        name="rows_data",
+    )(first, g, w, shifts)
+
+
+CHUNKS = 4
+
+
+def small_kernel(p_ref, out_ref, half_ref, core_in, core_out, y_in, x_out, x_in, z_out, z_in, send, recv):
+    rep, dp = lax.axis_index("rep"), lax.axis_index("dp")
+    par, upper = lax.rem(rep, 2), rep // 2
+    x, z = lax.rem(dp, 2), dp // 2
+    mate, far, beside = rep + 1 - 2 * par, rep + 2 - 4 * upper, dp + 1 - 2 * x
+    zs = [lax.rem(z + k, 4) for k in range(1, 4)]
+    barrier = pltpu.get_barrier_semaphore()
+    partners = [{"rep": mate}, {"rep": far}, {"dp": beside}] + [{"dp": 2 * k + x} for k in zs]
+    for partner in partners:
+        pl.semaphore_signal(barrier, inc=1, device_id=partner, device_id_type=MESH)
+    pl.semaphore_wait(barrier, len(partners))
+    rows = p_ref.shape[1] // CHUNKS
+    half, eighth = rows // 2, rows // 8
+
+    def span(c, at=0, size=rows):
+        return pl.ds(pl.multiple_of(c * rows + at, 16), size)
+
+    def remote(src, dst, c, slot, to, slot_in=None):
+        return pltpu.make_async_remote_copy(
+            src_ref=src,
+            dst_ref=dst,
+            send_sem=send.at[c, slot],
+            recv_sem=recv.at[c, slot if slot_in is None else slot_in],
+            device_id=to,
+            device_id_type=MESH,
+        )
+
+    def core_copy(c, hi):
+        return remote(
+            p_ref.at[2 * hi + 1 - par, span(c)], core_in.at[hi, span(c)], c, hi, {"rep": mate}
+        )
+
+    def y_copy(c):
+        return remote(core_out.at[span(c)], y_in.at[span(c)], c, 2, {"rep": far})
+
+    def x_copy(c):
+        return remote(
+            x_out.at[pl.ds(c * half, half)], x_in.at[pl.ds(c * half, half)], c, 3, {"dp": beside}
+        )
+
+    def z_copy(c, k, incoming):
+        sent = pl.ds(pl.multiple_of(c * half + k * eighth, 16), eighth)
+        slot = k if incoming else z
+        return remote(
+            z_out.at[sent], z_in.at[slot, pl.ds(c * eighth, eighth)], c, 4 + k, {"dp": 2 * k + x}, 4 + slot
+        )
+
+    def back_copy(c, k, incoming):
+        place = span(c, x * half + (k if incoming else z) * eighth, eighth)
+        return remote(
+            half_ref.at[place], half_ref.at[place], c, 8 + k, {"dp": 2 * k + x}, 8 + (k if incoming else z)
+        )
+
+    def last_copy(c, incoming):
+        place = span(c, (1 - x if incoming else x) * half, half)
+        return remote(half_ref.at[place], half_ref.at[place], c, 12, {"dp": beside})
+
+    def step(stage, c):
+        if stage == 0:
+            for hi in range(2):
+                core_copy(c, hi).start()
+        elif stage == 1:
+            for hi in range(2):
+                core_copy(c, hi).wait_recv()
+            core_out[span(c)] = (
+                p_ref[2 * (1 - upper) + par, span(c)].astype(F32)
+                + core_in[1 - upper, span(c)].astype(F32)
+            ).astype(BF16)
+            y_copy(c).start()
+        elif stage == 2:
+            y_copy(c).wait_recv()
+
+            def both(at):
+                place = span(c, at, half)
+                return (
+                    p_ref[rep, place].astype(F32)
+                    + core_in[upper, place].astype(F32)
+                    + y_in[place].astype(F32)
+                )
+
+            x_out[pl.ds(c * half, half)] = both((1 - x) * half).astype(BF16)
+            x_copy(c).start()
+            z_out[pl.ds(c * half, half)] = both(x * half).astype(BF16)
+        elif stage == 3:
+            x_copy(c).wait_recv()
+            at = pl.ds(c * half, half)
+            z_out[at] = (z_out[at].astype(F32) + x_in[at].astype(F32)).astype(BF16)
+            for k in zs:
+                z_copy(c, k, False).start()
+        elif stage == 4:
+            for k in zs:
+                z_copy(c, k, True).wait_recv()
+            z_in[z, pl.ds(c * eighth, eighth)] = z_out[
+                pl.ds(pl.multiple_of(c * half + z * eighth, 16), eighth)
+            ]
+            total = z_in[0, pl.ds(c * eighth, eighth)].astype(F32)
+            for k in range(1, 4):
+                total = total + z_in[k, pl.ds(c * eighth, eighth)].astype(F32)
+            half_ref[span(c, x * half + z * eighth, eighth)] = total.astype(BF16)
+            for k in zs:
+                back_copy(c, k, False).start()
+        elif stage == 5:
+            for k in zs:
+                back_copy(c, k, True).wait_recv()
+            last_copy(c, False).start()
+        else:
+            last_copy(c, True).wait_recv()
+            out_ref[span(c)] = half_ref[span(c)].astype(F32)
+            for hi in range(2):
+                core_copy(c, hi).wait_send()
+            y_copy(c).wait_send()
+            x_copy(c).wait_send()
+            for k in zs:
+                z_copy(c, k, False).wait_send()
+                back_copy(c, k, False).wait_send()
+            last_copy(c, False).wait_send()
+
+    for turn in range(CHUNKS + 6):
+        for c in range(CHUNKS):
+            if 0 <= turn - c <= 6:
+                step(turn - c, c)
+
+
+def small_total(parts):
+    quarters, rows, lanes = parts.shape
+    return pl.pallas_call(
+        small_kernel,
+        out_shape=jax.ShapeDtypeStruct((rows, lanes), F32),
+        in_specs=[pl.BlockSpec(memory_space=pltpu.VMEM)],
+        out_specs=pl.BlockSpec(memory_space=pltpu.VMEM),
+        scratch_shapes=[
+            pltpu.VMEM((rows, lanes), BF16),
+            pltpu.VMEM((2, rows, lanes), BF16),
+            pltpu.VMEM((rows, lanes), BF16),
+            pltpu.VMEM((rows, lanes), BF16),
+            pltpu.VMEM((rows // 2, lanes), BF16),
+            pltpu.VMEM((rows // 2, lanes), BF16),
+            pltpu.VMEM((rows // 2, lanes), BF16),
+            pltpu.VMEM((4, rows // 8, lanes), BF16),
+            pltpu.SemaphoreType.DMA((CHUNKS, 13)),
+            pltpu.SemaphoreType.DMA((CHUNKS, 13)),
+        ],
+        compiler_params=pltpu.CompilerParams(
+            collective_id=9, has_side_effects=True, vmem_limit_bytes=VMEM_LIMIT
+        ),
+        name="small_total",
+    )(parts)
 
 
 def silu_slope(value_in):
@@ -392,6 +670,21 @@
 
 def scatter_rep(value):
     return lax.psum_scatter(value.astype(BF16), "rep", scatter_dimension=0, tiled=True)
+
+
+def swap_x(value):
+    return lax.ppermute(value, "dp", [(k, k ^ 1) for k in range(lax.axis_size("dp"))])
+
+
+def own_half(value, parity):
+    halves = value.reshape((2, value.shape[0] // 2) + value.shape[1:])
+    return lax.dynamic_index_in_dim(halves, parity, 0, keepdims=False)
+
+
+def both_halves(mine, other, parity):
+    return jnp.concatenate(
+        [jnp.where(parity == 0, mine, other), jnp.where(parity == 0, other, mine)], 0
+    )
 
 
 def total_dp(value):
@@ -441,6 +734,15 @@
     ).astype(F32)
     shifts_own = shift_matrices(own_info, 2)
     shifts_all = shift_matrices(group_info, 1)
+    split = lax.axis_size("dp") == 8
+    if split:
+        side = lax.axis_index("dp") % 2
+        side_of = jnp.reshape(side, (1,)).astype(jnp.int32)
+        beside_row = first_row + group * (1 - 2 * side)
+        shifts_beside = shift_matrices(
+            geometry(lax.dynamic_slice_in_dim(layout, beside_row, group, 0), pixels), 1
+        )
+        columns = [[z_at * 2 + k for z_at in range(4)] for k in range(2)]
     zero = jnp.zeros((1,), jnp.int32)
     first = jnp.reshape(9 * parity, (1,)).astype(jnp.int32)
 
@@ -464,6 +766,9 @@
     pre_act = normed_three + inputs.astype(F32)
     trunk = jax.nn.silu(pre_act).astype(BF16)
     trunk_all = lax.all_gather(trunk, "rep", axis=0, tiled=True)
+
+    if split:
+        trunk_mine = swap_x(own_half(trunk_all, parity))
 
     headed = heads_forward(trunk_all, w_heads, shifts_all)
     own_gain = lax.dynamic_slice_in_dim(gain_head, rep * middle, middle, 0)
@@ -481,9 +786,15 @@
         jnp.concatenate([heads_all[1], heads_all[2], heads_all[3]], 1),
         jnp.concatenate([heads_all[0], heads_all[1], heads_all[2]], 1),
     )
+    if split:
+        source_mine = swap_x(own_half(source, parity))
     partial = rows_forward(first, source, w_messages, shifts_all, 2).reshape(
         2, 2, pixels, middle
     )
+
+    if split:
+        partial, trunk_mine = lax.optimization_barrier((partial, trunk_mine))
+        trunk_other = swap(trunk_mine, 1)
 
     def of_parity(value, which):
         return lax.dynamic_index_in_dim(value, which, 1, keepdims=False)
@@ -524,9 +835,11 @@
     grad_message = (grad_stream * gate).astype(BF16)
     gates_local = inner_rows(stream, grad_gate).astype(BF16)
     gates_local = gates_local.reshape(2, pixels, middle)
-    gates_share = lax.dynamic_index_in_dim(gates_local, parity, 0, keepdims=False).astype(
-        F32
-    ) + swap(lax.dynamic_index_in_dim(gates_local, 1 - parity, 0, keepdims=False), 1).astype(F32)
+    if not split:
+        gates_share = lax.dynamic_index_in_dim(gates_local, parity, 0, keepdims=False).astype(F32)
+        gates_share += swap(
+            lax.dynamic_index_in_dim(gates_local, 1 - parity, 0, keepdims=False), 1
+        ).astype(F32)
     direct = (grad_stream + against(grad_gate, own_gates)).astype(BF16)
 
     def both_parities(value, other):
@@ -538,9 +851,24 @@
 
     message_all = both_parities(grad_message, swap(grad_message, 1))
     direct_all = both_parities(direct, jnp.zeros_like(direct))
-    source_grad, messages_local = rows_back(
-        first, message_all, source, w_messages, shifts_all, 2, BF16
-    )
+    if split:
+        message_cut = message_all.reshape(4 * pixels, 4, 2, middle // 8)
+        cut_own = lax.dynamic_index_in_dim(message_cut, side, 2, keepdims=False)
+        cut_sent = lax.dynamic_index_in_dim(message_cut, 1 - side, 2, keepdims=False)
+        cut_own = cut_own.reshape(4 * pixels, middle // 2)
+        cut_beside = swap_x(cut_sent.reshape(4 * pixels, middle // 2))
+        source_grad = rows_data(
+            first, message_all, w_messages, shifts_all, 2, source.shape[1] // 2
+        )
+        source_grad, source_mine, cut_beside, trunk_other = lax.optimization_barrier(
+            (source_grad, source_mine, cut_beside, trunk_other)
+        )
+        source_beside = both_halves(source_mine, swap(source_mine, 1), parity)
+        trunk_beside = both_halves(trunk_mine, trunk_other, parity)
+    else:
+        source_grad, messages_local = rows_back(
+            first, message_all, source, w_messages, shifts_all, 2, BF16
+        )
     thirds = [source_grad[:, k * middle : (k + 1) * middle] for k in range(3)]
     by_head = jnp.stack(
         [
@@ -551,10 +879,21 @@
         ],
         0,
     )
-    feat_grad = lax.psum_scatter(by_head, "rep", scatter_dimension=0, tiled=False).astype(F32)
-    grad_messages = lax.psum_scatter(messages_local, "dp", scatter_dimension=1, tiled=True)
+    feat_grad = lax.psum_scatter(by_head, "rep", scatter_dimension=0, tiled=False)
+    if split:
+        messages_local = rows_split(
+            first, cut_own, cut_beside, source, source_beside, shifts_all, shifts_beside, 2, 9
+        )
+        feat_grad, messages_local, trunk_beside = lax.optimization_barrier(
+            (feat_grad, messages_local, trunk_beside)
+        )
+        grad_messages = lax.psum_scatter(
+            messages_local, "dp", scatter_dimension=0, tiled=True, axis_index_groups=columns
+        )
+    else:
+        grad_messages = lax.psum_scatter(messages_local, "dp", scatter_dimension=1, tiled=True)
     head_raw, gain_grad_head, shift_grad_head = norm_back(
-        feat_grad * silu_slope(normed_head),
+        feat_grad.astype(F32) * silu_slope(normed_head),
         unit_head,
         scale_head,
         own_gain,
@@ -563,18 +902,38 @@
         ("dp",),
     )
     head_low = head_raw.astype(BF16)
-    heads_local = heads_weight(head_low, trunk_all, shifts_all)
-    head_low, heads_local = lax.optimization_barrier((head_low, heads_local))
-    grad_heads = lax.psum_scatter(heads_local, "dp", scatter_dimension=1, tiled=True)
-    trunk_grad = lax.psum_scatter(
-        heads_data(head_low, w_heads, shifts_all), "rep", scatter_dimension=0, tiled=True
-    ).astype(F32)
+    if split:
+        head_beside = swap_x(head_low)
+        trunk_part = heads_data(head_low, w_heads, shifts_all)
+        trunk_part, head_beside = lax.optimization_barrier((trunk_part, head_beside))
+        heads_local = heads_split(
+            side_of,
+            head_low,
+            head_beside,
+            trunk_all,
+            trunk_beside,
+            shifts_all,
+            shifts_beside,
+            4,
+            256,
+        )
+    else:
+        heads_local = heads_weight(head_low, trunk_all, shifts_all)
+        grad_heads = lax.psum_scatter(heads_local, "dp", scatter_dimension=1, tiled=True)
+        trunk_part = heads_data(head_low, w_heads, shifts_all)
+    trunk_grad = lax.psum_scatter(trunk_part, "rep", scatter_dimension=0, tiled=True)
+    if split:
+        trunk_grad, heads_local = lax.optimization_barrier((trunk_grad, heads_local))
+        grad_heads = lax.psum_scatter(
+            heads_local, "dp", scatter_dimension=0, tiled=False, axis_index_groups=columns
+        )
+    trunk_grad = trunk_grad.astype(F32)
     pre_grad = trunk_grad * silu_slope(pre_act)
     expand_raw, grad_gain_wide, grad_shift_wide = norm_back(
         pre_grad, unit_three, scale_three, gain_wide, living, pixel_count, everyone
     )
     expand_low = expand_raw.astype(BF16)
-    grad_expand = scatter_rep(inner_rows(hidden_two, expand_low))
+    expand_local = inner_rows(hidden_two, expand_low).astype(BF16)
     hidden_two_grad = against(expand_low, w_expand)
     spatial_raw, gain_grad_two, shift_grad_two = norm_back(
         hidden_two_grad * silu_slope(normed_two),
@@ -589,7 +948,6 @@
     hidden_one_grad, spatial_local = rows_back(
         zero, spatial_low, hidden_one, w_spatial, shifts_own, 1, F32
     )
-    grad_spatial = scatter_rep(spatial_local)
     reduced_raw, gain_grad_one, shift_grad_one = norm_back(
         hidden_one_grad * silu_slope(normed_one),
         unit_one,
@@ -600,24 +958,72 @@
         everyone,
     )
     reduced_low = reduced_raw.astype(BF16)
-    grad_reduce = scatter_rep(inner_rows(inputs, reduced_low))
+    reduce_local = inner_rows(inputs, reduced_low).astype(BF16)
+    if split:
+        reduced_low, grad_messages = lax.optimization_barrier((reduced_low, grad_messages))
+        grad_messages = grad_messages.T
     input_grad = pre_grad + against(reduced_low, w_reduce)
-    grad_classes = scatter_rep(classes_local)
-    pieces = [
-        gates_share.astype(BF16),
-        grad_expand.reshape(-1, middle),
-        grad_spatial,
-        grad_classes.reshape(-1, middle),
-    ]
-    early = total_dp(jnp.concatenate(pieces, 0))
-    rows = [piece.shape[0] for piece in pieces]
-    starts = [sum(rows[:k]) for k in range(4)]
-    grad_gates, expand_sum, grad_spatial, classes_sum = [
-        early[at : at + size] for at, size in zip(starts, rows)
-    ]
-    grad_expand = expand_sum.reshape(grad_expand.shape)
-    grad_classes = classes_sum.reshape(grad_classes.shape)
-    grad_reduce = total_dp(grad_reduce)
+    if split:
+        wide = w_expand.shape[1]
+        cuts = wide // middle
+
+        def side_by_side(value):
+            value = value.reshape(4, -1, value.shape[1])
+            return jnp.concatenate(
+                [value[:, :, k : k + middle] for k in range(0, value.shape[2], middle)], 1
+            )
+
+        gates_zero = jnp.zeros_like(gates_local)
+        gates_every = jnp.where(
+            is_depth,
+            jnp.concatenate([gates_local, gates_zero], 0),
+            jnp.concatenate([gates_zero, gates_local], 0),
+        )
+        classes_wide = jnp.pad(classes_local.astype(BF16), ((0, 0), (0, 128 - classes)))
+        classes_wide = classes_wide.reshape(4, 4, -1, 128)
+        classes_wide = jnp.concatenate([classes_wide[:, k] for k in range(4)], 2)
+        pieces = [
+            reduce_local.reshape(4, -1, middle),
+            spatial_local.reshape(4, -1, middle),
+            side_by_side(expand_local),
+            gates_every,
+            classes_wide,
+        ]
+        rows = [piece.shape[1] for piece in pieces]
+        unit = 128 * CHUNKS
+        missing = -sum(rows) % unit
+        pieces.append(jnp.zeros((4, missing, middle), BF16))
+        summed = small_total(jnp.concatenate(pieces, 1))
+        starts = [sum(rows[:k]) for k in range(5)]
+        grad_reduce, grad_spatial, expand_sum, grad_gates, classes_sum = [
+            summed[at : at + size] for at, size in zip(starts, rows)
+        ]
+        expand_sum = expand_sum.reshape(cuts, -1, middle)
+        grad_expand = jnp.concatenate([expand_sum[k] for k in range(cuts)], 1)
+        classes_sum = jnp.concatenate(
+            [classes_sum[:, k * 128 : (k + 1) * 128] for k in range(4)], 0
+        )
+        grad_classes = classes_sum[:, :classes]
+    else:
+        grad_expand = scatter_rep(expand_local)
+        grad_spatial = scatter_rep(spatial_local)
+        grad_reduce = scatter_rep(reduce_local)
+        grad_classes = scatter_rep(classes_local)
+        pieces = [
+            gates_share.astype(BF16),
+            grad_expand.reshape(-1, middle),
+            grad_spatial,
+            grad_classes.reshape(-1, middle),
+        ]
+        early = total_dp(jnp.concatenate(pieces, 0))
+        rows = [piece.shape[0] for piece in pieces]
+        starts = [sum(rows[:k]) for k in range(4)]
+        grad_gates, expand_sum, grad_spatial, classes_sum = [
+            early[at : at + size] for at, size in zip(starts, rows)
+        ]
+        grad_expand = expand_sum.reshape(grad_expand.shape)
+        grad_classes = classes_sum.reshape(grad_classes.shape)
+        grad_reduce = total_dp(grad_reduce)
     grad_gain_mid = jnp.stack([gain_grad_one, gain_grad_two], 0)
     grad_shift_mid = jnp.stack([shift_grad_one, shift_grad_two], 0)
     head_norms = lax.all_gather(

time: 1240 us -> 761 us (0.61)
  waiting for transfers between devices: 776 us -> 77.9 us
  Pallas kernels: 238 us -> 445 us
  blocking collectives: 35.4 us -> 12.3 us
  other arithmetic: 88.8 us -> 107 us
  local copies, waits for them, and re-layouts: 37.7 us -> 53.4 us
    reduce_scatter x8 -> x3, waiting for transfers between devices: 521 us -> 0.02 us  [the longest x1 0.01 us: shards(): lax.psum_scatter(trunk_part, 'rep', scatter_dimension=0, tiled=True)]
    pallas_call x1 -> x4, Pallas kernels: 28 us -> 258 us  [the longest x1 177 us: small_total(): pl.pallas_call(small_kernel, out_shape=jax.ShapeDtypeStruct((rows, lanes)...]
    unnamed x14 -> x6, waiting for transfers between devices: 121 us -> 0.65 us
    reduce_scatter x1, waiting for transfers between devices: 44.5 us -> 4.95 us  [shards(): lax.psum_scatter(by_head, 'rep', scatter_dimension=0, tiled=False)]
    all_gather x1 -> x0, blocking collectives: 30.2 us -> none  [total_dp(): return lax.all_gather(share, 'dp', axis=0, tiled=True)[:rows].astype(F32)]
    pallas_call x2 -> x1, Pallas kernels: 37.1 us -> 11.3 us  [rows_back(): pl.pallas_call(functools.partial(rows_back_kernel, halves), grid_spec=plt...]
    all_gather x1 -> x0, waiting for transfers between devices: 19.2 us -> none  [total_dp(): return lax.all_gather(share, 'dp', axis=0, tiled=True)[:rows].astype(F32)]
    ppermute x0 -> x4, waiting for transfers between devices: none -> 12.9 us  [swap_x(): lax.ppermute(value, 'dp', [(k, k ^ 1) for k in range(lax.axis_size('dp'))])]
  transfers between devices with their start and end apart: 20 -> 18, of which waited for: 15 -> 7; matrix products, arithmetic and copies ran while one was open for 7% -> 16% of each run, Pallas kernels for 4% -> 47%
where the time goes in v2:
time: 761 us; the launch traced here: 750 us
  Pallas kernels  445 us (58%)
  other arithmetic  107 us (14%)
  waiting for transfers between devices  77.9 us (10%)
  local copies, waits for them, and re-layouts  53.4 us (7%)
  between operations  23.6 us (3%)
  matrix products  19.8 us (3%)
  blocking collectives  12.3 us (2%)
  starting transfers between devices  10.7 us (1%)
    pallas_call x1, Pallas kernels, small_total(): pl.pallas_call(small_kernel, out_shape=jax.ShapeDtypeStruct((rows, lanes)...  177 us
    pallas_call x8, Pallas kernels, total_of(): pl.pallas_call(functools.partial(total_kernel, sized), out_shape=jax.Shap...  88 us
    pallas_call x1, Pallas kernels, heads_split(): pl.pallas_call(functools.partial(heads_split_kernel, per_tap, units, lane...  42.8 us
    pallas_call x1, Pallas kernels, heads_forward(): pl.pallas_call(heads_forward_kernel, grid=(taps,), in_specs=[pl.BlockSpec...  32.1 us
    pallas_call x1, Pallas kernels, heads_data(): pl.pallas_call(heads_data_kernel, grid=(taps,), in_specs=[pl.BlockSpec((r...  30.4 us
    all_gather x1, waiting for transfers between devices, shards(): heads_all = lax.all_gather(rounded, 'rep', axis=0, tiled=False)  29.5 us
    all_gather x1, waiting for transfers between devices, shards(): trunk_all = lax.all_gather(trunk, 'rep', axis=0, tiled=True)  26.5 us
    pallas_call x2, Pallas kernels, rows_forward(): pl.pallas_call(rows_forward_kernel, grid_spec=pltpu.PrefetchScalarGridSpe...  25.5 us
  transfers between devices with their start and end apart: 18, of which 7 were waited for; matrix products, arithmetic and copies ran while one was open for 16% of the time, Pallas kernels for 47%

profile of v2, /device:TPU:28, one launch (start us, length us, event | category | flops | bytes accessed | tf_op | source)
XLA Modules:
  0.0 750.3 jit_solution(901482822386252370)
XLA Ops:
  15.9 2.6 multiply_reduce_fusion.7
  19.2 10.1 %total.8 = f32[8,128]{1,0:T(8,128)} custom-call(f32[8,128]{1,0:T(8,128)} %pad_maximum_fusion.11.x_ref), custom_call_target="tpu_custom_call" | custom-call | tf_op jit(solution)/shard_map/total/pallas_call | solution.py:629
  40.0 8.9 %rows_forward.2 = f32[256,512]{1,0:T(8,128)} custom-call(s32[1]{0:T(128)} %constant.95.clone.1.first_ref, bf16[256,512]{1,0:T(8,128)(2,1)} %multiply_convert_fusion.8.u_ref, bf16[4608,512]{1,0:T(8,128)(2,1)} %w_ref.11, bf16[9,1,256,256]{3,2,1,0:T(8,128)(2,1)} %convert_element_type.130.s_ref), custom_call_target="tpu_custom_call" | custom-call | flops 1207959552 | bytes 4718592 | tf_op jit(solution)/shard_map/rows_forward/pallas_call | solution.py:209
  50.7 11.1 %total.9 = f32[8,128]{1,0:T(8,128)} custom-call(f32[8,128]{1,0:T(8,128)} %pad_maximum_fusion.12.x_ref), custom_call_target="tpu_custom_call" | custom-call | tf_op jit(solution)/shard_map/total/pallas_call | solution.py:629
  64.0 3.2 multiply_reduce_fusion.1
  67.9 11.5 %total.10 = f32[32,128]{1,0:T(8,128)} custom-call(f32[32,128]{1,0:T(8,128)} %pad_maximum_fusion.9.x_ref), custom_call_target="tpu_custom_call" | custom-call | tf_op jit(solution)/shard_map/total/pallas_call | solution.py:629
  81.4 3.4 multiply_convert_fusion.3
  89.2 3.3 convert_element_type.134.s_ref
  93.2 26.5 %all-gather.4.cloned.1.call-done.u_ref = bf16[1024,2048]{1,0:T(8,128)(2,1)} async-done(((bf16[256,2048]{1,0:T(8,128)(2,1)}), bf16[1024,2048]{1,0:T(8,128)(2,1)}) %all-gather.4.cloned.1.call-update) | async-done | bytes 4194320 | tf_op jit(solution)/shard_map/all_gather | solution.py:768
  119.7 32.1 %heads_forward.1 = f32[1024,512]{1,0:T(8,128)} custom-call(bf16[1024,2048]{1,0:T(8,128)(2,1)} %all-gather.4.cloned.1.call-done.u_ref, bf16[512,18432]{1,0:T(8,128)(2,1)} %w_ref.10, bf16[9,4,256,256]{3,2,1,0:T(8,128)(2,1)} %convert_element_type.134.s_ref), custom_call_target="tpu_custom_call" | custom-call | flops 19327352832 | bytes 23068672 | tf_op jit(solution)/shard_map/heads_forward/pallas_call | solution.py:97
  151.8 1.9 multiply_reduce_fusion
  154.4 7.9 %total.11 = f32[8,128]{1,0:T(8,128)} custom-call(f32[8,128]{1,0:T(8,128)} %pad_maximum_fusion.13.x_ref), custom_call_target="tpu_custom_call" | custom-call | tf_op jit(solution)/shard_map/total/pallas_call | solution.py:629
  164.4 3.2 multiply_convert_fusion.2
  168.2 3.1 dynamic-slice_bitcast_fusion
  172.8 29.5 %all-gather.6.cloned.1.call-done = bf16[4096,512]{1,0:T(8,128)(2,1)} async-done(((bf16[1024,512]{1,0:T(8,128)(2,1)}), bf16[4096,512]{1,0:T(8,128)(2,1)}) %all-gather.6.cloned.1.call-update) | async-done | bytes 4194320 | tf_op jit(solution)/shard_map/all_gather | solution.py:781
  202.4 3.5 fusion.124
  205.8 2.4 maximum_select_fusion.u_ref
  208.5 16.6 %rows_forward.3 = f32[1024,512]{1,0:T(8,128)} custom-call(s32[1]{0:T(128)} %bitcast.68.first_ref, bf16[1024,1536]{1,0:T(8,128)(2,1)} %maximum_select_fusion.u_ref, bf16[6912,512]{1,0:T(8,128)(2,1)} %w_ref.9, bf16[9,4,256,256]{3,2,1,0:T(8,128)(2,1)} %convert_element_type.134.s_ref), custom_call_target="tpu_custom_call" | custom-call | flops 7247757312 | bytes 7077888 | tf_op jit(solution)/shard_map/rows_forward/pallas_call | solution.py:209
  225.1 2.3 dynamic-slice_bitcast_fusion.1
  232.3 1.9 bitcast_add_fusion
  235.4 2.1 collective-permute-done.4
  244.1 2.0 copy.42
  246.1 2.0 copy.41
  248.1 3.4 pad_maximum_fusion.4
  253.1 2.5 copy.43
  255.6 2.1 constant_dynamic-slice_fusion.1
  257.7 2.1 copy.44
  260.3 15.9 %rows_data.1 = bf16[1024,1536]{1,0:T(8,128)(2,1)} custom-call(s32[1]{0:T(128)} %bitcast.68.first_ref, bf16[1024,512]{1,0:T(8,128)(2,1)} %bitcast.333, bf16[6912,512]{1,0:T(8,128)(2,1)} %w_ref.9, bf16[9,4,256,256]{3,2,1,0:T(8,128)(2,1)} %convert_element_type.134.s_ref), custom_call_target="tpu_custom_call" | custom-call | flops 7247757312 | bytes 7077888 | tf_op jit(solution)/shard_map/rows_data/pallas_call | solution.py:385
  276.3 2.2 collective-permute-done.7
  278.5 10.7 %collective-permute-done.8.h_ref = bf16[1024,256]{1,0:T(8,128)(2,1)} collective-permute-done((bf16[1024,256]{1,0:T(8,128)(2,1)}, bf16[1024,256]{1,0:T(8,128)(2,1)}, u32[]{:S(2)}, u32[]{:S(2)}) %collective-permute-start.8) | collective-permute-done | bytes 524320 | tf_op jit(solution)/shard_map/ppermute | solution.py:676
  289.1 2.2 bitcast_select_fusion.1
  291.3 2.3 pad_maximum_fusion
  297.4 3.3 convert_element_type.147.r_ref
  301.6 3.4 broadcast_select_fusion.1
  305.0 2.6 pad_maximum_fusion.1.v_ref
  307.7 2.1 broadcast_select_fusion.3
  311.6 21.9 %rows_split.1 = bf16[256,6912]{1,0:T(8,128)(2,1)} custom-call(s32[1]{0:T(128)} %bitcast.68.first_ref, bf16[1024,256]{1,0:T(8,128)(2,1)} %copy.45.g_ref, bf16[1024,256]{1,0:T(8,128)(2,1)} %collective-permute-done.8.h_ref, bf16[1024,1536]{1,0:T(8,128)(2,1)} %maximum_select_fusion.u_ref, bf16[1024,1536]{1,0:T(8,128)(2,1)} %pad_maximum_fusion.2.v_ref, ...), custom_call_target="tpu_custom_call" | custom-call | flops 7247757312 | bytes 3538944 | tf_op jit(solution)/shard_map/rows_split/pallas_call | solution.py:349
  333.5 5.0 reduce-scatter.5.cloned.1.call-done
  338.4 3.2 multiply_reduce_fusion.3
  342.3 7.9 %total.12 = f32[8,128]{1,0:T(8,128)} custom-call(f32[8,128]{1,0:T(8,128)} %pad_maximum_fusion.14.x_ref), custom_call_target="tpu_custom_call" | custom-call | tf_op jit(solution)/shard_map/total/pallas_call | solution.py:629
  351.0 4.0 multiply_convert_fusion.1.g_ref
  356.5 30.4 %heads_data.1 = bf16[1024,2048]{1,0:T(8,128)(2,1)} custom-call(bf16[1024,512]{1,0:T(8,128)(2,1)} %multiply_convert_fusion.1.g_ref, bf16[512,18432]{1,0:T(8,128)(2,1)} %w_ref.10, bf16[9,4,256,256]{3,2,1,0:T(8,128)(2,1)} %convert_element_type.134.s_ref), custom_call_target="tpu_custom_call" | custom-call | flops 19327352832 | bytes 18874368 | tf_op jit(solution)/shard_map/heads_data/pallas_call | solution.py:146
  388.6 42.8 %heads_split.1 = bf16[4,512,2304]{2,1,0:T(8,128)(2,1)} custom-call(s32[1]{0:T(128)} %bitcast.111.x_ref, bf16[1024,512]{1,0:T(8,128)(2,1)} %multiply_convert_fusion.1.g_ref, bf16[1024,512]{1,0:T(8,128)(2,1)} %copy-done.82, bf16[1024,2048]{1,0:T(8,128)(2,1)} %all-gather.4.cloned.1.call-done.u_ref, bf16[1024,2048]{1,0:T(8,128)(2,1)} %pad_maximum_fusion.1.v_ref, ...), custom_call_target="tpu_custom_call" | custom-call | flops 19327352832 | bytes 18874368 | tf_op jit(solution)/shard_map/heads_split/pallas_call | solution.py:311
  434.2 2.6 convolution_convert_fusion.2
  439.5 12.3 %all_gather.15 = f32[2,2048]{1,0:T(2,128)S(1)} all-gather(f32[2,512]{1,0:T(2,128)S(1)} %pad_maximum_fusion.19), channel_id=1, replica_groups=mesh['dp'=8,'rep'=4] {'rep'}, dimensions={1}, use_global_device_ids=true | all-gather | bytes 20480 | tf_op jit(solution)/shard_map/all_gather | solution.py:1029
  452.5 4.0 multiply_reduce_fusion.2
  457.0 13.7 %total.13 = f32[32,128]{1,0:T(8,128)} custom-call(f32[32,128]{1,0:T(8,128)} %pad_maximum_fusion.10.x_ref), custom_call_target="tpu_custom_call" | custom-call | tf_op jit(solution)/shard_map/total/pallas_call | solution.py:629
  472.7 2.9 multiply_convert_fusion
  478.1 15.1 %total.14 = f32[8,128]{1,0:T(8,128)} custom-call(f32[8,128]{1,0:T(8,128)} %pad_maximum_fusion.15.x_ref), custom_call_target="tpu_custom_call" | custom-call | tf_op jit(solution)/shard_map/total/pallas_call | solution.py:629
  494.6 2.1 multiply_convert_fusion.6.g_ref
  496.7 11.3 %rows_back.1 = (f32[256,512]{1,0:T(8,128)}, bf16[4608,512]{1,0:T(8,128)(2,1)}) custom-call(s32[1]{0:T(128)} %constant.95.clone.1.first_ref, bf16[256,512]{1,0:T(8,128)(2,1)} %multiply_convert_fusion.6.g_ref, bf16[256,512]{1,0:T(8,128)(2,1)} %multiply_convert_fusion.8.u_ref, bf16[4608,512]{1,0:T(8,128)(2,1)} %w_ref.11, ...), custom_call_target="tpu_custom_call" | custom-call | flops 2415919104 | bytes 9437184 | tf_op jit(solution)/shard_map/rows_back/pallas_call | solution.py:252
  508.1 2.1 multiply_reduce_fusion.8
  510.8 10.6 %total.15 = f32[8,128]{1,0:T(8,128)} custom-call(f32[8,128]{1,0:T(8,128)} %pad_maximum_fusion.16.x_ref), custom_call_target="tpu_custom_call" | custom-call | tf_op jit(solution)/shard_map/total/pallas_call | solution.py:629
  522.8 2.4 multiply_convert_fusion.5
  525.2 2.1 fusion
  527.3 4.0 copy.46
  531.3 3.2 constant_dynamic-update-slice_fusion.1
  534.6 2.1 convolution_convert_fusion
  536.7 2.5 constant_dynamic-update-slice_fusion
  545.3 177.4 %small_total.1 = f32[2560,512]{1,0:T(8,128)} custom-call(bf16[4,2560,512]{2,1,0:T(8,128)(2,1)} %broadcast_dynamic-update-slice_fusion.p_ref), custom_call_target="tpu_custom_call" | custom-call | tf_op jit(solution)/shard_map/small_total/pallas_call | solution.py:533
  724.5 2.3 slice.288
  726.8 3.3 slice.289
  735.5 2.1 convolution_add_fusion
  738.9 4.2 bitcast_convert_fusion
  (324 shorter events, 83.4 us)
Async XLA Ops:
  7.2 56.8 %copy-start = (bf16[512,2048]{1,0:T(8,128)(2,1)S(1)}, bf16[512,2048]{1,0:T(8,128)(2,1)}, u32[]{:S(2)}) copy-start(bf16[512,2048]{1,0:T(8,128)(2,1)} %param.31) | copy-start | bytes 6291460
  7.2 112.5 %all-gather.4.cloned.1.call-start = ((), (), s32[]{:S(2)}) async-start(), calls=%async_computation.4 | async-start | bytes 5242880 | tf_op jit(solution)/shard_map/all_gather | solution.py:768
  15.2 17.6 %copy-start.44 = (f32[2,512]{1,0:T(2,128)S(1)}, f32[2,512]{1,0:T(2,128)}, u32[]{:S(2)}) copy-start(f32[2,512]{1,0:T(2,128)} %param.36) | copy-start | bytes 12292
  15.9 17.0 %copy-start.61 = (f32[2,512]{1,0:T(2,128)S(1)}, f32[2,512]{1,0:T(2,128)}, u32[]{:S(2)}) copy-start(f32[2,512]{1,0:T(2,128)} %param.37) | copy-start | bytes 12292
  18.5 30.3 %copy-start.14 = (f32[256,512]{1,0:T(8,128)}, f32[256,512]{1,0:T(8,128)S(1)}, u32[]{:S(2)}) copy-start(f32[256,512]{1,0:T(8,128)S(1)} %get-tuple-element.239) | copy-start | bytes 1572868
  30.1 18.8 %copy-start.35 = (f32[512]{0:T(512)}, f32[512]{0:T(512)S(1)}, u32[]{:S(2)}) copy-start(f32[512]{0:T(512)S(1)} %fusion.109) | copy-start | bytes 6148
  32.9 16.0 %copy-start.40 = (f32[1,512]{1,0:T(1,128)}, f32[1,512]{1,0:T(1,128)S(1)}, u32[]{:S(2)}) copy-start(f32[1,512]{1,0:T(1,128)S(1)} %slice.245) | copy-start | bytes 6148
  32.9 16.0 %copy-start.42 = (f32[1,512]{1,0:T(1,128)}, f32[1,512]{1,0:T(1,128)S(1)}, u32[]{:S(2)}) copy-start(f32[1,512]{1,0:T(1,128)S(1)} %get-tuple-element.193) | copy-start | bytes 6148
  32.9 31.1 %copy-start.78 = (f32[1,512]{1,0:T(1,128)}, f32[1,512]{1,0:T(1,128)S(1)}, u32[]{:S(2)}) copy-start(f32[1,512]{1,0:T(1,128)S(1)} %get-tuple-element.192) | copy-start | bytes 6148
  62.6 4.7 copy-start.53
  63.4 3.9 copy-start.49
  64.0 3.3 copy-start.75
  64.0 15.4 %copy-start.30 = (f32[2048]{0:T(1024)S(1)}, f32[2048]{0:T(1024)}, u32[]{:S(2)}) copy-start(f32[2048]{0:T(1024)} %param.38) | copy-start | bytes 24580
  64.0 17.4 %copy-start.5 = (bf16[256,2048]{1,0:T(8,128)(2,1)S(1)}, bf16[256,2048]{1,0:T(8,128)(2,1)}, u32[]{:S(2)}) copy-start(bf16[256,2048]{1,0:T(8,128)(2,1)} %param.25) | copy-start | bytes 3145732
  64.0 17.4 %copy-start.31 = (f32[2048]{0:T(1024)S(1)}, f32[2048]{0:T(1024)}, u32[]{:S(2)}) copy-start(f32[2048]{0:T(1024)} %param.39) | copy-start | bytes 24580
  81.4 3.5 copy-start.37
  84.8 117.5 %all-gather.6.cloned.1.call-start = ((), (), s32[]{:S(2)}) async-start(), calls=%async_computation.9 | async-start | bytes 5242880 | tf_op jit(solution)/shard_map/all_gather | solution.py:781
  167.7 170.7 %reduce-scatter.5.cloned.1.call-start = ((), (), s32[]{:S(2)}) async-start(), calls=%async_computation.5 | async-start | bytes 5242880 | tf_op jit(solution)/shard_map/reduce_scatter | solution.py:882
  171.3 53.8 %collective-permute-start = (bf16[512,2048]{1,0:T(8,128)(2,1)}, bf16[512,2048]{1,0:T(8,128)(2,1)}, u32[]{:S(2)}, u32[]{:S(2)}) collective-permute-start(bf16[512,2048]{1,0:T(8,128)(2,1)} %dynamic-slice_bitcast_fusion), channel_id=1, source_target_pairs={{0,4},{4,0},{8,12},{12,8},{16,20},{20,16},{24,28},{28,24},{1,5},{5... | collective-permute-start | bytes 6291464 | tf_op jit(solution)/shard_map/ppermute | solution.py:676
  225.1 3.9 copy-start.26
  227.4 4.9 collective-permute-start.1
  227.5 3.6 collective-permute-start.5
  228.9 8.5 %collective-permute-start.4 = (bf16[256,512]{1,0:T(8,128)(2,1)S(1)}, bf16[256,512]{1,0:T(8,128)(2,1)}, u32[]{:S(2)}, u32[]{:S(2)}) collective-permute-start(bf16[256,512]{1,0:T(8,128)(2,1)S(1)} %copy-done.26), channel_id=1, source_target_pairs={{0,2},{1,3},{2,0},{3,1},{4,6},{5,7},{6,4},{7,5},{8,10},{9,11},{10,... | collective-permute-start | bytes 786440 | tf_op jit(solution)/shard_map/ppermute | solution.py:668
  231.0 6.4 copy-start.38
  231.0 58.1 %collective-permute-start.9 = (bf16[512,2048]{1,0:T(8,128)(2,1)}, bf16[512,2048]{1,0:T(8,128)(2,1)}, u32[]{:S(2)}, u32[]{:S(2)}) collective-permute-start(bf16[512,2048]{1,0:T(8,128)(2,1)} %collective-permute-done), channel_id=1, source_target_pairs={{0,1},{1,0},{2,3},{3,2},{4,5},{5,4},{6,7},{7,6},{8,9},{9,8},{10,11... | collective-permute-start | bytes 6291464 | tf_op jit(solution)/shard_map/ppermute | solution.py:668
  231.1 3.2 copy-start.27
  234.9 4.2 copy-start.3
  239.2 3.2 copy-start.21
  239.2 4.8 collective-permute-start.6
  240.9 37.5 %collective-permute-start.7 = (bf16[512,1536]{1,0:T(8,128)(2,1)}, bf16[512,1536]{1,0:T(8,128)(2,1)}, u32[]{:S(2)}, u32[]{:S(2)}) collective-permute-start(bf16[512,1536]{1,0:T(8,128)(2,1)} %fusion.6), channel_id=1, source_target_pairs={{0,4},{4,0},{8,12},{12,8},{16,20},{20,16},{24,28},{28,24},{1,5},{5... | collective-permute-start | bytes 4718600 | tf_op jit(solution)/shard_map/ppermute | solution.py:676
  259.7 29.4 %collective-permute-start.8 = (bf16[1024,256]{1,0:T(8,128)(2,1)}, bf16[1024,256]{1,0:T(8,128)(2,1)}, u32[]{:S(2)}, u32[]{:S(2)}) collective-permute-start(bf16[1024,256]{1,0:T(8,128)(2,1)} %copy.44), channel_id=1, source_target_pairs={{0,4},{4,0},{8,12},{12,8},{16,20},{20,16},{24,28},{28,24},{1,5},{5... | collective-permute-start | bytes 1572872 | tf_op jit(solution)/shard_map/ppermute | solution.py:676
  260.3 28.8 %copy-start.18 = (bf16[2,2,256,512]{3,2,1,0:T(8,128)(2,1)S(1)}, bf16[2,2,256,512]{3,2,1,0:T(8,128)(2,1)}, u32[]{:S(2)}) copy-start(bf16[2,2,256,512]{3,2,1,0:T(8,128)(2,1)} %copy.40) | copy-start | bytes 3145732
  293.8 137.6 %reduce-scatter.7.cloned.1.call-start = ((), (), s32[]{:S(2)}) async-start(), calls=%async_computation.6 | async-start | bytes 5242880 | tf_op jit(solution)/shard_map/reduce_scatter | solution.py:924
  296.5 11.2 %collective-permute-start.10 = (bf16[512,1536]{1,0:T(8,128)(2,1)}, bf16[512,1536]{1,0:T(8,128)(2,1)}, u32[]{:S(2)}, u32[]{:S(2)}) collective-permute-start(bf16[512,1536]{1,0:T(8,128)(2,1)} %collective-permute-done.7), channel_id=1, source_target_pairs={{0,1},{1,0},{2,3},{3,2},{4,5},{5,4},{6,7},{7,6},{8,9},{9,8},{10,11... | collective-permute-start | bytes 4718600 | tf_op jit(solution)/shard_map/ppermute | solution.py:668
  333.5 17.5 %copy-start.56 = (f32[512]{0:T(512)S(1)}, f32[512]{0:T(512)}, u32[]{:S(2)}) copy-start(f32[512]{0:T(512)} %get-tuple-element.108) | copy-start | bytes 6148
  338.4 12.6 %copy-start.19 = (bf16[1,1024,512]{2,1,0:T(8,128)(2,1)S(1)}, bf16[1,1024,512]{2,1,0:T(8,128)(2,1)}, u32[]{:S(2)}) copy-start(bf16[1,1024,512]{2,1,0:T(8,128)(2,1)} %reduce-scatter.5.cloned.1.call-done) | copy-start | bytes 3145732
  355.0 31.9 %collective-permute-start.11 = (bf16[1024,512]{1,0:T(8,128)(2,1)}, bf16[1024,512]{1,0:T(8,128)(2,1)S(1)}, u32[]{:S(2)}, u32[]{:S(2)}) collective-permute-start(bf16[1024,512]{1,0:T(8,128)(2,1)} %multiply_convert_fusion.1.g_ref), channel_id=1, source_target_pairs={{0,4},{4,0},{8,12},{12,8},{16,20},{20,16},{24,28},{28,24},{1,5},{5... | collective-permute-start | bytes 3145736 | tf_op jit(solution)/shard_map/ppermute | solution.py:676
  387.8 342.3 %reduce-scatter.9.cloned.1.call-start = ((), (), s32[]{:S(2)}) async-start(), calls=%async_computation.7 | async-start | bytes 4423680 | tf_op jit(solution)/shard_map/reduce_scatter | solution.py:890
  388.4 350.5 %reduce-scatter.11.cloned.1.call-start = ((), (), s32[]{:S(2)}) async-start(), calls=%async_computation.8 | async-start | bytes 11796480 | tf_op jit(solution)/shard_map/reduce_scatter | solution.py:927
  432.1 6.8 collective-permute-start.3
  434.1 18.4 %copy-start.32 = (f32[2048]{0:T(1024)S(1)}, f32[2048]{0:T(1024)}, u32[]{:S(2)}) copy-start(f32[2048]{0:T(1024)} %param.39) | copy-start | bytes 24580
  434.2 18.2 %copy-start.2 = (f32[256,2048]{1,0:T(8,128)S(1)}, f32[256,2048]{1,0:T(8,128)}, u32[]{:S(2)}) copy-start(f32[256,2048]{1,0:T(8,128)} %get-tuple-element.240) | copy-start | bytes 6291460
  434.2 18.2 %copy-start.6 = (bf16[256,2048]{1,0:T(8,128)(2,1)S(1)}, bf16[256,2048]{1,0:T(8,128)(2,1)}, u32[]{:S(2)}) copy-start(bf16[256,2048]{1,0:T(8,128)(2,1)} %param.25) | copy-start | bytes 3145732
  438.3 84.5 %collective-permute-start.2 = (f32[256,512]{1,0:T(8,128)}, f32[256,512]{1,0:T(8,128)}, u32[]{:S(2)}, u32[]{:S(2)}) collective-permute-start(f32[256,512]{1,0:T(8,128)} %slice.314), channel_id=1, source_target_pairs={{0,2},{1,3},{2,0},{3,1},{4,6},{5,7},{6,4},{7,5},{8,10},{9,11},{10,... | collective-permute-start | bytes 1572872 | tf_op jit(solution)/shard_map/ppermute | solution.py:668
  452.4 20.3 %copy-start.34 = (f32[2048]{0:T(1024)S(1)}, f32[2048]{0:T(1024)}, u32[]{:S(2)}) copy-start(f32[2048]{0:T(1024)} %get-tuple-element.103) | copy-start | bytes 24580
  471.4 4.2 copy-start.33
  475.7 19.0 %copy-start.52 = (f32[1,512]{1,0:T(1,128)S(1)}, f32[1,512]{1,0:T(1,128)}, u32[]{:S(2)}) copy-start(f32[1,512]{1,0:T(1,128)} %get-tuple-element.167) | copy-start | bytes 6148
  496.7 11.4 %copy-start.15 = (f32[256,512]{1,0:T(8,128)S(1)}, f32[256,512]{1,0:T(8,128)}, u32[]{:S(2)}) copy-start(f32[256,512]{1,0:T(8,128)} %copy-done.14) | copy-start | bytes 1572868
  496.7 11.4 %copy-start.36 = (f32[512]{0:T(512)S(1)}, f32[512]{0:T(512)}, u32[]{:S(2)}) copy-start(f32[512]{0:T(512)} %copy-done.35) | copy-start | bytes 6148
  496.7 11.4 %copy-start.41 = (f32[1,512]{1,0:T(1,128)S(1)}, f32[1,512]{1,0:T(1,128)}, u32[]{:S(2)}) copy-start(f32[1,512]{1,0:T(1,128)} %copy-done.40) | copy-start | bytes 6148
  496.7 11.4 %copy-start.43 = (f32[1,512]{1,0:T(1,128)S(1)}, f32[1,512]{1,0:T(1,128)}, u32[]{:S(2)}) copy-start(f32[1,512]{1,0:T(1,128)} %copy-done.42) | copy-start | bytes 6148
  496.7 26.1 %copy-start.60 = (f32[1,512]{1,0:T(1,128)S(1)}, f32[1,512]{1,0:T(1,128)}, u32[]{:S(2)}) copy-start(f32[1,512]{1,0:T(1,128)} %get-tuple-element.166) | copy-start | bytes 6148
  521.5 3.7 copy-start.7
  525.2 9.3 %copy-start.51 = (f32[512]{0:T(512)S(1)}, f32[512]{0:T(512)}, u32[]{:S(2)}) copy-start(f32[512]{0:T(512)} %copy-done.49) | copy-start | bytes 6148
  525.2 9.3 %copy-start.55 = (f32[512]{0:T(512)S(1)}, f32[512]{0:T(512)}, u32[]{:S(2)}) copy-start(f32[512]{0:T(512)} %copy-done.53) | copy-start | bytes 6148
  525.2 9.3 %copy-start.77 = (f32[1,512]{1,0:T(1,128)S(1)}, f32[1,512]{1,0:T(1,128)}, u32[]{:S(2)}) copy-start(f32[1,512]{1,0:T(1,128)} %copy-done.75) | copy-start | bytes 6148
  525.2 9.3 %copy-start.80 = (f32[1,512]{1,0:T(1,128)S(1)}, f32[1,512]{1,0:T(1,128)}, u32[]{:S(2)}) copy-start(f32[1,512]{1,0:T(1,128)} %copy-done.78) | copy-start | bytes 6148
  527.3 7.3 copy-start.17
  527.3 9.4 %slice-start = ((s8[4718592]{0:T(1024)(128)(4,1)}), s8[524288]{0:T(1024)(128)(4,1)S(1)}, s32[]{:S(2)}) async-start(s8[4718592]{0:T(1024)(128)(4,1)} %bitcast.312), calls=%async_computation.10 | async-start | bytes 1048576
  531.3 5.4 slice-start.1
  539.2 3.4 copy-start.24
  726.8 4.8 copy-start.58
  726.8 4.8 copy-start.59
  726.8 5.4 copy-start.57
  (39 other events, 63.7 us)
Sparse Core Ops, SparseCore 0:
  85.0 34.7 all-gather.3
  167.8 34.5 all-gather.5
  293.9 44.4 reduce-scatter.4
  387.0 43.5 reduce-scatter.6
  432.8 69.2 reduce-scatter.8
  504.3 209.6 reduce-scatter.10

commit v3 on v2

--- a/solution.py
+++ b/solution.py
@@ -26,7 +26,7 @@
     return (row_of, col_of, living, height, map_width)
 
 
-def shift_matrices(shape_info, dilation):
+def neighbours(shape_info, dilation):
     row_of, col_of, living, height, map_width = shape_info
     span = row_of.shape[1]
     position = jnp.arange(span, dtype=jnp.int32)
@@ -43,9 +43,14 @@
                 & (target_col < map_width)
             )
             neighbour = position[None, :] + dilation * (step_row * map_width + step_col)
-            picked = jnp.where(inside, neighbour, -1)
-            every.append(picked[:, :, None] == position[None, None, :])
-    return jnp.stack(every, 0).astype(BF16)
+            every.append(jnp.where(inside, neighbour, -1))
+    return jnp.concatenate(every, 0).T
+
+
+def shift_matrices(shape_info, dilation):
+    devices, span = shape_info[0].shape
+    picks = neighbours(shape_info, dilation).T.reshape(9, devices, span, 1)
+    return (picks == jnp.arange(span, dtype=jnp.int32)).astype(BF16)
 
 
 def product(left_side, right_side):
@@ -70,44 +75,6 @@
 
 def cost(flops, moved):
     return pl.CostEstimate(flops=flops, bytes_accessed=moved, transcendentals=0)
-
-
-def heads_forward_kernel(u_ref, w_ref, s_ref, out_ref):
-    tap = pl.program_id(0)
-    blocks, span = s_ref.shape[1], s_ref.shape[2]
-    half = blocks // 2
-
-    @pl.when(tap == 0)
-    def _():
-        out_ref[...] = jnp.zeros_like(out_ref)
-
-    @pl.loop(0, 2)
-    def _(part):
-        rows = pl.ds(pl.multiple_of(part * half * span, half * span), half * span)
-        y = against(u_ref[rows, :], w_ref[...]).astype(BF16)
-        for k in range(half):
-            at = pl.ds(pl.multiple_of((part * half + k) * span, span), span)
-            out_ref[at, :] += product(s_ref[0, part * half + k], y[k * span : (k + 1) * span])
-
-
-def heads_forward(u, w_heads, shifts):
-    rows, wide = u.shape
-    outs = w_heads.shape[0]
-    taps, blocks, span, _ = shifts.shape
-    return pl.pallas_call(
-        heads_forward_kernel,
-        grid=(taps,),
-        in_specs=[
-            pl.BlockSpec((rows, wide), lambda t: (0, 0)),
-            pl.BlockSpec((outs, wide), lambda t: (0, t)),
-            pl.BlockSpec((1, blocks, span, span), lambda t: (t, 0, 0, 0)),
-        ],
-        out_specs=pl.BlockSpec((rows, outs), lambda t: (0, 0)),
-        out_shape=jax.ShapeDtypeStruct((rows, outs), F32),
-        compiler_params=params(),
-        cost_estimate=cost(2 * rows * wide * outs * taps, w_heads.size * 2 + u.size * 2),
-        name="heads_forward",
-    )(u, w_heads, shifts)
 
 
 def shifted(g_ref, s_ref):
@@ -554,6 +521,339 @@
     )(parts)
 
 
+def send_to(axis, to, src, dst, send_sem, recv_sem):
+    return pltpu.make_async_remote_copy(
+        src_ref=src,
+        dst_ref=dst,
+        send_sem=send_sem,
+        recv_sem=recv_sem,
+        device_id={axis: to},
+        device_id_type=MESH,
+    )
+
+
+def total_along(axis, size, block, slots, send_sems, recv_sems, meanwhile=None):
+    me = lax.axis_index(axis)
+    others = [lax.rem(me + k, size) for k in range(1, size)]
+    for other in others:
+        send_to(axis, other, block, slots.at[me], send_sems.at[other], recv_sems.at[me]).start()
+    slots[me] = block[...]
+    if meanwhile is not None:
+        meanwhile()
+    for other in others:
+        copy = send_to(
+            axis, other, block, slots.at[other], send_sems.at[other], recv_sems.at[other]
+        )
+        copy.wait_recv()
+        copy.wait_send()
+    total = slots[0]
+    for k in range(1, size):
+        total = total + slots[k]
+    return total
+
+
+def place_in_map(layout_ref, device, span):
+    position = lax.broadcasted_iota(jnp.int32, (span, 1), 0)
+    large = layout_ref[device, 1] == 16
+    row_of = jnp.where(large, position // 16, (position % 64) // 8)
+    col_of = jnp.where(large, position % 16, position % 8)
+    return position, row_of, col_of
+
+
+def live_mask(layout_ref, device, span):
+    position = lax.broadcasted_iota(jnp.int32, (span, 1), 0)
+    return position < layout_ref[device, 0] * layout_ref[device, 1] * layout_ref[device, 2]
+
+
+def live_column(layout_ref, device, span):
+    return jnp.where(live_mask(layout_ref, device, span), 1.0, 0.0)
+
+
+def inverse_count(areas_ref, span):
+    areas = areas_ref[:, 0:1] * areas_ref[:, 1:2] * areas_ref[:, 2:3]
+    return 1.0 / jnp.sum(jnp.minimum(areas, span).astype(F32), 0, keepdims=True)
+
+
+def shift_block(layout_ref, device, dilation, tap, span):
+    position, row_of, col_of = place_in_map(layout_ref, device, span)
+    height, map_width = layout_ref[device, 0], layout_ref[device, 1]
+    step_row, step_col = dilation * (tap // 3 - 1), dilation * (tap % 3 - 1)
+    target_row, target_col = row_of + step_row, col_of + step_col
+    inside = (
+        live_mask(layout_ref, device, span)
+        & (target_row >= 0)
+        & (target_row < height)
+        & (target_col >= 0)
+        & (target_col < map_width)
+    )
+    neighbour = jnp.where(inside, position + step_row * map_width + step_col, -1)
+    lanes = lax.broadcasted_iota(jnp.int32, (span, span), 1)
+    return jnp.where(neighbour == lanes, 1.0, 0.0).astype(BF16)
+
+
+def trunk_kernel(
+    sizes,
+    in_ref,
+    layout_ref,
+    areas_ref,
+    w_reduce_ref,
+    w_spatial_hbm,
+    w_expand_hbm,
+    w_heads_hbm,
+    gain_mid_ref,
+    shift_mid_ref,
+    gain_wide_ref,
+    shift_wide_ref,
+    reduced_ref,
+    sums_one_ref,
+    hidden_one_ref,
+    spatial_ref,
+    sums_two_ref,
+    hidden_two_ref,
+    expanded_ref,
+    sums_three_ref,
+    trunk_ref,
+    headed_ref,
+    own_shift_ref,
+    all_shift_ref,
+    w_spatial_ref,
+    w_expand_ref,
+    w_heads_ref,
+    block_mid,
+    block_wide,
+    slots_mid_rep,
+    slots_mid_dp,
+    slots_wide_rep,
+    slots_wide_dp,
+    load_sems,
+    rep_send,
+    rep_recv,
+    dp_send,
+    dp_recv,
+    gather_send,
+    gather_recv,
+):
+    n_rep, n_dp = sizes
+    rep = lax.axis_index("rep")
+    par, upper = lax.rem(rep, 2), rep // 2
+    mate, far = rep + 1 - 2 * par, rep + 2 - 4 * upper
+    span, wide = in_ref.shape
+    middle = w_reduce_ref.shape[1]
+    taps = own_shift_ref.shape[0]
+    loads = [
+        pltpu.make_async_copy(w_spatial_hbm, w_spatial_ref, load_sems.at[0]),
+        pltpu.make_async_copy(w_expand_hbm, w_expand_ref, load_sems.at[1]),
+    ]
+    heads_load = pltpu.make_async_copy(w_heads_hbm, w_heads_ref, load_sems.at[2])
+    for load in loads:
+        load.start()
+    heads_load.start()
+
+    barrier = pltpu.get_barrier_semaphore()
+    for axis, size in (("rep", n_rep), ("dp", n_dp)):
+        me = lax.axis_index(axis)
+        for k in range(1, size):
+            pl.semaphore_signal(
+                barrier, inc=1, device_id={axis: lax.rem(me + k, size)}, device_id_type=MESH
+            )
+    first_row = lax.axis_index("dp") * n_rep
+    live = live_column(layout_ref, first_row + rep, span)
+    inverse = inverse_count(areas_ref, span)
+
+    def make_own():
+        for t in range(taps):
+            own_shift_ref[t] = shift_block(layout_ref, first_row + rep, 2, t, span)
+
+    def make_all(first, last):
+        def fill():
+            for t in range(first, last):
+                for p in range(n_rep):
+                    all_shift_ref[t, p] = shift_block(layout_ref, first_row + p, 1, t, span)
+
+        return fill
+
+    def everywhere(number, value_ref, blocks, rep_slots, dp_slots, meanwhile, later):
+        masked = live * value_ref[...]
+        blocks[0, 0:1, :] = jnp.sum(masked, 0, keepdims=True)
+        blocks[0, 1:2, :] = jnp.sum(masked * value_ref[...], 0, keepdims=True)
+        if number == 0:
+            pl.semaphore_wait(barrier, n_rep + n_dp - 2)
+        blocks[1] = total_along(
+            "rep", n_rep, blocks.at[0], rep_slots, rep_send.at[number], rep_recv.at[number], meanwhile
+        )
+        return total_along(
+            "dp", n_dp, blocks.at[1], dp_slots, dp_send.at[number], dp_recv.at[number], later
+        )
+
+    def normed(value, sums, gain, shift):
+        center = sums[0:1] * inverse
+        scaling = lax.rsqrt(sums[1:2] * inverse - center * center + EPS)
+        return (value - center) * (scaling * gain) + shift
+
+    def silu(value):
+        return value * jax.nn.sigmoid(value)
+
+    reduced_ref[...] = product(in_ref[...], w_reduce_ref[...])
+    sums = everywhere(
+        0, reduced_ref, block_mid.at[0], slots_mid_rep.at[0], slots_mid_dp.at[0], make_own, None
+    )
+    sums_one_ref[...] = sums
+    hidden_one_ref[...] = silu(
+        normed(reduced_ref[...], sums, gain_mid_ref[0:1, :], shift_mid_ref[0:1, :])
+    ).astype(BF16)
+    loads[0].wait()
+    spatial_ref[...] = jnp.zeros_like(spatial_ref)
+
+    @pl.loop(0, taps)
+    def _(t):
+        moved = product(own_shift_ref[t], hidden_one_ref[...]).astype(BF16)
+        at = pl.ds(pl.multiple_of(t * middle, middle), middle)
+        spatial_ref[...] += product(moved, w_spatial_ref[at, :])
+
+    sums = everywhere(
+        1, spatial_ref, block_mid.at[1], slots_mid_rep.at[1], slots_mid_dp.at[1], make_all(0, 5), None
+    )
+    sums_two_ref[...] = sums
+    hidden_two_ref[...] = silu(
+        normed(spatial_ref[...], sums, gain_mid_ref[1:2, :], shift_mid_ref[1:2, :])
+    ).astype(BF16)
+    loads[1].wait()
+    expanded_ref[...] = product(hidden_two_ref[...], w_expand_ref[...])
+    sums = everywhere(
+        2, expanded_ref, block_wide, slots_wide_rep, slots_wide_dp, make_all(5, 9), None
+    )
+    sums_three_ref[...] = sums
+
+    own_rows = pl.ds(pl.multiple_of(par * span, span), span)
+    mate_rows = pl.ds(pl.multiple_of((1 - par) * span, span), span)
+    pre = normed(expanded_ref[...], sums, gain_wide_ref[...], shift_wide_ref[...])
+    trunk_ref[upper, own_rows, :] = silu(pre + in_ref[...].astype(F32)).astype(BF16)
+    parts = 4
+    piece = span // parts
+
+    def rows(parity, k):
+        return pl.ds(pl.multiple_of(parity * span + k * piece, piece), piece)
+
+    def across(side, k):
+        at = trunk_ref.at[side, rows(par, k)]
+        return send_to("rep", far, at, at, gather_send.at[k], gather_recv.at[k])
+
+    def own_pass(parity):
+        at = trunk_ref.at[upper, pl.ds(pl.multiple_of(parity * span, span), span)]
+        return send_to("rep", mate, at, at, gather_send.at[parts], gather_recv.at[parts])
+
+    def far_pass(parity, k):
+        at = trunk_ref.at[1 - upper, rows(parity, k)]
+        slot = parts + 1 + k
+        return send_to("rep", mate, at, at, gather_send.at[slot], gather_recv.at[slot])
+
+    for k in range(parts):
+        across(upper, k).start()
+    own_pass(par).start()
+    headed_ref[...] = jnp.zeros_like(headed_ref)
+    own_pass(1 - par).wait_recv()
+    heads_load.wait()
+
+    def convolve(side):
+        @pl.loop(0, taps)
+        def _(t):
+            at = pl.ds(pl.multiple_of(t * wide, wide), wide)
+            y = against(trunk_ref[side], w_heads_ref[:, at]).astype(BF16)
+            for k in range(2):
+                place = pl.ds(k * span, span)
+                headed_ref[side, place, :] += product(
+                    all_shift_ref[t, 2 * side + k], y[k * span : (k + 1) * span]
+                )
+
+    convolve(upper)
+    for k in range(parts):
+        across(1 - upper, k).wait_recv()
+        far_pass(par, k).start()
+    for k in range(parts):
+        far_pass(1 - par, k).wait_recv()
+    convolve(1 - upper)
+    for k in range(parts):
+        across(upper, k).wait_send()
+        far_pass(par, k).wait_send()
+    own_pass(par).wait_send()
+
+
+def trunk_forward(
+    inputs,
+    layout,
+    w_reduce,
+    w_spatial,
+    w_expand,
+    w_heads,
+    gain_mid,
+    shift_mid,
+    gain_wide,
+    shift_wide,
+):
+    span, wide = inputs.shape
+    middle = w_reduce.shape[1]
+    n_rep, n_dp = lax.axis_size("rep"), lax.axis_size("dp")
+    taps = 9
+    vmem = pl.BlockSpec(memory_space=pltpu.VMEM)
+    hbm = pl.BlockSpec(memory_space=pl.ANY)
+    smem = pl.BlockSpec(memory_space=pltpu.SMEM)
+    dma = pltpu.SemaphoreType.DMA
+    shape = jax.ShapeDtypeStruct
+    return pl.pallas_call(
+        functools.partial(trunk_kernel, (n_rep, n_dp)),
+        in_specs=[vmem, smem, vmem, vmem] + [hbm] * 3 + [vmem] * 4,
+        out_specs=[vmem] * 12,
+        out_shape=[
+            shape((span, middle), F32),
+            shape((2, middle), F32),
+            shape((span, middle), BF16),
+            shape((span, middle), F32),
+            shape((2, middle), F32),
+            shape((span, middle), BF16),
+            shape((span, wide), F32),
+            shape((2, wide), F32),
+            shape((2, 2 * span, wide), BF16),
+            shape((2, 2 * span, w_heads.shape[0]), F32),
+            shape((taps, span, span), BF16),
+            shape((taps, n_rep, span, span), BF16),
+        ],
+        scratch_shapes=[
+            pltpu.VMEM(w_spatial.shape, BF16),
+            pltpu.VMEM(w_expand.shape, BF16),
+            pltpu.VMEM(w_heads.shape, BF16),
+            pltpu.VMEM((2, 2, 2, middle), F32),
+            pltpu.VMEM((2, 2, wide), F32),
+            pltpu.VMEM((2, n_rep, 2, middle), F32),
+            pltpu.VMEM((2, n_dp, 2, middle), F32),
+            pltpu.VMEM((n_rep, 2, wide), F32),
+            pltpu.VMEM((n_dp, 2, wide), F32),
+            dma((3,)),
+            dma((3, n_rep)),
+            dma((3, n_rep)),
+            dma((3, n_dp)),
+            dma((3, n_dp)),
+            dma((9,)),
+            dma((9,)),
+        ],
+        compiler_params=pltpu.CompilerParams(
+            collective_id=10, has_side_effects=True, vmem_limit_bytes=VMEM_LIMIT
+        ),
+        name="trunk_forward",
+    )(
+        inputs,
+        layout,
+        layout,
+        w_reduce,
+        w_spatial,
+        w_expand,
+        w_heads,
+        gain_mid,
+        shift_mid,
+        gain_wide[None, :],
+        shift_wide[None, :],
+    )
+
+
 def silu_slope(value_in):
     sigma_of = jax.nn.sigmoid(value_in)
     return sigma_of * (1.0 + value_in * (1.0 - sigma_of))
@@ -732,8 +1032,6 @@
     pixel_count = jnp.sum(
         jnp.minimum(layout[:, 0] * layout[:, 1] * layout[:, 2], pixels)
     ).astype(F32)
-    shifts_own = shift_matrices(own_info, 2)
-    shifts_all = shift_matrices(group_info, 1)
     split = lax.axis_size("dp") == 8
     if split:
         side = lax.axis_index("dp") % 2
@@ -746,31 +1044,47 @@
     zero = jnp.zeros((1,), jnp.int32)
     first = jnp.reshape(9 * parity, (1,)).astype(jnp.int32)
 
-    reduced = product(inputs, w_reduce)
-    sums_one, squares_one = moments(reduced, living, everyone)
+    (
+        reduced,
+        sums_one,
+        hidden_one,
+        spatial,
+        sums_two,
+        hidden_two,
+        expanded,
+        sums_three,
+        trunk_all,
+        headed,
+        shifts_own,
+        shifts_all,
+    ) = trunk_forward(
+        inputs,
+        layout,
+        w_reduce,
+        w_spatial,
+        w_expand,
+        w_heads,
+        gain_mid,
+        shift_mid,
+        gain_wide,
+        shift_wide,
+    )
+    shifts_own = shifts_own[:, None]
+    trunk_all = trunk_all.reshape(group * pixels, -1)
+    headed = headed.reshape(group * pixels, middle)
     normed_one, unit_one, scale_one = normalize(
-        reduced, sums_one, squares_one, pixel_count, gain_mid[0], shift_mid[0]
-    )
-    hidden_one = jax.nn.silu(normed_one).astype(BF16)
-    spatial = rows_forward(zero, hidden_one, w_spatial, shifts_own, 1)
-    sums_two, squares_two = moments(spatial, living, everyone)
+        reduced, sums_one[0], sums_one[1], pixel_count, gain_mid[0], shift_mid[0]
+    )
     normed_two, unit_two, scale_two = normalize(
-        spatial, sums_two, squares_two, pixel_count, gain_mid[1], shift_mid[1]
-    )
-    hidden_two = jax.nn.silu(normed_two).astype(BF16)
-    expanded = product(hidden_two, w_expand)
-    sums_three, squares_three = moments(expanded, living, everyone)
+        spatial, sums_two[0], sums_two[1], pixel_count, gain_mid[1], shift_mid[1]
+    )
     normed_three, unit_three, scale_three = normalize(
-        expanded, sums_three, squares_three, pixel_count, gain_wide, shift_wide
+        expanded, sums_three[0], sums_three[1], pixel_count, gain_wide, shift_wide
     )
     pre_act = normed_three + inputs.astype(F32)
-    trunk = jax.nn.silu(pre_act).astype(BF16)
-    trunk_all = lax.all_gather(trunk, "rep", axis=0, tiled=True)
-
     if split:
         trunk_mine = swap_x(own_half(trunk_all, parity))
 
-    headed = heads_forward(trunk_all, w_heads, shifts_all)
     own_gain = lax.dynamic_slice_in_dim(gain_head, rep * middle, middle, 0)
     own_shift = lax.dynamic_slice_in_dim(shift_head, rep * middle, middle, 0)
     sums_head, squares_head = moments(headed, living_all, ("dp",))

time: 761 us -> 694 us (0.912)
  other arithmetic: 107 us -> 74.3 us
  waiting for transfers between devices: 77.9 us -> 55.3 us
  matrix products: 19.8 us -> 11 us
    pallas_call x1, Pallas kernels: 32.1 us -> 75.1 us  [trunk_forward(): pl.pallas_call(functools.partial(trunk_kernel, (n_rep, n_dp)), in_specs=[...]
    pallas_call x8 -> x5, Pallas kernels: 88 us -> 56.7 us  [total_of(): pl.pallas_call(functools.partial(total_kernel, sized), out_shape=jax.Shap...]
    all_gather x1 -> x0, waiting for transfers between devices: 26.5 us -> none  [shards(): trunk_all = lax.all_gather(trunk, 'rep', axis=0, tiled=True)]
    pallas_call x2 -> x1, Pallas kernels: 25.5 us -> 16.5 us  [rows_forward(): pl.pallas_call(rows_forward_kernel, grid_spec=pltpu.PrefetchScalarGridSpe...]
    convert_element_type x5 -> x2, other arithmetic: 12 us -> 3.19 us  [the longest x1 3.18 us: shift_matrices(): return (picks == jnp.arange(span, dtype=jnp.int32)).astype(BF16)]
    unnamed x180 -> x103, local copies, waits for them, and re-layouts: 12.4 us -> 16 us
  transfers between devices with their start and end apart: 18 -> 17, of which waited for: 7 -> 6; matrix products, arithmetic and copies ran while one was open for 16% -> 16% of each run, Pallas kernels for 47% -> 52%
where the time goes in v3:
time: 694 us; the launch traced here: 684 us
  Pallas kernels  448 us (65%)
  other arithmetic  74.3 us (11%)
  local copies, waits for them, and re-layouts  55.3 us (8%)
  waiting for transfers between devices  55.3 us (8%)
  between operations  17.5 us (3%)
  blocking collectives  12 us (2%)
  matrix products  11 us (2%)
  starting transfers between devices  10.3 us (1%)
    pallas_call x1, Pallas kernels, small_total(): pl.pallas_call(small_kernel, out_shape=jax.ShapeDtypeStruct((rows, lanes)...  178 us
    pallas_call x1, Pallas kernels, trunk_forward(): pl.pallas_call(functools.partial(trunk_kernel, (n_rep, n_dp)), in_specs=[...  75.1 us
    pallas_call x5, Pallas kernels, total_of(): pl.pallas_call(functools.partial(total_kernel, sized), out_shape=jax.Shap...  56.7 us
    pallas_call x1, Pallas kernels, heads_split(): pl.pallas_call(functools.partial(heads_split_kernel, per_tap, units, lane...  42.8 us
    pallas_call x1, Pallas kernels, heads_data(): pl.pallas_call(heads_data_kernel, grid=(taps,), in_specs=[pl.BlockSpec((r...  30.4 us
    all_gather x1, waiting for transfers between devices, shards(): heads_all = lax.all_gather(rounded, 'rep', axis=0, tiled=False)  29.5 us
    pallas_call x1, Pallas kernels, rows_split(): pl.pallas_call(rows_split_kernel, grid_spec=pltpu.PrefetchScalarGridSpec(...  21.6 us
    pallas_call x1, Pallas kernels, rows_forward(): pl.pallas_call(rows_forward_kernel, grid_spec=pltpu.PrefetchScalarGridSpe...  16.5 us
  transfers between devices with their start and end apart: 17, of which 6 were waited for; matrix products, arithmetic and copies ran while one was open for 16% of the time, Pallas kernels for 52%

profile of v3, /device:TPU:28, one launch (start us, length us, event | category | flops | bytes accessed | tf_op | source)
XLA Modules:
  0.0 683.6 jit_solution(1402067044165203281)
XLA Ops:
  7.3 1.4 minimum_reduce_fusion
  12.9 75.1 %trunk_forward.1 = (f32[256,512]{1,0:T(8,128)}, f32[2,512]{1,0:T(2,128)}, bf16[256,512]{1,0:T(8,128)(2,1)}, f32[256,512]{1,0:T(8,128)}, f32[2,512]{1,0:T(2,128)}...) custom-call(bf16[256,2048]{1,0:T(8,128)(2,1)} %in_ref.1, ...), custom_call_target="tpu_custom_call" | custom-call | tf_op jit(solution)/shard_map/trunk_forward/pallas_call | solution.py:802
  88.0 2.1 multiply_reduce_fusion
  90.7 8.2 %total.5 = f32[8,128]{1,0:T(8,128)} custom-call(f32[8,128]{1,0:T(8,128)} %pad_maximum_fusion.10.x_ref), custom_call_target="tpu_custom_call" | custom-call | tf_op jit(solution)/shard_map/total/pallas_call | solution.py:929
  101.3 1.6 multiply_convert_fusion.2
  103.5 3.2 dynamic-slice_bitcast_fusion
  106.6 1.5 collective-permute-start
  108.2 29.5 %all-gather.2.cloned.1.call-done = bf16[4,1024,512]{2,1,0:T(8,128)(2,1)} async-done(((bf16[1,1024,512]{2,1,0:T(8,128)(2,1)}), bf16[4,1024,512]{2,1,0:T(8,128)(2,1)}) %all-gather.2.cloned.1.call-update) | async-done | bytes 4194320 | tf_op jit(solution)/shard_map/all_gather | solution.py:1095
  137.7 4.7 fusion.56
  142.3 2.0 maximum_select_fusion.u_ref
  144.3 16.5 %rows_forward.1 = f32[1024,512]{1,0:T(8,128)} custom-call(s32[1]{0:T(128)} %bitcast.10.first_ref, bf16[1024,1536]{1,0:T(8,128)(2,1)} %maximum_select_fusion.u_ref, bf16[6912,512]{1,0:T(8,128)(2,1)} %w_ref.5, bf16[9,4,256,256]{3,2,1,0:T(8,128)(2,1)} %get-tuple-element.46.s_ref), custom_call_target="tpu_custom_call" | custom-call | flops 7247757312 | bytes 7077888 | tf_op jit(solution)/shard_map/rows_forward/pallas_call | solution.py:176
  160.9 2.3 dynamic-slice_bitcast_fusion.1
  163.2 1.5 collective-permute-start.5
  167.9 1.9 bitcast_add_fusion
  171.0 2.2 collective-permute-done.4
  173.2 1.7 multiply_convert_fusion.3
  175.5 1.5 fusion.10
  177.0 1.5 collective-permute-start.7
  180.2 2.0 copy.63
  182.2 2.0 copy.62
  184.2 3.4 pad_maximum_fusion.4
  187.6 1.5 reshape_reshape.3
  189.2 2.5 copy.64
  191.6 2.1 constant_dynamic-slice_fusion.1
  195.3 16.0 %rows_data.1 = bf16[1024,1536]{1,0:T(8,128)(2,1)} custom-call(s32[1]{0:T(128)} %bitcast.10.first_ref, bf16[1024,512]{1,0:T(8,128)(2,1)} %bitcast.256, bf16[6912,512]{1,0:T(8,128)(2,1)} %w_ref.5, bf16[9,4,256,256]{3,2,1,0:T(8,128)(2,1)} %get-tuple-element.46.s_ref), custom_call_target="tpu_custom_call" | custom-call | flops 7247757312 | bytes 7077888 | tf_op jit(solution)/shard_map/rows_data/pallas_call | solution.py:352
  211.3 3.3 collective-permute-done.7
  214.6 10.2 %collective-permute-done.8.h_ref = bf16[1024,256]{1,0:T(8,128)(2,1)S(1)} collective-permute-done((bf16[1024,256]{1,0:T(8,128)(2,1)}, bf16[1024,256]{1,0:T(8,128)(2,1)S(1)}, u32[]{:S(2)}, u32[]{:S(2)}) %collective-permute-start.8) | collective-permute-done | bytes 524320 | tf_op jit(solution)/shard_map/ppermute | solution.py:976
  224.8 2.3 bitcast_select_fusion.1
  227.1 2.2 pad_maximum_fusion
  230.3 3.2 fusion.r_ref
  234.5 3.0 broadcast_select_fusion.1
  237.6 2.8 pad_maximum_fusion.1.v_ref
  240.4 2.3 broadcast_select_fusion.3
  242.7 1.8 pad_maximum_fusion.2.v_ref
  244.5 21.6 %rows_split.1 = bf16[256,6912]{1,0:T(8,128)(2,1)} custom-call(s32[1]{0:T(128)} %bitcast.10.first_ref, bf16[1024,256]{1,0:T(8,128)(2,1)} %copy.66.g_ref, bf16[1024,256]{1,0:T(8,128)(2,1)} %copy-done.44, bf16[1024,1536]{1,0:T(8,128)(2,1)} %maximum_select_fusion.u_ref, bf16[1024,1536]{1,0:T(8,128)(2,1)} %pad_maximum_fusion.2.v_ref, ...), custom_call_target="tpu_custom_call" | custom-call | flops 7247757312 | bytes 3538944 | tf_op jit(solution)/shard_map/rows_split/pallas_call | solution.py:316
  266.1 8.0 %reduce-scatter.5.cloned.1.call-done = bf16[1,1024,512]{2,1,0:T(8,128)(2,1)} async-done(((bf16[4,1024,512]{2,1,0:T(8,128)(2,1)}), bf16[1,1024,512]{2,1,0:T(8,128)(2,1)}) %reduce-scatter.5.cloned.1.call-update) | async-done | bytes 1048592 | tf_op jit(solution)/shard_map/reduce_scatter | solution.py:1196
  274.1 2.8 multiply_reduce_fusion.2
  277.5 7.9 %total.6 = f32[8,128]{1,0:T(8,128)} custom-call(f32[8,128]{1,0:T(8,128)} %pad_maximum_fusion.11.x_ref), custom_call_target="tpu_custom_call" | custom-call | tf_op jit(solution)/shard_map/total/pallas_call | solution.py:929
  286.2 2.4 multiply_convert_fusion.1.g_ref
  288.6 1.5 collective-permute-start.11
  290.2 30.4 %heads_data.1 = bf16[1024,2048]{1,0:T(8,128)(2,1)} custom-call(bf16[1024,512]{1,0:T(8,128)(2,1)} %multiply_convert_fusion.1.g_ref, bf16[512,18432]{1,0:T(8,128)(2,1)} %w_ref.6, bf16[9,4,256,256]{3,2,1,0:T(8,128)(2,1)} %get-tuple-element.46.s_ref), custom_call_target="tpu_custom_call" | custom-call | flops 19327352832 | bytes 18874368 | tf_op jit(solution)/shard_map/heads_data/pallas_call | solution.py:113
  322.4 42.8 %heads_split.1 = bf16[4,512,2304]{2,1,0:T(8,128)(2,1)} custom-call(s32[1]{0:T(128)} %bitcast.57.x_ref, bf16[1024,512]{1,0:T(8,128)(2,1)} %multiply_convert_fusion.1.g_ref, bf16[1024,512]{1,0:T(8,128)(2,1)} %copy-done.43, bf16[1024,2048]{1,0:T(8,128)(2,1)} %bitcast.255, bf16[1024,2048]{1,0:T(8,128)(2,1)} %pad_maximum_fusion.1.v_ref, ...), custom_call_target="tpu_custom_call" | custom-call | flops 19327352832 | bytes 18874368 | tf_op jit(solution)/shard_map/heads_split/pallas_call | solution.py:278
  369.2 1.8 collective-permute-start.3
  374.4 12.0 %all_gather.8 = f32[2,2048]{1,0:T(2,128)S(1)} all-gather(f32[2,512]{1,0:T(2,128)S(1)} %pad_maximum_fusion.16), channel_id=1, replica_groups=mesh['dp'=8,'rep'=4] {'rep'}, dimensions={1}, use_global_device_ids=true | all-gather | bytes 20480 | tf_op jit(solution)/shard_map/all_gather | solution.py:1343
  387.0 2.7 multiply_reduce_fusion.1
  390.3 14.0 %total.7 = f32[32,128]{1,0:T(8,128)} custom-call(f32[32,128]{1,0:T(8,128)} %pad_maximum_fusion.9.x_ref), custom_call_target="tpu_custom_call" | custom-call | tf_op jit(solution)/shard_map/total/pallas_call | solution.py:929
  406.3 2.3 multiply_convert_fusion
  408.6 1.7 multiply_reduce_fusion.6
  410.9 14.8 %total.8 = f32[8,128]{1,0:T(8,128)} custom-call(f32[8,128]{1,0:T(8,128)} %pad_maximum_fusion.12.x_ref), custom_call_target="tpu_custom_call" | custom-call | tf_op jit(solution)/shard_map/total/pallas_call | solution.py:929
  427.1 2.1 multiply_convert_fusion.5.g_ref
  429.2 11.3 %rows_back.1 = (f32[256,512]{1,0:T(8,128)}, bf16[4608,512]{1,0:T(8,128)(2,1)}) custom-call(s32[1]{0:T(128)} %constant.128.clone.1.first_ref, bf16[256,512]{1,0:T(8,128)(2,1)} %multiply_convert_fusion.5.g_ref, bf16[256,512]{1,0:T(8,128)(2,1)} %get-tuple-element.64.u_ref, bf16[4608,512]{1,0:T(8,128)(2,1)} %w_ref.7, bf16[9,1,256,256]{3,2,1,0:T(8,128)(2,1)} %bitcast.306), custom_call_target="tpu_custom_call" | custom-call | flops 2415919104 | bytes 9437184 | tf_op jit(solution)/shard_map/rows_back/pallas_call | solution.py:219
  440.5 2.1 multiply_reduce_fusion.5
  443.3 11.7 %total.9 = f32[8,128]{1,0:T(8,128)} custom-call(f32[8,128]{1,0:T(8,128)} %pad_maximum_fusion.13.x_ref), custom_call_target="tpu_custom_call" | custom-call | tf_op jit(solution)/shard_map/total/pallas_call | solution.py:929
  455.7 2.4 multiply_convert_fusion.4
  458.1 2.1 fusion.1
  460.2 3.9 copy.67
  464.2 3.2 constant_dynamic-update-slice_fusion.1
  468.1 4.8 constant_dynamic-update-slice_fusion
  479.0 177.5 %small_total.1 = f32[2560,512]{1,0:T(8,128)} custom-call(bf16[4,2560,512]{2,1,0:T(8,128)(2,1)} %broadcast_dynamic-update-slice_fusion.p_ref), custom_call_target="tpu_custom_call" | custom-call | tf_op jit(solution)/shard_map/small_total/pallas_call | solution.py:500
  656.5 1.9 slice.288
  658.4 2.3 slice.282
  660.7 3.3 slice.283
  669.1 2.1 convolution_add_fusion
  672.5 4.2 bitcast_convert_fusion
  (198 shorter events, 45.3 us)
Async XLA Ops:
  7.2 162.7 %copy-start = (bf16[1024,512]{1,0:T(8,128)(2,1)S(1)}, bf16[1024,512]{1,0:T(8,128)(2,1)}, u32[]{:S(2)}) copy-start(bf16[1024,512]{1,0:T(8,128)(2,1)} %param.25) | copy-start | bytes 3145732
  7.2 130.5 %all-gather.2.cloned.1.call-start = ((), (), s32[]{:S(2)}) async-start(), calls=%async_computation.4 | async-start | bytes 5242880 | tf_op jit(solution)/shard_map/all_gather | solution.py:1095
  88.0 13.2 %copy-start.2 = (f32[2,512,512]{2,1,0:T(8,128)S(1)}, f32[2,512,512]{2,1,0:T(8,128)}, u32[]{:S(2)}) copy-start(f32[2,512,512]{2,1,0:T(8,128)} %get-tuple-element.45) | copy-start | bytes 6291460
  102.9 171.2 %reduce-scatter.5.cloned.1.call-start = ((), (), s32[]{:S(2)}) async-start(), calls=%async_computation.5 | async-start | bytes 5242880 | tf_op jit(solution)/shard_map/reduce_scatter | solution.py:1196
  106.6 54.2 %collective-permute-start = (bf16[512,2048]{1,0:T(8,128)(2,1)}, bf16[512,2048]{1,0:T(8,128)(2,1)}, u32[]{:S(2)}, u32[]{:S(2)}) collective-permute-start(bf16[512,2048]{1,0:T(8,128)(2,1)} %dynamic-slice_bitcast_fusion), channel_id=1, source_target_pairs={{0,4},{4,0},{8,12},{12,8},{16,20},{20,16},{24,28},{28,24},{1,5},{5... | collective-permute-start | bytes 6291464 | tf_op jit(solution)/shard_map/ppermute | solution.py:976
  160.9 2.4 copy-start.42
  160.9 3.9 copy-start.28
  163.2 4.7 collective-permute-start.1
  163.2 3.6 collective-permute-start.5
  164.7 8.5 %collective-permute-start.4 = (bf16[256,512]{1,0:T(8,128)(2,1)S(1)}, bf16[256,512]{1,0:T(8,128)(2,1)}, u32[]{:S(2)}, u32[]{:S(2)}) collective-permute-start(bf16[256,512]{1,0:T(8,128)(2,1)S(1)} %copy-done.28), channel_id=1, source_target_pairs={{0,2},{1,3},{2,0},{3,1},{4,6},{5,7},{6,4},{7,5},{8,10},{9,11},{10,... | collective-permute-start | bytes 786440 | tf_op jit(solution)/shard_map/ppermute | solution.py:968
  166.8 47.7 %collective-permute-start.9 = (bf16[512,2048]{1,0:T(8,128)(2,1)}, bf16[512,2048]{1,0:T(8,128)(2,1)}, u32[]{:S(2)}, u32[]{:S(2)}) collective-permute-start(bf16[512,2048]{1,0:T(8,128)(2,1)} %collective-permute-done), channel_id=1, source_target_pairs={{0,1},{1,0},{2,3},{3,2},{4,5},{5,4},{6,7},{7,6},{8,9},{9,8},{10,11... | collective-permute-start | bytes 6291464 | tf_op jit(solution)/shard_map/ppermute | solution.py:968
  167.9 2.6 copy-start.26
  169.9 0.8 copy-start.29
  170.5 4.4 copy-start.3
  173.2 1.8 copy-start.13
  173.2 1.8 copy-start.14
  173.2 1.9 copy-start.15
  173.2 2.2 copy-start.16
  174.9 3.6 copy-start.18
  174.9 5.2 collective-permute-start.6
  177.0 37.6 %collective-permute-start.7 = (bf16[512,1536]{1,0:T(8,128)(2,1)}, bf16[512,1536]{1,0:T(8,128)(2,1)}, u32[]{:S(2)}, u32[]{:S(2)}) collective-permute-start(bf16[512,1536]{1,0:T(8,128)(2,1)} %fusion.10), channel_id=1, source_target_pairs={{0,4},{4,0},{8,12},{12,8},{16,20},{20,16},{24,28},{28,24},{1,5},{5... | collective-permute-start | bytes 4718600 | tf_op jit(solution)/shard_map/ppermute | solution.py:976
  194.7 30.1 %collective-permute-start.8 = (bf16[1024,256]{1,0:T(8,128)(2,1)}, bf16[1024,256]{1,0:T(8,128)(2,1)S(1)}, u32[]{:S(2)}, u32[]{:S(2)}) collective-permute-start(bf16[1024,256]{1,0:T(8,128)(2,1)} %copy.65), channel_id=1, source_target_pairs={{0,4},{4,0},{8,12},{12,8},{16,20},{20,16},{24,28},{28,24},{1,5},{5... | collective-permute-start | bytes 1572872 | tf_op jit(solution)/shard_map/ppermute | solution.py:976
  195.3 29.5 %copy-start.9 = (bf16[2,2,256,512]{3,2,1,0:T(8,128)(2,1)S(1)}, bf16[2,2,256,512]{3,2,1,0:T(8,128)(2,1)}, u32[]{:S(2)}) copy-start(bf16[2,2,256,512]{3,2,1,0:T(8,128)(2,1)} %copy.61) | copy-start | bytes 3145732
  224.8 2.3 copy-start.44
  229.4 135.9 %reduce-scatter.7.cloned.1.call-start = ((), (), s32[]{:S(2)}) async-start(), calls=%async_computation.6 | async-start | bytes 5242880 | tf_op jit(solution)/shard_map/reduce_scatter | solution.py:1238
  229.7 10.7 %collective-permute-start.10 = (bf16[512,1536]{1,0:T(8,128)(2,1)}, bf16[512,1536]{1,0:T(8,128)(2,1)}, u32[]{:S(2)}, u32[]{:S(2)}) collective-permute-start(bf16[512,1536]{1,0:T(8,128)(2,1)} %collective-permute-done.7), channel_id=1, source_target_pairs={{0,1},{1,0},{2,3},{3,2},{4,5},{5,4},{6,7},{7,6},{8,9},{9,8},{10,11... | collective-permute-start | bytes 4718600 | tf_op jit(solution)/shard_map/ppermute | solution.py:968
  230.3 3.2 copy-start.20
  274.1 12.1 %copy-start.10 = (bf16[1,1024,512]{2,1,0:T(8,128)(2,1)S(1)}, bf16[1,1024,512]{2,1,0:T(8,128)(2,1)}, u32[]{:S(2)}) copy-start(bf16[1,1024,512]{2,1,0:T(8,128)(2,1)} %reduce-scatter.5.cloned.1.call-done) | copy-start | bytes 3145732
  288.6 32.0 %collective-permute-start.11 = (bf16[1024,512]{1,0:T(8,128)(2,1)}, bf16[1024,512]{1,0:T(8,128)(2,1)S(1)}, u32[]{:S(2)}, u32[]{:S(2)}) collective-permute-start(bf16[1024,512]{1,0:T(8,128)(2,1)} %multiply_convert_fusion.1.g_ref), channel_id=1, source_target_pairs={{0,4},{4,0},{8,12},{12,8},{16,20},{20,16},{24,28},{28,24},{1,5},{5... | collective-permute-start | bytes 3145736 | tf_op jit(solution)/shard_map/ppermute | solution.py:976
  320.6 1.0 copy-start.43
  321.6 342.4 %reduce-scatter.9.cloned.1.call-start = ((), (), s32[]{:S(2)}) async-start(), calls=%async_computation.7 | async-start | bytes 4423680 | tf_op jit(solution)/shard_map/reduce_scatter | solution.py:1204
  322.1 350.3 %reduce-scatter.11.cloned.1.call-start = ((), (), s32[]{:S(2)}) async-start(), calls=%async_computation.8 | async-start | bytes 11796480 | tf_op jit(solution)/shard_map/reduce_scatter | solution.py:1241
  365.2 0.7 copy-start.37
  365.2 0.7 copy-start.30
  365.2 0.8 copy-start.31
  365.2 3.3 copy-start.36
  365.2 3.4 copy-start.35
  365.2 3.4 copy-start.40
  365.2 3.4 copy-start.41
  365.2 5.8 copy-start.4
  365.3 6.1 copy-start.19
  365.3 6.1 copy-start.27
  369.2 71.3 %copy-start.34 = (f32[1,512]{1,0:T(1,128)}, f32[1,512]{1,0:T(1,128)S(1)}, u32[]{:S(2)}) copy-start(f32[1,512]{1,0:T(1,128)S(1)} %get-tuple-element.205) | copy-start | bytes 6148
  369.2 4.5 collective-permute-start.3
  371.2 15.8 %copy-start.32 = (f32[2048]{0:T(1024)S(1)}, f32[2048]{0:T(1024)}, u32[]{:S(2)}) copy-start(f32[2048]{0:T(1024)} %param.31) | copy-start | bytes 24580
  371.3 15.6 %copy-start.5 = (bf16[256,2048]{1,0:T(8,128)(2,1)S(1)}, bf16[256,2048]{1,0:T(8,128)(2,1)}, u32[]{:S(2)}) copy-start(bf16[256,2048]{1,0:T(8,128)(2,1)} %in_ref.1) | copy-start | bytes 3145732
  371.3 15.6 %copy-start.8 = (f32[256,2048]{1,0:T(8,128)S(1)}, f32[256,2048]{1,0:T(8,128)}, u32[]{:S(2)}) copy-start(f32[256,2048]{1,0:T(8,128)} %get-tuple-element.59) | copy-start | bytes 6291460
  373.5 82.2 %collective-permute-start.2 = (f32[256,512]{1,0:T(8,128)}, f32[256,512]{1,0:T(8,128)}, u32[]{:S(2)}, u32[]{:S(2)}) collective-permute-start(f32[256,512]{1,0:T(8,128)} %slice.304), channel_id=1, source_target_pairs={{0,2},{1,3},{2,0},{3,1},{4,6},{5,7},{6,4},{7,5},{8,10},{9,11},{10,... | collective-permute-start | bytes 1572872 | tf_op jit(solution)/shard_map/ppermute | solution.py:968
  404.9 3.7 copy-start.33
  406.2 2.4 copy-start.17
  406.2 2.4 copy-start.24
  408.6 1.7 copy-start.11
  429.2 11.3 %copy-start.21 = (f32[256,512]{1,0:T(8,128)S(1)}, f32[256,512]{1,0:T(8,128)}, u32[]{:S(2)}) copy-start(f32[256,512]{1,0:T(8,128)} %get-tuple-element.67) | copy-start | bytes 1572868
  455.0 3.2 copy-start.6
  464.2 3.2 copy-start.12
  464.2 3.2 copy-start.23
  472.9 3.5 copy-start.25
  660.6 4.8 copy-start.39
  660.7 5.4 copy-start.38
  666.6 2.5 copy-start.7
  669.1 2.1 copy-start.22
  671.1 5.5 copy-start.1
Sparse Core Ops, SparseCore 0:
  103.1 34.5 all-gather.1
  229.5 44.5 reduce-scatter.4
  320.7 43.6 reduce-scatter.6
  366.6 69.2 reduce-scatter.8
  438.0 209.6 reduce-scatter.10

commit v4 on v3

--- a/solution.py
+++ b/solution.py
@@ -152,44 +152,6 @@
         cost_estimate=cost(2 * rows * wide * outs * taps, outs * taps * wide * 2),
         name="heads_weight",
     )(g, u, shifts)
-
-
-def rows_forward_kernel(first_ref, u_ref, w_ref, s_ref, out_ref):
-    blocks, span = s_ref.shape[1], s_ref.shape[2]
-
-    @pl.when(pl.program_id(0) == 0)
-    def _():
-        out_ref[...] = jnp.zeros_like(out_ref)
-
-    y = product(u_ref[...], w_ref[...]).astype(BF16)
-    for k in range(blocks):
-        at = pl.ds(k * span, span)
-        out_ref[at, :] += product(s_ref[0, k], y[k * span : (k + 1) * span])
-
-
-def rows_forward(first, u, w, shifts, halves):
-    rows = u.shape[0]
-    depth = u.shape[1] // halves
-    outs = w.shape[1]
-    steps = w.shape[0] // depth
-    taps, blocks, span, _ = shifts.shape
-    return pl.pallas_call(
-        rows_forward_kernel,
-        grid_spec=pltpu.PrefetchScalarGridSpec(
-            num_scalar_prefetch=1,
-            grid=(steps,),
-            in_specs=[
-                pl.BlockSpec((rows, depth), lambda b, f: (0, (b + f[0]) % halves)),
-                pl.BlockSpec((depth, outs), lambda b, f: (b, 0)),
-                pl.BlockSpec((1, blocks, span, span), lambda b, f: ((b + f[0]) // halves, 0, 0, 0)),
-            ],
-            out_specs=pl.BlockSpec((rows, outs), lambda b, f: (0, 0)),
-        ),
-        out_shape=jax.ShapeDtypeStruct((rows, outs), F32),
-        compiler_params=params(),
-        cost_estimate=cost(2 * rows * w.size, w.size * 2),
-        name="rows_forward",
-    )(first, u, w, shifts)
 
 
 def rows_back_kernel(halves, first_ref, g_ref, u_ref, w_ref, s_ref, du_ref, dw_ref, total):
@@ -289,84 +251,6 @@
         cost_estimate=cost(2 * rows * wide * outs * taps, outs * taps * wide * 2),
         name="heads_split",
     )(x, g, h, u, v, s, r)
-
-
-def rows_split_kernel(first_ref, g_ref, h_ref, u_ref, v_ref, s_ref, r_ref, out_ref):
-    blocks, span = s_ref.shape[1], s_ref.shape[2]
-    total = 0.0
-    for a_ref, b_ref, m_ref in ((g_ref, u_ref, s_ref), (h_ref, v_ref, r_ref)):
-        taken = jnp.concatenate(
-            [
-                inner_rows(a_ref[k * span : (k + 1) * span, :], m_ref[0, k]).astype(BF16)
-                for k in range(blocks)
-            ],
-            1,
-        )
-        total = total + product(taken, b_ref[...])
-    out_ref[...] = total.astype(BF16)
-
-
-def rows_split(first, g, h, u, v, s, r, halves, steps):
-    rows, outs = g.shape
-    depth = u.shape[1] // halves
-    taps, blocks, span, _ = s.shape
-    side = pl.BlockSpec((rows, outs), lambda b, f: (0, 0))
-    values = pl.BlockSpec((rows, depth), lambda b, f: (0, (b + f[0]) % halves))
-    picks = pl.BlockSpec((1, blocks, span, span), lambda b, f: ((b + f[0]) // halves, 0, 0, 0))
-    return pl.pallas_call(
-        rows_split_kernel,
-        grid_spec=pltpu.PrefetchScalarGridSpec(
-            num_scalar_prefetch=1,
-            grid=(steps,),
-            in_specs=[side, side, values, values, picks, picks],
-            out_specs=pl.BlockSpec((outs, depth), lambda b, f: (0, b)),
-        ),
-        out_shape=jax.ShapeDtypeStruct((outs, steps * depth), BF16),
-        compiler_params=params(),
-        cost_estimate=cost(4 * rows * outs * steps * depth, outs * steps * depth * 2),
-        name="rows_split",
-    )(first, g, h, u, v, s, r)
-
-
-def rows_data_kernel(halves, first_ref, g_ref, w_ref, s_ref, du_ref, total):
-    step = pl.program_id(0)
-    depth = w_ref.shape[0]
-    which = (step + first_ref[0]) % halves
-
-    @pl.when(step == 0)
-    def _():
-        total[...] = jnp.zeros_like(total)
-
-    total[which] += against(shifted(g_ref, s_ref), w_ref[...])
-
-    @pl.when(step == pl.num_programs(0) - 1)
-    def _():
-        for k in range(halves):
-            du_ref[:, k * depth : (k + 1) * depth] = total[k].astype(du_ref.dtype)
-
-
-def rows_data(first, g, w, shifts, halves, depth):
-    rows, outs = g.shape
-    steps = w.shape[0] // depth
-    taps, blocks, span, _ = shifts.shape
-    return pl.pallas_call(
-        functools.partial(rows_data_kernel, halves),
-        grid_spec=pltpu.PrefetchScalarGridSpec(
-            num_scalar_prefetch=1,
-            grid=(steps,),
-            in_specs=[
-                pl.BlockSpec((rows, outs), lambda b, f: (0, 0)),
-                pl.BlockSpec((depth, outs), lambda b, f: (b, 0)),
-                pl.BlockSpec((1, blocks, span, span), lambda b, f: ((b + f[0]) // halves, 0, 0, 0)),
-            ],
-            out_specs=pl.BlockSpec((rows, halves * depth), lambda b, f: (0, 0)),
-            scratch_shapes=[pltpu.VMEM((halves, rows, depth), F32)],
-        ),
-        out_shape=jax.ShapeDtypeStruct((rows, halves * depth), BF16),
-        compiler_params=params(),
-        cost_estimate=cost(2 * rows * w.size, w.size * 2),
-        name="rows_data",
-    )(first, g, w, shifts)
 
 
 CHUNKS = 4
@@ -854,6 +738,523 @@
     )
 
 
+MOVES = 28
+
+
+def message_kernel(split, n_dp, classes, *refs):
+    refs = list(refs)
+
+    def take(count):
+        taken, refs[:count] = refs[:count], []
+        return taken
+
+    layout_ref, areas_ref, headed_ref, s_ref, w_hbm, gates_w_ref, classes_w_ref = take(7)
+    gain_ref, shift_ref, cot_ref, labels_ref = take(4)
+    depth_ref, logits_ref, gates_ref, classes_ref, low_ref, norm_ref = take(6)
+    if split:
+        (out_ref,) = take(1)
+    else:
+        heads_ref, gm_ref = take(2)
+    w_ref, live_ref, acc_ref, acc_in, stream_ref, direct_ref, cot_in, labels_in = take(8)
+    depth_out, logits_out, picked_ref, far_ref, near_ref = take(5)
+    core_out, core_in, far_out, far_in, near_out, near_in = take(6)
+    sums_ref, slots_ref, load_sem, send, recv, dp_send, dp_recv = take(7)
+    if split:
+        heads_ref, gm_ref, beside_ref, cut_own, cut_out, cut_in, cut_taken = take(7)
+
+    rep = lax.axis_index("rep")
+    par, upper = lax.rem(rep, 2), rep // 2
+    mate, far = rep + 1 - 2 * par, rep + 2 - 4 * upper
+    first_row = lax.axis_index("dp") * 4
+    side_x = lax.rem(lax.axis_index("dp"), 2)
+    beside = lax.axis_index("dp") + 1 - 2 * side_x
+    span = s_ref.shape[2]
+    middle = headed_ref.shape[2]
+    small = middle // 2
+    load = pltpu.make_async_copy(w_hbm, w_ref, load_sem)
+    load.start()
+
+    barrier = pltpu.get_barrier_semaphore()
+    me_dp = lax.axis_index("dp")
+    for to in (mate, far):
+        pl.semaphore_signal(barrier, inc=1, device_id={"rep": to}, device_id_type=MESH)
+    for k in range(1, n_dp):
+        pl.semaphore_signal(
+            barrier, inc=1, device_id={"dp": lax.rem(me_dp + k, n_dp)}, device_id_type=MESH
+        )
+
+    def move(number, src, dst, to, axis="rep"):
+        return send_to(axis, to, src, dst, send.at[number], recv.at[number])
+
+    def block(parity):
+        return pl.ds(pl.multiple_of(parity * span, span), span)
+
+    for p in range(4):
+        live_ref[p // 2, (p % 2) * span : (p % 2 + 1) * span, :] = live_column(
+            layout_ref, first_row + p, span
+        )
+    inverse = inverse_count(areas_ref, span)
+
+    def add_up(number, left, right):
+        sums_ref[number, 0:1, :] = left
+        sums_ref[number, 1:2, :] = right
+        return total_along(
+            "dp", n_dp, sums_ref.at[number], slots_ref.at[number], dp_send.at[number], dp_recv.at[number]
+        )
+
+    def column_sum(value):
+        return jnp.sum(value, 0, keepdims=True)
+
+    left, right = 0.0, 0.0
+    for side in range(2):
+        masked = live_ref[side] * headed_ref[side]
+        left = left + column_sum(masked)
+        right = right + column_sum(masked * headed_ref[side])
+    pl.semaphore_wait(barrier, n_dp + 1)
+    move(9, cot_ref, cot_in, far).start()
+    move(10, labels_ref, labels_in, far).start()
+    sums = add_up(0, left, right)
+    center = sums[0:1] * inverse
+    scaling = lax.rsqrt(sums[1:2] * inverse - center * center + EPS)
+    gain = gain_ref[pl.ds(rep, 1), :]
+    shift = shift_ref[pl.ds(rep, 1), :]
+
+    def across(head, part):
+        at = heads_ref.at[head, part // 2, pl.ds((part % 2) * span, span)]
+        return move(part, at, at, far)
+
+    def relay(head, part):
+        at = heads_ref.at[head, part // 2, pl.ds((part % 2) * span, span)]
+        return move(5 + part, at, at, mate)
+
+    def own_head(head):
+        return move(4, heads_ref.at[head], heads_ref.at[head], mate)
+
+    for side in range(2):
+        normed = (headed_ref[side] - center) * (scaling * gain) + shift
+        heads_ref[rep, side] = (normed * jax.nn.sigmoid(normed)).astype(BF16)
+        for k in range(2):
+            across(rep, 2 * side + k).start()
+    own_head(rep).start()
+    if split:
+        x_own = move(23, heads_ref.at[rep], beside_ref.at[rep], beside, "dp")
+        x_far = move(24, heads_ref.at[far], beside_ref.at[far], beside, "dp")
+        x_own.start()
+
+    def tap_of(i):
+        return par * 5 + i
+
+    def row_of(i, head_at):
+        return pl.multiple_of(par * (3 * small) + i * (3 * middle) + head_at * middle, small)
+
+    half_row = (1 - par) * (12 * middle)
+    full_row = pl.multiple_of(half_row + par * small, small)
+    part_row = pl.multiple_of(half_row + (1 - par) * middle, small)
+    part_lanes = pl.ds(pl.multiple_of(par * small, small), small)
+    local = 2 * upper
+    remote = 2 * (1 - upper)
+    local_head = 1 + upper
+    part_head = 2 - upper
+    full_head = 2 * par + 1 - upper
+
+    def wrows(row, depth):
+        return w_ref[pl.ds(row, depth), :]
+
+    def gather_taps(tap, side, y):
+        y = y.astype(BF16)
+        for k in range(2):
+            acc_ref[side, k * span : (k + 1) * span, :] += product(
+                s_ref[tap, 2 * side + k], y[k * span : (k + 1) * span]
+            )
+
+    acc_ref[...] = jnp.zeros_like(acc_ref)
+    own_head(mate).wait_recv()
+    load.wait()
+
+    @pl.loop(0, 8)
+    def _(n):
+        i, side = n // 2, n % 2
+        gather_taps(
+            tap_of(i), side, product(heads_ref[local_head, side], wrows(row_of(i, local), middle))
+        )
+
+    @pl.when(par == upper)
+    def _():
+        @pl.loop(0, 2)
+        def _(side):
+            gather_taps(4, side, product(heads_ref[full_head, side], wrows(full_row, middle)))
+
+    for part in range(4):
+        across(far, part).wait_recv()
+        relay(far, part).start()
+    if split:
+        x_far.start()
+    for part in range(4):
+        relay(far + 1 - 2 * par, part).wait_recv()
+
+    @pl.loop(0, 8)
+    def _(n):
+        i, side = n // 2, n % 2
+        y = product(heads_ref[remote, side], wrows(row_of(i, 1 - upper), middle))
+        y = y + product(heads_ref[remote + 1, side], wrows(row_of(i, 2 - upper), middle))
+        gather_taps(tap_of(i), side, y)
+
+    @pl.loop(0, 2)
+    def _(side):
+        gather_taps(
+            4, side, product(heads_ref[part_head, side, :, part_lanes], wrows(part_row, small))
+        )
+
+    @pl.when(par != upper)
+    def _():
+        @pl.loop(0, 2)
+        def _(side):
+            gather_taps(4, side, product(heads_ref[full_head, side], wrows(full_row, middle)))
+
+    def acc_move(side):
+        return move(11 + side, acc_ref.at[side, block(1 - par)], acc_in.at[side], mate)
+
+    for side in range(2):
+        acc_move(side).start()
+
+    own_gates = gates_w_ref[pl.ds(pl.multiple_of(upper * middle, middle), middle), :]
+    classes_ref[...] = jnp.zeros_like(classes_ref)
+    move(9, cot_ref, cot_in, far).wait_recv()
+    move(10, labels_ref, labels_in, far).wait_recv()
+    gates_total = 0.0
+
+    def gm_move(side, parity):
+        at = gm_ref.at[side, block(parity)]
+        return move(13 + side, at, at, mate)
+
+    for side in range(2):
+        acc_move(side).wait_recv()
+        message = acc_ref[side, block(par), :] + acc_in[side]
+        stream = heads_ref[3 * upper, side, block(par), :]
+        gate = jax.nn.sigmoid(product(stream, own_gates))
+        full = stream.astype(F32) + gate * message
+        alive = live_ref[side, block(par), :]
+
+        @pl.when(upper == 0)
+        def _():
+            cot = (cot_ref if side == 0 else cot_in)[...].astype(F32)
+            stream_ref[side] = alive * cot
+            (depth_ref if side == 0 else depth_out)[...] = alive * full
+
+        @pl.when(upper == 1)
+        def _():
+            labels = (labels_in if side == 0 else labels_ref)[...]
+            full_low = full.astype(BF16)
+            logits = product(full_low, classes_w_ref[...])
+            (logits_out if side == 0 else logits_ref)[...] = alive * logits
+            lanes = lax.broadcasted_iota(jnp.int32, logits.shape, 1)
+            shown = jnp.where(lanes < classes, logits, -1e30)
+            grown = jnp.exp(shown - jnp.max(shown, 1, keepdims=True))
+            probs = grown / jnp.sum(grown, 1, keepdims=True)
+            slope = (alive * (probs - jnp.where(lanes == labels, 1.0, 0.0))).astype(BF16)
+            classes_ref[...] += inner_rows(full_low, slope)
+            stream_ref[side] = against(slope, classes_w_ref[...])
+
+        grad = stream_ref[side]
+        grad_gate = (grad * message * gate * (1.0 - gate)).astype(BF16)
+        gm_ref[side, block(par), :] = (grad * gate).astype(BF16)
+        gm_move(side, par).start()
+        gates_total = gates_total + inner_rows(stream, grad_gate)
+        direct_ref[side] = grad + against(grad_gate, own_gates)
+
+    gates_ref[...] = gates_total.astype(BF16)
+
+    @pl.when(upper == 0)
+    def _():
+        move(15, depth_out, depth_ref, far).start()
+
+    @pl.when(upper == 1)
+    def _():
+        move(16, logits_out, logits_ref, far).start()
+
+    for side in range(2):
+        gm_move(side, 1 - par).wait_recv()
+    if split:
+        lanes = lax.broadcasted_iota(jnp.int32, (middle, small), 1)
+        wanted = (lanes // 64) * 128 + lanes % 64
+        source = lax.broadcasted_iota(jnp.int32, (middle, small), 0)
+        for cut, which in ((cut_out, 1 - side_x), (cut_own, side_x)):
+            pick = jnp.where(source == wanted + 64 * which, 1.0, 0.0).astype(BF16)
+            for side in range(2):
+                cut[side] = product(gm_ref[side], pick).astype(BF16)
+        x_cut = move(27, cut_out, cut_in, beside, "dp")
+        x_cut.start()
+
+    @pl.loop(0, 10)
+    def _(n):
+        i, side = n // 2, n % 2
+        tap = jnp.where(i == 4, 4, tap_of(i))
+        for k in range(2):
+            at = pl.ds(k * span, span)
+            picked_ref[i, side, at, :] = inner_rows(
+                s_ref[tap, 2 * side + k], gm_ref[side, at, :]
+            ).astype(BF16)
+
+    far_ref[...] = jnp.zeros_like(far_ref)
+    near_ref[...] = jnp.zeros_like(near_ref)
+
+    @pl.loop(0, 8)
+    def _(n):
+        i, side = n // 2, n % 2
+        for j in range(2):
+            far_ref[j, side] += against(
+                picked_ref[i, side], wrows(row_of(i, 1 - upper + j), middle)
+            )
+
+    @pl.loop(0, 2)
+    def _(side):
+        far_ref[upper, side, :, part_lanes] += against(picked_ref[4, side], wrows(part_row, small))
+
+    @pl.when(par != upper)
+    def _():
+        @pl.loop(0, 2)
+        def _(side):
+            far_ref[2 * par - 1 + upper, side] += against(
+                picked_ref[4, side], wrows(full_row, middle)
+            )
+
+    core_out[...] = far_ref[1 - par].astype(BF16)
+    to_mate = move(17, core_out, core_in, mate)
+    to_mate.start()
+
+    def far_move(part):
+        at = pl.ds((part % 2) * span, span)
+        return move(18 + part, far_out.at[part // 2, at], far_in.at[part // 2, at], far)
+
+    @pl.loop(0, 8)
+    def _(n):
+        i, side = n // 2, n % 2
+        near_ref[side] += against(picked_ref[i, side], wrows(row_of(i, local), middle))
+
+    to_mate.wait_recv()
+    for part in range(4):
+        at = pl.ds((part % 2) * span, span)
+        far_out[part // 2, at, :] = (
+            far_ref[par, part // 2, at, :] + core_in[part // 2, at, :].astype(F32)
+        ).astype(BF16)
+        far_move(part).start()
+
+    @pl.when(par == upper)
+    def _():
+        @pl.loop(0, 2)
+        def _(side):
+            near_ref[side] += against(picked_ref[4, side], wrows(full_row, middle))
+
+        near_out[...] = near_ref[...].astype(BF16)
+        for side in range(2):
+            near_ref[side, block(par), :] = direct_ref[side]
+            near_ref[side, block(1 - par), :] = jnp.zeros((span, middle), F32)
+
+    @pl.when(par != upper)
+    def _():
+        for side in range(2):
+            near_out[side, block(par), :] = direct_ref[side].astype(BF16)
+            near_out[side, block(1 - par), :] = jnp.zeros((span, middle), BF16)
+
+    near_move = move(22, near_out, near_in, mate)
+    near_move.start()
+
+    if split:
+        x_own.wait_recv()
+        relay_own = move(25, beside_ref.at[rep], beside_ref.at[rep], mate)
+        relay_own.start()
+        x_far.wait_recv()
+        relay_far = move(26, beside_ref.at[far], beside_ref.at[far], mate)
+        relay_far.start()
+        x_cut.wait_recv()
+        move(25, beside_ref.at[mate], beside_ref.at[mate], mate).wait_recv()
+        other = far + 1 - 2 * par
+        move(26, beside_ref.at[other], beside_ref.at[other], mate).wait_recv()
+
+        def fill(tap):
+            for p in range(4):
+                at = pl.ds(p * span, span)
+                cut_taken[0, :, at] = inner_rows(
+                    cut_own[p // 2, pl.ds((p % 2) * span, span), :], s_ref[tap, p]
+                ).astype(BF16)
+                cut_taken[1, :, at] = inner_rows(
+                    cut_in[p // 2, pl.ds((p % 2) * span, span), :],
+                    shift_block(layout_ref, beside * 4 + p, 1, tap, span),
+                ).astype(BF16)
+
+        def gradient(head, lanes):
+            total = 0.0
+            for number, held in enumerate((heads_ref, beside_ref)):
+                for side in range(2):
+                    total = total + product(
+                        cut_taken[number, :, side * 2 * span : (side + 1) * 2 * span],
+                        held[head, side, :, lanes],
+                    )
+            return total.astype(BF16)
+
+        @pl.loop(0, 4)
+        def _(i):
+            fill(tap_of(i))
+            for at in range(3):
+                for k in range(2):
+                    row = pl.multiple_of(row_of(i, at) + k * small, small)
+                    out_ref[:, pl.ds(row, small)] = gradient(
+                        at + 1 - upper, pl.ds(k * small, small)
+                    )
+
+        fill(4)
+        for k in range(2):
+            row = pl.multiple_of(full_row + k * small, small)
+            out_ref[:, pl.ds(row, small)] = gradient(full_head, pl.ds(k * small, small))
+        out_ref[:, pl.ds(part_row, small)] = gradient(part_head, part_lanes)
+
+    near_move.wait_recv()
+    left, right = 0.0, 0.0
+
+    def backward(side):
+        unit = (headed_ref[side] - center) * scaling
+        normed = unit * gain + shift
+        sigma = jax.nn.sigmoid(normed)
+        return unit, sigma * (1.0 + normed * (1.0 - sigma))
+
+    for side in range(2):
+        for part in (2 * side, 2 * side + 1):
+            far_move(part).wait_recv()
+        unit, slope = backward(side)
+        grad = near_ref[side] + near_in[side].astype(F32) + far_in[side].astype(F32)
+        grad = grad * slope
+        near_ref[side] = grad
+        masked = live_ref[side] * grad
+        left = left + column_sum(masked * unit)
+        right = right + column_sum(masked)
+    sums = add_up(1, left, right)
+    norm_ref[...] = sums
+    for side in range(2):
+        unit = (headed_ref[side] - center) * scaling
+        low_ref[side] = (
+            live_ref[side]
+            * (gain * scaling)
+            * (near_ref[side] - sums[1:2] * inverse - unit * (sums[0:1] * inverse))
+        ).astype(BF16)
+
+    for part in range(4):
+        across(rep, part).wait_send()
+        relay(far, part).wait_send()
+        far_move(part).wait_send()
+    own_head(rep).wait_send()
+    move(9, cot_ref, cot_in, far).wait_send()
+    move(10, labels_ref, labels_in, far).wait_send()
+    for side in range(2):
+        acc_move(side).wait_send()
+        gm_move(side, par).wait_send()
+    to_mate.wait_send()
+    near_move.wait_send()
+
+    @pl.when(upper == 0)
+    def _():
+        move(15, depth_out, depth_ref, far).wait_send()
+        move(16, logits_out, logits_ref, far).wait_recv()
+
+    @pl.when(upper == 1)
+    def _():
+        move(16, logits_out, logits_ref, far).wait_send()
+        move(15, depth_out, depth_ref, far).wait_recv()
+
+    if split:
+        for copy in (x_own, x_far, x_cut, relay_own, relay_far):
+            copy.wait_send()
+
+
+def message_streams(
+    split, layout, headed, shifts, w_messages, w_gates, w_classes, gain, shift, cot, labels
+):
+    n_dp = lax.axis_size("dp")
+    span, middle = cot.shape
+    small = middle // 2
+    classes = w_classes.shape[1]
+    vmem = pl.BlockSpec(memory_space=pltpu.VMEM)
+    dma = pltpu.SemaphoreType.DMA
+    shape = jax.ShapeDtypeStruct
+    halves = (2, 2 * span, middle)
+    heads = (4, 2, 2 * span, middle)
+    out_shape = [
+        shape((span, middle), F32),
+        shape((span, 128), F32),
+        shape((middle, middle), BF16),
+        shape((middle, 128), F32),
+        shape(halves, BF16),
+        shape((2, middle), F32),
+    ]
+    if split:
+        out_shape += [shape((small, w_messages.shape[0]), BF16)]
+    else:
+        out_shape += [shape(heads, BF16), shape(halves, BF16)]
+    scratch = [
+        pltpu.VMEM(w_messages.shape, BF16),
+        pltpu.VMEM((2, 2 * span, 1), F32),
+        pltpu.VMEM(halves, F32),
+        pltpu.VMEM((2, span, middle), F32),
+        pltpu.VMEM((2, span, middle), F32),
+        pltpu.VMEM((2, span, middle), F32),
+        pltpu.VMEM((span, middle), BF16),
+        pltpu.VMEM((span, 128), jnp.int32),
+        pltpu.VMEM((span, middle), F32),
+        pltpu.VMEM((span, 128), F32),
+        pltpu.VMEM((5,) + halves, BF16),
+        pltpu.VMEM((2,) + halves, F32),
+        pltpu.VMEM(halves, F32),
+        pltpu.VMEM(halves, BF16),
+        pltpu.VMEM(halves, BF16),
+        pltpu.VMEM(halves, BF16),
+        pltpu.VMEM(halves, BF16),
+        pltpu.VMEM(halves, BF16),
+        pltpu.VMEM(halves, BF16),
+        pltpu.VMEM((2, 2, middle), F32),
+        pltpu.VMEM((2, n_dp, 2, middle), F32),
+        dma,
+        dma((MOVES,)),
+        dma((MOVES,)),
+        dma((2, n_dp)),
+        dma((2, n_dp)),
+    ]
+    if split:
+        scratch += [
+            pltpu.VMEM(heads, BF16),
+            pltpu.VMEM(halves, BF16),
+            pltpu.VMEM(heads, BF16),
+            pltpu.VMEM((2, 2 * span, small), BF16),
+            pltpu.VMEM((2, 2 * span, small), BF16),
+            pltpu.VMEM((2, 2 * span, small), BF16),
+            pltpu.VMEM((2, small, 4 * span), BF16),
+        ]
+    return pl.pallas_call(
+        functools.partial(message_kernel, split, n_dp, classes),
+        in_specs=[pl.BlockSpec(memory_space=pltpu.SMEM)]
+        + [vmem] * 3
+        + [pl.BlockSpec(memory_space=pl.ANY)]
+        + [vmem] * 6,
+        out_specs=[vmem] * len(out_shape),
+        out_shape=out_shape,
+        scratch_shapes=scratch,
+        compiler_params=pltpu.CompilerParams(
+            collective_id=11, has_side_effects=True, vmem_limit_bytes=VMEM_LIMIT
+        ),
+        name="message_streams",
+    )(
+        layout,
+        layout,
+        headed,
+        shifts,
+        w_messages,
+        w_gates,
+        jnp.pad(w_classes, ((0, 0), (0, 128 - classes))),
+        gain.reshape(4, middle),
+        shift.reshape(4, middle),
+        cot,
+        jnp.broadcast_to(labels[:, None], (span, 128)),
+    )
+
+
 def silu_slope(value_in):
     sigma_of = jax.nn.sigmoid(value_in)
     return sigma_of * (1.0 + value_in * (1.0 - sigma_of))
@@ -1071,7 +1472,6 @@
     )
     shifts_own = shifts_own[:, None]
     trunk_all = trunk_all.reshape(group * pixels, -1)
-    headed = headed.reshape(group * pixels, middle)
     normed_one, unit_one, scale_one = normalize(
         reduced, sums_one[0], sums_one[1], pixel_count, gain_mid[0], shift_mid[0]
     )
@@ -1085,137 +1485,47 @@
     if split:
         trunk_mine = swap_x(own_half(trunk_all, parity))
 
-    own_gain = lax.dynamic_slice_in_dim(gain_head, rep * middle, middle, 0)
-    own_shift = lax.dynamic_slice_in_dim(shift_head, rep * middle, middle, 0)
-    sums_head, squares_head = moments(headed, living_all, ("dp",))
-    normed_head, unit_head, scale_head = normalize(
-        headed, sums_head, squares_head, pixel_count, own_gain, own_shift
-    )
-    rounded = jax.nn.silu(normed_head).astype(BF16)
-    heads_all = lax.all_gather(rounded, "rep", axis=0, tiled=False)
-
-    is_depth = upper == 0
-    source = jnp.where(
-        is_depth,
-        jnp.concatenate([heads_all[1], heads_all[2], heads_all[3]], 1),
-        jnp.concatenate([heads_all[0], heads_all[1], heads_all[2]], 1),
-    )
+    upper_is_depth = upper == 0
+    depth, logits, gates_local, classes_local, head_low, head_norm, *rest = message_streams(
+        split,
+        layout,
+        headed,
+        shifts_all,
+        w_messages,
+        w_gates,
+        w_classes,
+        gain_head,
+        shift_head,
+        cot_depth,
+        labels,
+    )
+    logits = logits[:, :classes]
+    classes_local = classes_local[:, :classes]
+    head_low = head_low.reshape(group * pixels, middle)
+    is_depth = upper_is_depth
     if split:
-        source_mine = swap_x(own_half(source, parity))
-    partial = rows_forward(first, source, w_messages, shifts_all, 2).reshape(
-        2, 2, pixels, middle
-    )
-
-    if split:
-        partial, trunk_mine = lax.optimization_barrier((partial, trunk_mine))
-        trunk_other = swap(trunk_mine, 1)
-
-    def of_parity(value, which):
-        return lax.dynamic_index_in_dim(value, which, 1, keepdims=False)
-
-    def rows_of(value):
-        return value.reshape(2 * pixels, value.shape[-1])
-
-    message = rows_of(of_parity(partial, parity) + swap(of_parity(partial, 1 - parity), 1))
-    stream = rows_of(
-        of_parity(
-            jnp.where(is_depth, heads_all[0], heads_all[3]).reshape(2, 2, pixels, middle), parity
-        )
-    )
-    own_gates = lax.dynamic_slice_in_dim(w_gates, upper * middle, middle, 0)
-    stream_living = rows_of(of_parity(group_living.reshape(2, 2, pixels, 1), parity))
-    cot_other = swap(cot_depth, 2)
-    labels_other = swap(labels, 2)
-    stream_cot = jnp.concatenate([cot_depth, cot_other], 0).astype(F32)
-    stream_labels = jnp.concatenate([labels_other, labels], 0)
-    gate = jax.nn.sigmoid(product(stream, own_gates))
-    full = stream.astype(F32) + gate * message
-    full_low = full.astype(BF16)
-    logits_full = product(full_low, w_classes)
-    probs = jax.nn.softmax(logits_full, axis=1)
-    onehot_table = (
-        stream_labels[:, None] == jnp.arange(classes, dtype=jnp.int32)[None, :]
-    ).astype(F32)
-    grad_logits = (stream_living * (probs - onehot_table)).astype(BF16)
-    classes_local = inner_rows(full_low, jnp.where(is_depth, 0.0, 1.0).astype(BF16) * grad_logits)
-    grad_stream = jnp.where(
-        is_depth, stream_living * stream_cot, against(grad_logits, w_classes)
-    )
-    depth_other = swap(full[pixels:], 2)
-    logits_other = swap(logits_full[:pixels], 2)
-    depth = living * jnp.where(is_depth, full[:pixels], depth_other)
-    logits = living * jnp.where(is_depth, logits_other, logits_full[pixels:])
-    grad_gate = (grad_stream * message * gate * (1.0 - gate)).astype(BF16)
-    grad_message = (grad_stream * gate).astype(BF16)
-    gates_local = inner_rows(stream, grad_gate).astype(BF16)
-    gates_local = gates_local.reshape(2, pixels, middle)
-    if not split:
-        gates_share = lax.dynamic_index_in_dim(gates_local, parity, 0, keepdims=False).astype(F32)
+        head_low, trunk_mine = lax.optimization_barrier((head_low, trunk_mine))
+        trunk_beside = both_halves(trunk_mine, swap(trunk_mine, 1), parity)
+        grad_messages = lax.psum_scatter(
+            rest[0], "dp", scatter_dimension=0, tiled=True, axis_index_groups=columns
+        )
+    else:
+        heads_all, message_all = rest
+        heads_all = heads_all.reshape(4, group * pixels, middle)
+        source = jnp.where(
+            is_depth,
+            jnp.concatenate([heads_all[1], heads_all[2], heads_all[3]], 1),
+            jnp.concatenate([heads_all[0], heads_all[1], heads_all[2]], 1),
+        )
+        _, messages_local = rows_back(
+            first, message_all.reshape(4 * pixels, middle), source, w_messages, shifts_all, 2, BF16
+        )
+        grad_messages = lax.psum_scatter(messages_local, "dp", scatter_dimension=1, tiled=True)
+        gates_cut = gates_local.reshape(2, pixels, middle)
+        gates_share = lax.dynamic_index_in_dim(gates_cut, parity, 0, keepdims=False).astype(F32)
         gates_share += swap(
-            lax.dynamic_index_in_dim(gates_local, 1 - parity, 0, keepdims=False), 1
+            lax.dynamic_index_in_dim(gates_cut, 1 - parity, 0, keepdims=False), 1
         ).astype(F32)
-    direct = (grad_stream + against(grad_gate, own_gates)).astype(BF16)
-
-    def both_parities(value, other):
-        value = value.reshape(2, pixels, middle)
-        other = other.reshape(2, pixels, middle)
-        even = jnp.where(parity == 0, value, other)
-        odd = jnp.where(parity == 0, other, value)
-        return jnp.stack([even, odd], 1).reshape(4 * pixels, middle)
-
-    message_all = both_parities(grad_message, swap(grad_message, 1))
-    direct_all = both_parities(direct, jnp.zeros_like(direct))
-    if split:
-        message_cut = message_all.reshape(4 * pixels, 4, 2, middle // 8)
-        cut_own = lax.dynamic_index_in_dim(message_cut, side, 2, keepdims=False)
-        cut_sent = lax.dynamic_index_in_dim(message_cut, 1 - side, 2, keepdims=False)
-        cut_own = cut_own.reshape(4 * pixels, middle // 2)
-        cut_beside = swap_x(cut_sent.reshape(4 * pixels, middle // 2))
-        source_grad = rows_data(
-            first, message_all, w_messages, shifts_all, 2, source.shape[1] // 2
-        )
-        source_grad, source_mine, cut_beside, trunk_other = lax.optimization_barrier(
-            (source_grad, source_mine, cut_beside, trunk_other)
-        )
-        source_beside = both_halves(source_mine, swap(source_mine, 1), parity)
-        trunk_beside = both_halves(trunk_mine, trunk_other, parity)
-    else:
-        source_grad, messages_local = rows_back(
-            first, message_all, source, w_messages, shifts_all, 2, BF16
-        )
-    thirds = [source_grad[:, k * middle : (k + 1) * middle] for k in range(3)]
-    by_head = jnp.stack(
-        [
-            jnp.where(is_depth, direct_all, thirds[0]),
-            jnp.where(is_depth, thirds[0], thirds[1]),
-            jnp.where(is_depth, thirds[1], thirds[2]),
-            jnp.where(is_depth, thirds[2], direct_all),
-        ],
-        0,
-    )
-    feat_grad = lax.psum_scatter(by_head, "rep", scatter_dimension=0, tiled=False)
-    if split:
-        messages_local = rows_split(
-            first, cut_own, cut_beside, source, source_beside, shifts_all, shifts_beside, 2, 9
-        )
-        feat_grad, messages_local, trunk_beside = lax.optimization_barrier(
-            (feat_grad, messages_local, trunk_beside)
-        )
-        grad_messages = lax.psum_scatter(
-            messages_local, "dp", scatter_dimension=0, tiled=True, axis_index_groups=columns
-        )
-    else:
-        grad_messages = lax.psum_scatter(messages_local, "dp", scatter_dimension=1, tiled=True)
-    head_raw, gain_grad_head, shift_grad_head = norm_back(
-        feat_grad.astype(F32) * silu_slope(normed_head),
-        unit_head,
-        scale_head,
-        own_gain,
-        living_all,
-        pixel_count,
-        ("dp",),
-    )
-    head_low = head_raw.astype(BF16)
     if split:
         head_beside = swap_x(head_low)
         trunk_part = heads_data(head_low, w_heads, shifts_all)
@@ -1287,6 +1597,7 @@
                 [value[:, :, k : k + middle] for k in range(0, value.shape[2], middle)], 1
             )
 
+        gates_local = gates_local.reshape(2, pixels, middle)
         gates_zero = jnp.zeros_like(gates_local)
         gates_every = jnp.where(
             is_depth,
@@ -1341,7 +1652,7 @@
     grad_gain_mid = jnp.stack([gain_grad_one, gain_grad_two], 0)
     grad_shift_mid = jnp.stack([shift_grad_one, shift_grad_two], 0)
     head_norms = lax.all_gather(
-        jnp.stack([gain_grad_head, shift_grad_head], 0), "rep", axis=1, tiled=True
+        head_norm, "rep", axis=1, tiled=True
     )
     return (
         depth,

time: 694 us -> 625 us (0.901)
  Pallas kernels: 448 us -> 510 us
  waiting for transfers between devices: 55.3 us -> 1.11 us
  other arithmetic: 74.3 us -> 36.8 us
  local copies, waits for them, and re-layouts: 55.3 us -> 34.8 us
  starting transfers between devices: 10.3 us -> 2.72 us
    pallas_call x3 -> x1, Pallas kernels: 54.1 us -> 133 us  [message_streams(): pl.pallas_call(functools.partial(message_kernel, split, n_dp, classes), i...]
    all_gather x1 -> x0, waiting for transfers between devices: 29.5 us -> none  [shards(): heads_all = lax.all_gather(rounded, 'rep', axis=0, tiled=False)]
    pallas_call x5 -> x3, Pallas kernels: 56.7 us -> 38.8 us  [total_of(): pl.pallas_call(functools.partial(total_kernel, sized), out_shape=jax.Shap...]
    ppermute x4 -> x2, waiting for transfers between devices: 13.5 us -> 0.01 us  [swap_x(): lax.ppermute(value, 'dp', [(k, k ^ 1) for k in range(lax.axis_size('dp'))])]
    reduce_scatter x2 -> x1, waiting for transfers between devices: 8.02 us -> 0.01 us  [shards(): lax.psum_scatter(rest[0], 'dp', scatter_dimension=0, tiled=True, axis_ind...]
    unnamed x103 -> x83, local copies, waits for them, and re-layouts: 16 us -> 13.8 us
  transfers between devices with their start and end apart: 17 -> 6, of which waited for: 6 -> 1; matrix products, arithmetic and copies ran while one was open for 16% -> 11% of each run, Pallas kernels for 52% -> 71%
where the time goes in v4:
time: 625 us; the launch traced here: 615 us
  Pallas kernels  510 us (82%)
  other arithmetic  36.8 us (6%)
  local copies, waits for them, and re-layouts  34.8 us (6%)
  between operations  17.1 us (3%)
  matrix products  7.76 us (1%)
    pallas_call x1, Pallas kernels, small_total(): pl.pallas_call(small_kernel, out_shape=jax.ShapeDtypeStruct((rows, lanes)...  180 us
    pallas_call x1, Pallas kernels, message_streams(): pl.pallas_call(functools.partial(message_kernel, split, n_dp, classes), i...  133 us
    pallas_call x1, Pallas kernels, trunk_forward(): pl.pallas_call(functools.partial(trunk_kernel, (n_rep, n_dp)), in_specs=[...  74.9 us
    pallas_call x1, Pallas kernels, heads_split(): pl.pallas_call(functools.partial(heads_split_kernel, per_tap, units, lane...  41.4 us
    pallas_call x3, Pallas kernels, total_of(): pl.pallas_call(functools.partial(total_kernel, sized), out_shape=jax.Shap...  38.8 us
    pallas_call x1, Pallas kernels, heads_data(): pl.pallas_call(heads_data_kernel, grid=(taps,), in_specs=[pl.BlockSpec((r...  30.3 us
    unnamed x83, local copies, waits for them, and re-layouts  13.8 us
  transfers between devices with their start and end apart: 6, of which 1 were waited for; matrix products, arithmetic and copies ran while one was open for 11% of the time, Pallas kernels for 71%

profile of v4, /device:TPU:28, one launch (start us, length us, event | category | flops | bytes accessed | tf_op | source)
XLA Modules:
  0.0 615.4 jit_solution(8213700837506998435)
XLA Ops:
  7.2 1.4 copy.44.layout_ref.areas_ref.refs_0_.refs_1_
  8.6 74.9 %trunk_forward.1 = (f32[256,512]{1,0:T(8,128)}, f32[2,512]{1,0:T(2,128)}, bf16[256,512]{1,0:T(8,128)(2,1)}, f32[256,512]{1,0:T(8,128)}, f32[2,512]{1,0:T(2,128)}...) custom-call(bf16[256,2048]{1,0:T(8,128)(2,1)} %in_ref.1, ...), custom_call_target="tpu_custom_call" | custom-call | tf_op jit(solution)/shard_map/trunk_forward/pallas_call | solution.py:686
  83.6 1.7 dynamic-slice_bitcast_fusion
  85.3 1.8 collective-permute-start
  87.2 0.6 reshape.145.refs_7_
  87.8 0.6 reshape.146.refs_8_
  88.5 0.7 pad.9.refs_6_
  89.2 0.8 broadcast_in_dim.22.refs_10_
  90.0 133.1 %message_streams.1 = (f32[256,512]{1,0:T(8,128)}, f32[256,128]{1,0:T(8,128)}, bf16[512,512]{1,0:T(8,128)(2,1)}, f32[512,128]{1,0:T(8,128)}, bf16[2,512,512]{2,1,...) custom-call(s32[32,3]{1,0:T(8,128)} %copy.44.layout_ref.areas_ref.refs_0_.refs_1_, ...), custom_call_target="tpu_custom_call" | custom-call | tf_op jit(solution)/shard_map/message_streams/pallas_call | solution.py:1230
  223.1 0.7 collective-permute-start.1
  223.8 30.3 %heads_data.1 = bf16[1024,2048]{1,0:T(8,128)(2,1)} custom-call(bf16[1024,512]{1,0:T(8,128)(2,1)} %bitcast.156, bf16[512,18432]{1,0:T(8,128)(2,1)} %w_ref.2, bf16[9,4,256,256]{3,2,1,0:T(8,128)(2,1)} %get-tuple-element.46.refs_3_.s_ref), custom_call_target="tpu_custom_call" | custom-call | flops 19327352832 | bytes 18874368 | tf_op jit(solution)/shard_map/heads_data/pallas_call | solution.py:113
  254.2 0.9 copy-done.33
  255.2 0.7 reduce-scatter.6.cloned.1.call-update
  256.7 3.4 fusion.r_ref
  260.4 2.2 broadcast_select_fusion.1
  262.5 2.7 pad_maximum_fusion.v_ref
  265.3 41.4 %heads_split.1 = bf16[4,512,2304]{2,1,0:T(8,128)(2,1)} custom-call(s32[1]{0:T(128)} %bitcast.4.x_ref, bf16[1024,512]{1,0:T(8,128)(2,1)} %bitcast.157, bf16[1024,512]{1,0:T(8,128)(2,1)} %copy-done.33, bf16[1024,2048]{1,0:T(8,128)(2,1)} %bitcast.117, bf16[1024,2048]{1,0:T(8,128)(2,1)} %pad_maximum_fusion.v_ref, ...), custom_call_target="tpu_custom_call" | custom-call | flops 19327352832 | bytes 18874368 | tf_op jit(solution)/shard_map/heads_split/pallas_call | solution.py:240
  306.9 0.6 minimum_reduce_fusion
  308.2 0.7 copy.51
  311.5 5.2 all_gather.3
  316.7 0.6 slice_multiply_fusion.1
  317.4 0.6 fusion.19
  318.0 3.3 multiply_reduce_fusion
  321.3 0.6 pad_maximum_fusion.5.x_ref
  321.9 15.2 %total.3 = f32[32,128]{1,0:T(8,128)} custom-call(f32[32,128]{1,0:T(8,128)} %pad_maximum_fusion.5.x_ref), custom_call_target="tpu_custom_call" | custom-call | tf_op jit(solution)/shard_map/total/pallas_call | solution.py:1330
  337.1 0.7 slice_bitcast_fusion.4
  337.8 1.3 broadcast_divide_fusion
  339.1 2.4 multiply_convert_fusion
  341.6 1.7 multiply_reduce_fusion.3
  343.9 12.9 %total.4 = f32[8,128]{1,0:T(8,128)} custom-call(f32[8,128]{1,0:T(8,128)} %pad_maximum_fusion.6.x_ref), custom_call_target="tpu_custom_call" | custom-call | tf_op jit(solution)/shard_map/total/pallas_call | solution.py:1330
  356.8 1.4 fusion.21
  358.2 2.1 multiply_convert_fusion.2.g_ref
  360.3 11.3 %rows_back.1 = (f32[256,512]{1,0:T(8,128)}, bf16[4608,512]{1,0:T(8,128)(2,1)}) custom-call(s32[1]{0:T(128)} %constant.85.clone.1.first_ref, bf16[256,512]{1,0:T(8,128)(2,1)} %multiply_convert_fusion.2.g_ref, bf16[256,512]{1,0:T(8,128)(2,1)} %get-tuple-element.61.u_ref, bf16[4608,512]{1,0:T(8,128)(2,1)} %w_ref.3, bf16[9,1,256,256]{3,2,1,0:T(8,128)(2,1)} %bitcast.154), custom_call_target="tpu_custom_call" | custom-call | flops 2415919104 | bytes 9437184 | tf_op jit(solution)/shard_map/rows_back/pallas_call | solution.py:181
  371.5 2.1 multiply_reduce_fusion.2
  373.7 0.6 pad_maximum_fusion.7.x_ref
  374.3 10.7 %total.5 = f32[8,128]{1,0:T(8,128)} custom-call(f32[8,128]{1,0:T(8,128)} %pad_maximum_fusion.7.x_ref), custom_call_target="tpu_custom_call" | custom-call | tf_op jit(solution)/shard_map/total/pallas_call | solution.py:1330
  385.0 1.3 fusion.20
  386.3 1.4 multiply_convert_fusion.1
  387.7 2.1 fusion.1
  389.8 4.0 copy.46
  393.7 3.2 constant_dynamic-update-slice_fusion.1
  397.0 2.0 convolution_convert_fusion
  398.9 2.5 constant_dynamic-update-slice_fusion
  401.4 0.8 slice_dynamic-update-slice_fusion.3
  402.3 0.8 slice_dynamic-update-slice_fusion.2
  403.1 0.8 slice_dynamic-update-slice_fusion.1
  403.9 0.9 slice_dynamic-update-slice_fusion
  404.8 1.3 select_dynamic-update-slice_fusion
  406.1 0.7 maximum_dynamic-update-slice_fusion
  406.8 0.8 broadcast_dynamic-update-slice_fusion.p_ref
  407.6 180.1 %small_total.1 = f32[2560,512]{1,0:T(8,128)} custom-call(bf16[4,2560,512]{2,1,0:T(8,128)(2,1)} %broadcast_dynamic-update-slice_fusion.p_ref), custom_call_target="tpu_custom_call" | custom-call | tf_op jit(solution)/shard_map/small_total/pallas_call | solution.py:384
  587.7 1.9 slice.213
  589.5 2.3 slice.207
  591.8 3.3 slice.208
  595.1 0.8 fusion.17
  595.9 0.7 copy.52
  596.6 0.6 pad_maximum_fusion.9
  597.2 0.6 pad_maximum_fusion.8
  597.8 1.4 fusion.18
  599.2 1.0 pad_maximum_fusion.1
  600.3 2.1 convolution_add_fusion
  602.3 1.3 convert_bitcast_fusion
  603.6 4.2 bitcast_convert_fusion
  607.9 0.8 copy.66
  (102 shorter events, 2.7 us)
Async XLA Ops:
  7.2 299.6 %reduce-scatter.4.cloned.1.call-start = ((), (), s32[]{:S(2)}) async-start(), calls=%async_computation.3 | async-start | bytes 5242880 | tf_op jit(solution)/shard_map/reduce_scatter | solution.py:1548
  83.5 3.6 copy-start.22
  83.5 4.2 copy-start.23
  83.6 4.8 copy-start.13
  83.6 5.6 copy-start.31
  85.3 137.8 %collective-permute-start = (bf16[512,2048]{1,0:T(8,128)(2,1)S(1)}, bf16[512,2048]{1,0:T(8,128)(2,1)}, u32[]{:S(2)}, u32[]{:S(2)}) collective-permute-start(bf16[512,2048]{1,0:T(8,128)(2,1)S(1)} %dynamic-slice_bitcast_fusion), channel_id=1, source_target_pairs={{0,4},{4,0},{8,12},{12,8},{16,20},{20,16},{24,28},{28,24},{1,5},{5... | collective-permute-start | bytes 6291464 | tf_op jit(solution)/shard_map/ppermute | solution.py:1377
  223.1 31.1 %collective-permute-start.1 = (bf16[1024,512]{1,0:T(8,128)(2,1)}, bf16[1024,512]{1,0:T(8,128)(2,1)S(1)}, u32[]{:S(2)}, u32[]{:S(2)}) collective-permute-start(bf16[1024,512]{1,0:T(8,128)(2,1)} %bitcast.155), channel_id=1, source_target_pairs={{0,4},{4,0},{8,12},{12,8},{16,20},{20,16},{24,28},{28,24},{1,5},{5... | collective-permute-start | bytes 3145736 | tf_op jit(solution)/shard_map/ppermute | solution.py:1377
  254.2 1.0 copy-start.33
  255.2 0.9 copy-start.16
  255.2 340.0 %reduce-scatter.6.cloned.1.call-start = ((), (), s32[]{:S(2)}) async-start(), calls=%async_computation.4 | async-start | bytes 4423680 | tf_op jit(solution)/shard_map/reduce_scatter | solution.py:1509
  255.9 347.7 %reduce-scatter.8.cloned.1.call-start = ((), (), s32[]{:S(2)}) async-start(), calls=%async_computation.5 | async-start | bytes 11796480 | tf_op jit(solution)/shard_map/reduce_scatter | solution.py:1551
  255.9 4.4 collective-permute-start.2
  306.7 1.5 copy-start.20
  306.7 1.5 copy-start.12
  306.7 1.5 copy-start.11
  306.7 4.8 copy-start.30
  306.7 10.0 %copy-start.19 = (f32[2,512]{1,0:T(2,128)S(1)}, f32[2,512]{1,0:T(2,128)}, u32[]{:S(2)}) copy-start(f32[2,512]{1,0:T(2,128)} %shift_mid_ref.1) | copy-start | bytes 12292
  306.7 10.0 %copy-start.18 = (f32[2,512]{1,0:T(2,128)S(1)}, f32[2,512]{1,0:T(2,128)}, u32[]{:S(2)}) copy-start(f32[2,512]{1,0:T(2,128)} %gain_mid_ref.1) | copy-start | bytes 12292
  306.7 10.0 %copy-start.28 = (f32[2,512]{1,0:T(2,128)S(1)}, f32[2,512]{1,0:T(2,128)}, u32[]{:S(2)}) copy-start(f32[2,512]{1,0:T(2,128)} %get-tuple-element.58) | copy-start | bytes 12292
  306.7 10.0 %copy-start.29 = (f32[2,512]{1,0:T(2,128)S(1)}, f32[2,512]{1,0:T(2,128)}, u32[]{:S(2)}) copy-start(f32[2,512]{1,0:T(2,128)} %get-tuple-element.59) | copy-start | bytes 12292
  306.7 10.6 %copy-start.10 = (f32[512,128]{1,0:T(8,128)S(1)}, f32[512,128]{1,0:T(8,128)}, u32[]{:S(2)}) copy-start(f32[512,128]{1,0:T(8,128)} %get-tuple-element.70) | copy-start | bytes 786436
  306.8 10.6 %copy-start.32 = (pred[128]{0:T(512)(128)(4,1)S(1)}, pred[128]{0:T(512)(128)(4,1)}, u32[]{:S(2)}) copy-start(pred[128]{0:T(512)(128)(4,1)} %constant.87.clone.1) | copy-start | bytes 388
  306.8 11.2 %copy-start = (bf16[256,2048]{1,0:T(8,128)(2,1)S(1)}, bf16[256,2048]{1,0:T(8,128)(2,1)}, u32[]{:S(2)}) copy-start(bf16[256,2048]{1,0:T(8,128)(2,1)} %in_ref.1) | copy-start | bytes 3145732
  306.8 11.2 %copy-start.14 = (f32[2048]{0:T(1024)S(1)}, f32[2048]{0:T(1024)}, u32[]{:S(2)}) copy-start(f32[2048]{0:T(1024)} %param.31) | copy-start | bytes 24580
  317.3 54.2 %copy-start.17 = (f32[1,512]{1,0:T(1,128)}, f32[1,512]{1,0:T(1,128)S(1)}, u32[]{:S(2)}) copy-start(f32[1,512]{1,0:T(1,128)S(1)} %get-tuple-element.154) | copy-start | bytes 6148
  337.8 3.7 copy-start.15
  339.1 2.4 copy-start.3
  339.1 2.4 copy-start.9
  341.6 1.7 copy-start.2
  360.2 11.3 %copy-start.4 = (f32[256,512]{1,0:T(8,128)S(1)}, f32[256,512]{1,0:T(8,128)}, u32[]{:S(2)}) copy-start(f32[256,512]{1,0:T(8,128)} %get-tuple-element.64) | copy-start | bytes 1572868
  360.2 26.1 %copy-start.21 = (f32[1,512]{1,0:T(1,128)S(1)}, f32[1,512]{1,0:T(1,128)}, u32[]{:S(2)}) copy-start(f32[1,512]{1,0:T(1,128)} %get-tuple-element.152) | copy-start | bytes 6148
  389.7 7.2 %copy-start.6 = (bf16[256,512]{1,0:T(8,128)(2,1)S(1)}, bf16[256,512]{1,0:T(8,128)(2,1)}, u32[]{:S(2)}) copy-start(bf16[256,512]{1,0:T(8,128)(2,1)} %get-tuple-element.68) | copy-start | bytes 786436
  389.7 9.2 %slice-start = ((s8[4718592]{0:T(1024)(128)(4,1)}), s8[524288]{0:T(1024)(128)(4,1)S(1)}, s32[]{:S(2)}) async-start(s8[4718592]{0:T(1024)(128)(4,1)} %bitcast.114), calls=%async_computation.6 | async-start | bytes 1048576
  393.7 5.2 slice-start.1
  401.4 3.4 copy-start.8
  591.8 4.8 copy-start.25
  591.8 4.8 copy-start.27
  591.8 5.4 copy-start.24
  591.8 5.4 copy-start.26
  597.8 2.5 copy-start.1
  600.2 2.1 copy-start.5
  603.6 4.3 copy-start.7
Sparse Core Ops, SparseCore 0:
  254.3 44.3 reduce-scatter.3
  301.2 69.2 reduce-scatter.5
  373.0 210.4 reduce-scatter.7
